TPU v7x, 32 devices: a whole 2x2x4 slice. The times are simulated.
32 devices in a mesh: roll: 16 (over z, y, x), exp: 2 (over core).
Axes of the slice: x: 2, y: 2, z: 4, core: 2. Of those that a mesh axis runs over, the one named last changes fastest.
Arguments:
- kda_prefill: bfloat16 [64, 32, 128, 128], P('roll', 'exp'), may hold values from -6 to 6
- latent_prefill: bfloat16 [64, 64, 576], P('roll', 'exp'), may hold values from -6 to 6
- prompt_len: int32 [64], replicated, may hold values from 1 to 64, as said below
- sample_counts: int32 [16, 4], replicated, may hold values from 1 to 16, 32 in all within a row
- kda_q: bfloat16 [2, 512, 4096], P(None, 'roll', 'exp'), may hold values from -6 to 6
- kda_k: bfloat16 [2, 512, 4096], P(None, 'roll', 'exp'), may hold values from -6 to 6
- kda_v: bfloat16 [2, 512, 4096], P(None, 'roll', 'exp'), may hold values from -6 to 6
- kda_decay: float32 [2, 512, 4096], P(None, 'roll', 'exp'), may hold values from 0.005 to 0.5
- kda_beta: float32 [2, 512, 32], P(None, 'roll', 'exp'), may hold values from 0.1 to 0.9
- mla_q: bfloat16 [2, 512, 18432], P(None, 'roll', 'exp'), may hold values from -6 to 6
- mla_new: bfloat16 [2, 512, 576], P(None, 'roll'), may hold values from -6 to 6
- w_uv: bfloat16 [32, 512, 128], P('exp'), may hold values from -0.25 to 0.25
Outputs:
- kda_out: bfloat16 [2, 512, 4096], P(None, 'roll', 'exp')
- mla_out: bfloat16 [2, 512, 4096], P(None, 'roll', 'exp')
Inputs may be any that keep to these rules, and one draw needn't show every extreme that they name: `prompt_len`: some prompt has length 1 and some has 64. `sample_counts`: each owner's row sums to 32; some prompt has 16 samples.
All inputs are finite; a program needn't handle non-finite values.
Results may differ from a plain program's by a relative error of at most 0.0057.
Values may be sent and summed in bfloat16 or wider, within the bound.
No kernel may reach another device: no remote copies, remote signals or barrier semaphores. Data moves between devices by JAX's collectives and lax.ppermute only.
A program may use at most 128 MiB of HBM per device.

v0:
```python
import jax
import jax.numpy as jnp
from jax import lax
from jax.sharding import PartitionSpec as P

DK = 128
RR = 64


def unit_rows(values):
    return values * lax.rsqrt(jnp.sum(values * values, axis=-1, keepdims=True) + 1e-06)


def delta_run(state, query_all, key_all, value_all, decay_all, beta_all):
    batch, heads, key_dim, value_dim = state.shape
    step_count = query_all.shape[0]
    outputs = []
    for step_index in range(step_count):
        query_now = unit_rows(
            query_all[step_index].astype(jnp.float32).reshape(batch, heads, key_dim)
        )
        key_now = unit_rows(key_all[step_index].astype(jnp.float32).reshape(batch, heads, key_dim))
        value_now = value_all[step_index].astype(jnp.float32).reshape(batch, heads, value_dim)
        keep_rate = jnp.exp(-decay_all[step_index].reshape(batch, heads, key_dim))
        beta_now = beta_all[step_index]
        probes = jnp.stack([key_now * keep_rate, query_now * keep_rate], axis=2)
        projected = jnp.einsum("bhkv,bhjk->bhjv", state, probes, precision=lax.Precision.HIGHEST)
        guess = projected[:, :, 0]
        correction = beta_now[..., None] * (value_now - guess)
        intersection = jnp.sum(key_now * query_now, axis=-1, keepdims=True)
        reading = projected[:, :, 1] + intersection * correction
        outputs.append(reading.reshape(batch, heads * value_dim).astype(jnp.bfloat16))
        if step_index + 1 < step_count:
            state = state * keep_rate[..., None] + key_now[..., None] * correction[..., None, :]
    return jnp.stack(outputs)


def latent_run(cache, cache_lengths, query_all, fresh_all, up_value):
    batch, cache_len, width = cache.shape
    step_count = query_all.shape[0]
    heads, rank, value_dim = up_value.shape
    keys_all = jnp.concatenate([cache, jnp.swapaxes(fresh_all, 0, 1)], axis=1)
    prompt_valid = jnp.arange(cache_len, dtype=jnp.int32)[None, :] < cache_lengths[:, None]
    score_scale = (DK + RR) ** (-0.5)
    outputs = []
    for step_index in range(step_count):
        fresh_valid = jnp.arange(step_count, dtype=jnp.int32) <= step_index
        valid = jnp.concatenate(
            [prompt_valid, jnp.broadcast_to(fresh_valid[None, :], (batch, step_count))], axis=1
        )
        query_now = query_all[step_index].reshape(batch, heads, width)
        scores = (
            jnp.einsum("bhc,blc->bhl", query_now, keys_all, preferred_element_type=jnp.float32)
            * score_scale
        )
        scores = jnp.where(valid[:, None, :], scores, -1e30)
        top_score = jnp.max(scores, axis=-1, keepdims=True)
        raised = jnp.exp(scores - top_score)
        weights = (raised / jnp.sum(raised, axis=-1, keepdims=True)).astype(jnp.bfloat16)
        context = jnp.einsum(
            "bhl,blr->bhr", weights, keys_all[..., :rank], preferred_element_type=jnp.float32
        ).astype(jnp.bfloat16)
        result = jnp.einsum("bhr,hrv->bhv", context, up_value, preferred_element_type=jnp.float32)
        outputs.append(result.reshape(batch, heads * value_dim).astype(jnp.bfloat16))
    return jnp.stack(outputs)


def on_device(
    kda_prefill,
    latent_prefill,
    prompt_len,
    sample_counts,
    kda_q,
    kda_k,
    kda_v,
    kda_decay,
    kda_beta,
    mla_q,
    mla_new,
    w_uv,
):
    group_size = lax.axis_size("roll")
    device_index = lax.axis_index("roll")
    per_device = kda_q.shape[1]
    per_owner = kda_prefill.shape[0]
    offsets = jnp.arange(per_device, dtype=jnp.int32)
    bounds = jnp.cumsum(sample_counts, axis=1)
    own_bounds = lax.dynamic_index_in_dim(bounds, device_index, 0, keepdims=False)
    own_local = jnp.sum((own_bounds[None, :] <= offsets[:, None]).astype(jnp.int32), axis=1)
    own_states = kda_prefill[own_local]
    own_latent = latent_prefill[own_local]
    source = (device_index + offsets) % group_size
    source_local = jnp.sum((bounds[source] <= offsets[:, None]).astype(jnp.int32), axis=1)
    prompt_ids = source * per_owner + source_local
    cache_lengths = prompt_len[prompt_ids]
    slots = (per_device + group_size - 1) // group_size
    targets = jnp.arange(group_size, dtype=jnp.int32)[:, None]
    layer_ids = jnp.arange(slots, dtype=jnp.int32)[None, :]
    wanted = (device_index - targets) % group_size + layer_ids * group_size
    present = (wanted < per_device).reshape(-1)
    picked = jnp.minimum(wanted, per_device - 1).reshape(-1)
    send_states = jnp.where(
        present[:, None, None, None], own_states[picked], jnp.zeros((), jnp.bfloat16)
    )
    send_latent = jnp.where(present[:, None, None], own_latent[picked], jnp.zeros((), jnp.bfloat16))
    got_states, got_latent = (
        lax.all_to_all(send_states, "roll", split_axis=0, concat_axis=0, tiled=True),
        lax.all_to_all(send_latent, "roll", split_axis=0, concat_axis=0, tiled=True),
    )
    arrival = source * slots + offsets // group_size
    states = got_states[arrival]
    latent = got_latent[arrival]
    kda_out = delta_run(states.astype(jnp.float32), kda_q, kda_k, kda_v, kda_decay, kda_beta)
    full_cache = lax.all_gather(latent, "exp", axis=1, tiled=True)
    mla_out = latent_run(full_cache, cache_lengths, mla_q, mla_new, w_uv)
    return (kda_out, mla_out)


def solution(mesh):
    return jax.shard_map(
        on_device,
        mesh=mesh,
        in_specs=(
            P("roll", "exp", None, None),
            P("roll", "exp", None),
            P(),
            P(),
            P(None, "roll", "exp"),
            P(None, "roll", "exp"),
            P(None, "roll", "exp"),
            P(None, "roll", "exp"),
            P(None, "roll", "exp"),
            P(None, "roll", "exp"),
            P(None, "roll", None),
            P("exp", None, None),
        ),
        out_specs=(P(None, "roll", "exp"), P(None, "roll", "exp")),
        check_vma=False,
    )
```

profile of v0, /device:TPU:28, one launch (start us, length us, event | category | flops | bytes accessed | tf_op | source)
XLA Modules:
  0.0 536.9 jit_solution(11031678494281563657)
XLA Ops:
  7.4 0.9 copy.26
  8.7 2.7 gather_fusion.5
  11.4 2.1 gather_fusion.6
  13.5 1.3 broadcast_select_fusion.1
  14.8 6.9 %all-to-all-start.1 = ((bf16[32,32,576]{2,1,0:T(8,128)(2,1)}), bf16[32,32,576]{2,1,0:T(8,128)(2,1)S(1)}, u32[]{:S(2)}, u32[]{:S(2)}) async-start(bf16[32,32,576]{2,1,0:T(8,128)(2,1)} %broadcast_select_fusion.1), calls=%async_computation.1 | async-start | bytes 2621440 | tf_op jit(solution)/shard_map/all_to_all | solution.py:108
  21.7 7.1 %gather_fusion = bf16[32,16,128,128]{3,2,1,0:T(8,128)(2,1)} fusion(bf16[4,16,128,128]{3,2,1,0:T(8,128)(2,1)S(1)} %copy-done, s32[1024]{0:T(1024)S(1)} %pad_clamp_fusion.4), kind=kCustom, calls=%fused_computation | custom fusion | bytes 33554560 | tf_op jit(solution)/shard_map/gather | solution.py:90
  28.9 13.0 %gather_fusion.1 = bf16[32,16,128,128]{3,2,1,0:T(8,128)(2,1)} fusion(bf16[32,16,128,128]{3,2,1,0:T(8,128)(2,1)} %gather_fusion, s32[1024]{0:T(1024)S(1)} %pad_clamp_fusion.3), kind=kCustom, calls=%fused_computation.1 | custom fusion | bytes 33554560 | tf_op jit(solution)/shard_map/gather | solution.py:103
  41.9 14.0 %broadcast_select_fusion = bf16[32,16,128,128]{3,2,1,0:T(8,128)(2,1)} fusion(bf16[32,16,128,128]{3,2,1,0:T(8,128)(2,1)} %gather_fusion.1, pred[32]{0:T(512)(128)(4,1)S(1)} %lt.102), kind=kLoop, calls=%fused_computation.20 | loop fusion | flops 8388608 | bytes 33554464 | tf_op jit(solution)/shard_map/jit(_where)/select_n | solution.py:102
  55.9 6.9 %all-to-all-start = ((bf16[32,16,128,128]{3,2,1,0:T(8,128)(2,1)}), bf16[32,16,128,128]{3,2,1,0:T(8,128)(2,1)}, u32[]{:S(2)}, u32[]{:S(2)}) async-start(bf16[32,16,128,128]{3,2,1,0:T(8,128)(2,1)} %broadcast_select_fusion), calls=%async_computation | async-start | bytes 33554432 | tf_op jit(solution)/shard_map/all_to_all | solution.py:107
  62.8 0.8 fusion.52
  63.7 0.9 fusion.51
  65.4 3.1 fusion.2
  69.2 0.9 negate_exponential_fusion
  70.1 0.9 fusion.70
  71.1 1.8 gather_fusion.7
  72.9 2.1 reshape.487
  74.9 1.0 reshape.489
  75.9 2.0 exp.48
  78.0 1.0 reshape.495
  79.0 1.0 reshape.491
  80.0 1.0 reshape.493
  81.0 2.0 exp.50
  83.0 0.7 copy.39
  84.0 4.9 fusion.3
  89.1 0.8 mul.317
  90.1 0.7 mul.345
  91.7 1.4 reshape_squeeze.8
  93.1 1.4 reshape_squeeze.9
  95.5 1.3 multiply_multiply_fusion.3
  96.7 3.0 multiply_multiply_fusion.1
  99.7 2.9 fusion.27
  102.9 3.6 fusion.16
  106.4 1.6 fusion.28
  108.2 3.0 fusion.25
  112.1 3.6 fusion.17
  115.7 1.6 fusion.29
  117.5 0.7 pad_maximum_fusion.23
  118.2 325.3 %all-to-all-done = bf16[32,16,128,128]{3,2,1,0:T(8,128)(2,1)} async-done(((bf16[32,16,128,128]{3,2,1,0:T(8,128)(2,1)}), bf16[32,16,128,128]{3,2,1,0:T(8,128)(2,1)}, u32[]{:S(2)}, u32[]{:S(2)}) %all-to-all-start) | async-done | bytes 16777248 | tf_op jit(solution)/shard_map/all_to_all | solution.py:107
  443.5 13.0 %gather_fusion.2 = bf16[32,16,128,128]{3,2,1,0:T(8,128)(2,1)} fusion(bf16[32,16,128,128]{3,2,1,0:T(8,128)(2,1)} %all-to-all-done, s32[1024]{0:T(1024)S(1)} %pad_clamp_fusion.2), kind=kCustom, calls=%fused_computation.2 | custom fusion | bytes 33554560 | tf_op jit(solution)/shard_map/gather | solution.py:111
  456.6 15.8 %fusion.30 = f32[32,16,2,128]{3,2,1,0:T(2,128)S(1)} fusion(bf16[32,16,128,128]{3,2,1,0:T(8,128)(2,1)} %gather_fusion.2, f32[32,16,1,128]{3,2,1,0:T(1,128)S(1)} %get-tuple-element.25, f32[32,16,1,128]{3,2,1,0:T(1,128)S(1)} %get-tuple-element.24), kind=kOutput, calls=%fused_computation.44 | convolution fusion | flops 201457664 | bytes 17825792 | tf_op jit(solution)/shard_map/bhkv,bhjk->bhjv/dot_general | solution.py:27
  472.3 2.5 slice_reduce_fusion.3
  474.8 45.1 %fusion.4 = f32[32,16,2,128]{3,2,1,0:T(2,128)S(1)} fusion(bf16[32,16,128,128]{3,2,1,0:T(8,128)(2,1)S(1)} %copy-done.3, f32[32,16,128]{2,1,0:T(8,128)S(1)} %bitcast.71, f32[32,16,128]{2,1,0:T(8,128)S(1)} %copy-done.11, f32[32,16,128]{2,1,0:T(8,128)S(1)} %bitcast.72, f32[32,16,1,128]{3,2,1,0:T(1,128)S(1)} %copy-done.27, f32[32,16,1,128]{3,2,1,0:T(1,128)S(1)} %copy-done.26), kind=kOutput, calls=%fused_computation.12 | convolution fusion | flops 235012096 | bytes 18612224 | tf_op jit(solution)/shard_map/bhkv,bhjk->bhjv/dot_general | solution.py:27
  520.0 2.0 slice_reduce_fusion
  522.0 1.7 squeeze.22
  523.7 1.7 squeeze.23
  525.4 1.7 squeeze.10
  527.1 0.7 squeeze.11
  527.9 1.4 add_convert_fusion.1
  (124 shorter events, 6.9 us)
Async XLA Ops:
  7.2 14.5 %copy-start = (bf16[4,16,128,128]{3,2,1,0:T(8,128)(2,1)S(1)}, bf16[4,16,128,128]{3,2,1,0:T(8,128)(2,1)}, u32[]{:S(2)}) copy-start(bf16[4,16,128,128]{3,2,1,0:T(8,128)(2,1)} %param.12) | copy-start | bytes 6291460
  14.8 41.1 %all-to-all-start.1 = ((bf16[32,32,576]{2,1,0:T(8,128)(2,1)}), bf16[32,32,576]{2,1,0:T(8,128)(2,1)S(1)}, u32[]{:S(2)}, u32[]{:S(2)}) async-start(bf16[32,32,576]{2,1,0:T(8,128)(2,1)} %broadcast_select_fusion.1), calls=%async_computation.1 | async-start | bytes 2621440 | tf_op jit(solution)/shard_map/all_to_all | solution.py:108
  55.9 6.9 %copy-start.22 = (bf16[2,32,2048]{2,1,0:T(8,128)(2,1)S(1)}, bf16[2,32,2048]{2,1,0:T(8,128)(2,1)}, u32[]{:S(2)}) copy-start(bf16[2,32,2048]{2,1,0:T(8,128)(2,1)} %param.16) | copy-start | bytes 786436
  55.9 7.8 %copy-start.23 = (bf16[2,32,2048]{2,1,0:T(8,128)(2,1)S(1)}, bf16[2,32,2048]{2,1,0:T(8,128)(2,1)}, u32[]{:S(2)}) copy-start(bf16[2,32,2048]{2,1,0:T(8,128)(2,1)} %param.17) | copy-start | bytes 786436
  55.9 387.6 %all-to-all-start = ((bf16[32,16,128,128]{3,2,1,0:T(8,128)(2,1)}), bf16[32,16,128,128]{3,2,1,0:T(8,128)(2,1)}, u32[]{:S(2)}, u32[]{:S(2)}) async-start(bf16[32,16,128,128]{3,2,1,0:T(8,128)(2,1)} %broadcast_select_fusion), calls=%async_computation | async-start | bytes 33554432 | tf_op jit(solution)/shard_map/all_to_all | solution.py:107
  62.8 36.9 %all-gather.3.cloned.1.call-start = ((), (), s32[]{:S(2)}) async-start(), calls=%async_computation.2 | async-start | bytes 3932160 | tf_op jit(solution)/shard_map/all_gather | solution.py:114
  63.6 4.9 copy-start.20
  63.6 5.6 %copy-start.21 = (f32[2,32,2048]{2,1,0:T(8,128)S(1)}, f32[2,32,2048]{2,1,0:T(8,128)}, u32[]{:S(2)}) copy-start(f32[2,32,2048]{2,1,0:T(8,128)} %param.19) | copy-start | bytes 1572868
  64.5 5.6 %copy-start.6 = (bf16[2,32,9216]{2,1,0:T(8,128)(2,1)S(1)}, bf16[2,32,9216]{2,1,0:T(8,128)(2,1)}, u32[]{:S(2)}) copy-start(bf16[2,32,9216]{2,1,0:T(8,128)(2,1)} %param.21) | copy-start | bytes 3538948
  70.1 2.7 copy-start.31
  70.1 4.8 copy-start.12
  71.0 7.9 %copy-start.13 = (f32[1,32,2048]{2,1,0:T(8,128)S(1)}, f32[1,32,2048]{2,1,0:T(8,128)}, u32[]{:S(2)}) copy-start(f32[1,32,2048]{2,1,0:T(8,128)} %get-tuple-element.18) | copy-start | bytes 786436
  72.8 5.2 copy-start.16
  72.8 10.2 %copy-start.15 = (f32[4,8,16,128]{3,1,2,0:T(8,128)S(1)}, f32[4,8,16,128]{3,1,2,0:T(8,128)}, u32[]{:S(2)}) copy-start(f32[4,8,16,128]{3,1,2,0:T(8,128)} %get-tuple-element.10) | copy-start | bytes 786436
  72.8 10.9 %copy-start.14 = (f32[32,16,128]{2,1,0:T(8,128)S(1)}, f32[32,16,128]{2,1,0:T(8,128)}, u32[]{:S(2)}) copy-start(f32[32,16,128]{2,1,0:T(8,128)} %fusion.2) | copy-start | bytes 786436
  80.0 11.6 %copy-start.28 = (bf16[2,32,576]{2,1,0:T(8,128)(2,1)S(1)}, bf16[2,32,576]{2,1,0:T(8,128)(2,1)}, u32[]{:S(2)}) copy-start(bf16[2,32,576]{2,1,0:T(8,128)(2,1)} %param.22) | copy-start | bytes 221188
  80.0 11.7 %copy-start.5 = (bf16[1,32,9216]{2,1,0:T(8,128)(2,1)S(1)}, bf16[1,32,9216]{2,1,0:T(8,128)(2,1)}, u32[]{:S(2)}) copy-start(bf16[1,32,9216]{2,1,0:T(8,128)(2,1)} %get-tuple-element.6) | copy-start | bytes 1769476
  83.9 11.4 %copy-start.10 = (f32[32,16,128]{2,1,0:T(8,128)}, f32[32,16,128]{2,1,0:T(8,128)S(1)}, u32[]{:S(2)}) copy-start(f32[32,16,128]{2,1,0:T(8,128)S(1)} %broadcast_multiply_fusion) | copy-start | bytes 786436
  83.9 10.7 %copy-start.2 = (s32[64]{0:T(128)S(1)}, s32[64]{0:T(128)}, u32[]{:S(2)}) copy-start(s32[64]{0:T(128)} %param.14) | copy-start | bytes 772
  88.9 6.5 %copy-start.17 = (f32[32,16,1,128]{3,2,1,0:T(1,128)S(1)}, f32[32,16,1,128]{3,2,1,0:T(1,128)}, u32[]{:S(2)}) copy-start(f32[32,16,1,128]{3,2,1,0:T(1,128)} %reshape.487) | copy-start | bytes 786436
  88.9 6.6 %copy-start.18 = (f32[32,16,1,128]{3,2,1,0:T(1,128)S(1)}, f32[32,16,1,128]{3,2,1,0:T(1,128)}, u32[]{:S(2)}) copy-start(f32[32,16,1,128]{3,2,1,0:T(1,128)} %reshape.489) | copy-start | bytes 786436
  89.0 6.5 %copy-start.19 = (f32[32,16,1,128]{3,2,1,0:T(1,128)S(1)}, f32[32,16,1,128]{3,2,1,0:T(1,128)}, u32[]{:S(2)}) copy-start(f32[32,16,1,128]{3,2,1,0:T(1,128)} %exp.48) | copy-start | bytes 786436
  91.7 8.0 %copy-start.29 = (bf16[2,32,576]{2,0,1:T(2,128)(2,1)}, bf16[2,32,576]{2,0,1:T(2,128)(2,1)S(1)}, u32[]{:S(2)}) copy-start(bf16[2,32,576]{2,0,1:T(2,128)(2,1)S(1)} %copy.45) | copy-start | bytes 221188
  102.6 3.8 copy-start.4
  108.2 3.9 copy-start.30
  111.2 0.7 copy-start.25
  456.5 15.8 %copy-start.9 = (f32[32,16,1,128]{3,2,1,0:T(1,128)S(1)}, f32[32,16,1,128]{3,2,1,0:T(1,128)}, u32[]{:S(2)}) copy-start(f32[32,16,1,128]{3,2,1,0:T(1,128)} %reshape.495) | copy-start | bytes 786436
  456.5 18.3 %copy-start.3 = (bf16[32,16,128,128]{3,2,1,0:T(8,128)(2,1)S(1)}, bf16[32,16,128,128]{3,2,1,0:T(8,128)(2,1)}, u32[]{:S(2)}) copy-start(bf16[32,16,128,128]{3,2,1,0:T(8,128)(2,1)} %gather_fusion.2) | copy-start | bytes 50331652
  456.5 18.3 %copy-start.11 = (f32[32,16,128]{2,1,0:T(8,128)S(1)}, f32[32,16,128]{2,1,0:T(8,128)}, u32[]{:S(2)}) copy-start(f32[32,16,128]{2,1,0:T(8,128)} %copy-done.10) | copy-start | bytes 786436
  456.5 18.3 %copy-start.24 = (f32[4,8,16,128]{3,2,1,0:T(8,128)S(1)}, f32[4,8,16,128]{3,2,1,0:T(8,128)}, u32[]{:S(2)}) copy-start(f32[4,8,16,128]{3,2,1,0:T(8,128)} %copy.39) | copy-start | bytes 786436
  456.5 18.3 %copy-start.26 = (f32[32,16,1,128]{3,2,1,0:T(1,128)S(1)}, f32[32,16,1,128]{3,2,1,0:T(1,128)}, u32[]{:S(2)}) copy-start(f32[32,16,1,128]{3,2,1,0:T(1,128)} %get-tuple-element.14) | copy-start | bytes 786436
  456.6 18.3 %copy-start.27 = (f32[32,16,1,128]{3,2,1,0:T(1,128)S(1)}, f32[32,16,1,128]{3,2,1,0:T(1,128)}, u32[]{:S(2)}) copy-start(f32[32,16,1,128]{3,2,1,0:T(1,128)} %get-tuple-element.15) | copy-start | bytes 786436
  474.8 55.2 %copy-start.1 = (bf16[4,16,128,128]{3,2,1,0:T(8,128)(2,1)S(1)}, bf16[4,16,128,128]{3,2,1,0:T(8,128)(2,1)}, u32[]{:S(2)}) copy-start(bf16[4,16,128,128]{3,2,1,0:T(8,128)(2,1)} %param.12) | copy-start | bytes 6291460
  520.0 7.9 %copy-start.7 = (f32[1,32,2048]{2,1,0:T(8,128)S(1)}, f32[1,32,2048]{2,1,0:T(8,128)}, u32[]{:S(2)}) copy-start(f32[1,32,2048]{2,1,0:T(8,128)} %mul.317) | copy-start | bytes 786436
  520.0 7.9 %copy-start.8 = (f32[1,32,2048]{2,1,0:T(8,128)S(1)}, f32[1,32,2048]{2,1,0:T(8,128)}, u32[]{:S(2)}) copy-start(f32[1,32,2048]{2,1,0:T(8,128)} %mul.345) | copy-start | bytes 786436
Sparse Core Ops, SparseCore 0:
  73.0 12.5 all-gather.2
where the time goes:
time: 538 us; the launch traced here: 537 us
  waiting for transfers between devices  325 us (60%)
  matrix products  77.2 us (14%)
  local copies, waits for them, and re-layouts  67.9 us (13%)
  other arithmetic  38 us (7%)
  between operations  14.5 us (3%)
  starting transfers between devices  13.9 us (3%)
    all_to_all x1, waiting for transfers between devices, on_device(): lax.all_to_all(send_states, 'roll', split_axis=0, concat_axis=0, tiled=True)  325 us
    dot_general x2, matrix products, delta_run(): jnp.einsum('bhkv,bhjk->bhjv', state, probes, precision=lax.Precision.HIGH...  60.9 us
    select_n x1, other arithmetic, on_device(): jnp.where(present[:, None, None, None], own_states[picked], jnp.zeros((),...  14 us
    gather x1, local copies, waits for them, and re-layouts, on_device(): states = got_states[arrival]  13 us
    gather x1, local copies, waits for them, and re-layouts, on_device(): own_states[picked]  13 us
  transfers between devices with their start and end apart: 3, of which 1 were waited for; matrix products, arithmetic and copies ran while one was open for 16% of the time, Pallas kernels for 0%

commit v1 on v0

v1 whole, which is shorter than its diff:
```python
import functools

import jax
import jax.numpy as jnp
from jax import lax
from jax.experimental import pallas as pl
from jax.experimental.pallas import tpu as pltpu
from jax.sharding import PartitionSpec as P

F32 = jnp.float32
BF16 = jnp.bfloat16
NEG = -1e30


def split(x, n):
    if n & (n - 1) == 0:
        return lax.shift_right_logical(x, jnp.full_like(x, n.bit_length() - 1)), x & (n - 1)
    return lax.div(x, jnp.full_like(x, n)), lax.rem(x, jnp.full_like(x, n))


def wrap(x, n):
    return jnp.where(x < 0, x + n, x)


def lanes(shape, dim):
    return lax.broadcasted_iota(jnp.int32, shape, dim)


def prompt_at(counts_ref, owner, j):
    bound = jnp.int32(0)
    k = jnp.zeros_like(j)
    for i in range(counts_ref.shape[1]):
        bound = bound + counts_ref[owner, i]
        k = k + (bound <= j).astype(jnp.int32)
    return k


def fan_slot(row, me, group, slots, steps):
    other, rest = split(row, slots * steps)
    slot, step = split(rest, steps)
    return other, slot, step


def plane_slot(row, carry_of, cols, pairs, steps, per_shift):
    shift, rest = split(row, per_shift)
    hop, rest = split(rest, pairs * steps)
    pair, step = split(rest, steps)
    i = wrap(hop - carry_of(shift), cols["depth"]) + cols["depth"] * pair
    return step, i, shift + cols["width"] * i


def dot(a, b):
    return lax.dot_general(a, b, (((1,), (0,)), ((), ())), preferred_element_type=F32)


def dot_t(a, b):
    return lax.dot_general(a, b, (((1,), (1,)), ((), ())), preferred_element_type=F32)


def reads_kernel(geo, q_ref, k_ref, g_ref, b_ref, r_ref, a_ref, raw):
    steps, per, width = q_ref.shape
    heads = b_ref.shape[2]
    dk = width // heads
    me = lax.axis_index("roll")
    coef = [[] for _ in range(steps * (steps + 1) // 2)]
    for h in range(heads):
        sl = slice(h * dk, (h + 1) * dk)
        qs, ks, ds, bs = [], [], [], []
        for t in range(steps):
            q = q_ref[t, :, sl].astype(F32)
            k = k_ref[t, :, sl].astype(F32)
            qs.append(q * lax.rsqrt(jnp.sum(q * q, axis=1, keepdims=True) + 1e-06))
            ks.append(k * lax.rsqrt(jnp.sum(k * k, axis=1, keepdims=True) + 1e-06))
            ds.append(jnp.exp(-g_ref[t, :, sl]))
            bs.append(b_ref[t, :, h : h + 1])
        n = 0
        for t in range(steps):
            u = qs[t]
            for i in range(t, -1, -1):
                a = bs[i] * jnp.sum(ks[i] * u, axis=1, keepdims=True)
                u = ds[i] * (u - a * ks[i])
                coef[n].append(a)
                n += 1
            raw[t * per : (t + 1) * per, sl] = u.astype(BF16)
    for n, c in enumerate(coef):
        a_ref[n] = jnp.concatenate(c, axis=1)
    rows = r_ref.shape[0]
    group, slots = geo["group"], geo["slots"]
    row, col = lanes((rows, steps * per), 0), lanes((rows, steps * per), 1)
    other, slot, step = fan_slot(row, me, group, slots, steps)
    j = wrap(other - me, group) + group * slot
    pick = ((col == step * per + j) & (j < per)).astype(F32).astype(BF16)
    r_ref[...] = dot(pick, raw[...]).astype(BF16)


def state_kernel(geo, counts_ref, r_ref, s_ref, y_ref):
    rows = r_ref.shape[0]
    prompts, heads, dk, dv = s_ref.shape
    me = lax.axis_index("roll")
    group, slots, steps = geo["group"], geo["slots"], geo["steps"]
    row = lanes((rows, dk), 0)
    other, slot, step = fan_slot(row, me, group, slots, steps)
    j = wrap(me - other, group) + group * slot
    k = prompt_at(counts_ref, me, j)
    keep = [(k == p).astype(F32).astype(BF16) for p in range(prompts)]
    for h in range(heads):
        r = r_ref[:, h * dk : (h + 1) * dk]
        acc = dot(r * keep[0], s_ref[0, h])
        for p in range(1, prompts):
            acc = acc + dot(r * keep[p], s_ref[p, h])
        y_ref[:, h * dv : (h + 1) * dv] = acc.astype(BF16)


def kda_out_kernel(geo, y_ref, a_ref, v_ref, o_ref):
    steps, per, width = v_ref.shape
    heads = a_ref.shape[2]
    dv = width // heads
    rows = y_ref.shape[0]
    me = lax.axis_index("roll")
    group, slots = geo["group"], geo["slots"]
    row, col = lanes((steps * per, rows), 0), lanes((steps * per, rows), 1)
    other, slot, step = fan_slot(col, me, group, slots, steps)
    j = wrap(other - me, group) + group * slot
    pick = ((row == step * per + j) & (j < per)).astype(F32).astype(BF16)
    for h in range(heads):
        sl = slice(h * dv, (h + 1) * dv)
        y = dot(pick, y_ref[:, sl])
        n = 0
        for t in range(steps):
            out = y[t * per : (t + 1) * per]
            for i in range(t, -1, -1):
                out = out + a_ref[n, :, h : h + 1] * v_ref[i, :, sl].astype(F32)
                n += 1
            o_ref[t, :, sl] = out.astype(BF16)


def send_pick(geo, shape, row_dim, b):
    row, col = lanes(shape, row_dim), lanes(shape, 1 - row_dim)
    width = geo["width"]

    def carry(shift):
        return (b + shift >= width).astype(jnp.int32)

    step, i, j = plane_slot(row, carry, geo, geo["pairs"], geo["steps"], geo["per_shift"])
    hit = (col == step * geo["per"] + j) & (i < geo["per"] // width)
    return hit.astype(F32).astype(BF16)


def send_kernel(geo, q_ref, f_ref, *o_refs):
    total, wide = q_ref.shape
    fresh = f_ref.shape[1]
    me = lax.axis_index("roll")
    _, b = split(me, geo["width"])
    n = geo["per_shift"]
    pick = send_pick(geo, (n * geo["width"], total), 0, b)
    step = geo["chunk"]
    for at in range(0, wide, step):
        out = dot(pick, q_ref[:, at : at + step]).astype(BF16)
        for s, o_ref in enumerate(o_refs):
            o_ref[:, at : at + step] = out[s * n : (s + 1) * n]
    out = dot(pick, f_ref[...]).astype(BF16)
    for s, o_ref in enumerate(o_refs):
        o_ref[:, wide : wide + fresh] = out[s * n : (s + 1) * n]
        o_ref[:, wide + fresh :] = jnp.zeros((n, o_ref.shape[1] - wide - fresh), BF16)


def latent_kernel(geo, counts_ref, len_ref, w_ref, *refs):
    width, hops, pairs, steps = geo["width"], geo["hops"], geo["pairs"], geo["steps"]
    depth, halves, cache, prompts = geo["depth"], geo["halves"], geo["cache"], geo["prompts"]
    n, tile = geo["per_shift"], geo["tile"]
    q_refs, refs = refs[:width], refs[width:]
    k_refs, refs = refs[:halves], refs[halves:]
    o_refs, (qp, k_even, k_odd, ctx) = refs[:width], refs[width:]
    heads, rank, dv = w_ref.shape
    wide = o_refs[0].shape[1] // dv * geo["entry"]
    entry, padded = geo["entry"], k_even.shape[1]
    me = lax.axis_index("roll")
    half = lax.axis_index("exp")
    a, b = split(me, width)
    rows = n * width
    row, col = lanes((rows, rows), 0), lanes((rows, rows), 1)
    hop, rest = split(row, tile)
    shift, rest = split(rest, pairs * steps)
    regroup = (col == shift * n + hop * (pairs * steps) + rest).astype(F32).astype(BF16)
    shift2, rest2 = split(row, n)
    hop2, rest2 = split(rest2, pairs * steps)
    back = (col == hop2 * tile + shift2 * (pairs * steps) + rest2).astype(F32).astype(BF16)
    step = geo["chunk"]
    total = q_refs[0].shape[1]
    for at in range(0, total, step):
        to = min(at + step, total)
        part = jnp.concatenate([q[:, at:to] for q in q_refs], axis=0)
        qp[:, at:to] = dot(regroup, part).astype(BF16)
    per_half = prompts * cache // halves
    local = cache // halves
    keys = prompts * cache
    cols = k_even.shape[0]
    k_even[:, entry:] = jnp.zeros((cols, padded - entry), BF16)
    k_even[keys:, :] = jnp.zeros((cols - keys, padded), BF16)
    scale = geo["scale"]
    half_heads = heads // 2
    for hop in range(hops):
        owner_a = a + hop
        owner = jnp.where(owner_a >= depth, owner_a - depth, owner_a) * width + b
        for e in range(halves):
            k_even[e * per_half : (e + 1) * per_half, :entry] = k_refs[e][
                hop * per_half : (hop + 1) * per_half, :
            ]
        k_even[keys : keys + tile, :] = qp[hop * tile : (hop + 1) * tile, wide : wide + padded]
        k_odd[...] = pltpu.roll(k_even[...].astype(F32), padded - entry, 1).astype(BF16)
        r0 = lanes((tile, cols), 0)
        c0 = lanes((tile, cols), 1)
        shift, rest = split(r0, pairs * steps)
        pair, step_r = split(rest, steps)
        carry = (shift > b).astype(jnp.int32)
        i = wrap(hop - carry, depth) + depth * pair
        k = prompt_at(counts_ref, owner, shift + width * i)
        e, rest = split(c0, per_half)
        kk, pos = split(rest, local)
        e = e + half
        pos = jnp.where(e >= halves, e - halves, e) * local + pos
        length = jnp.zeros_like(pos)
        for p in range(prompts):
            length = jnp.where(kk == p, len_ref[owner * prompts + p], length)
        in_prompt = (c0 < keys) & (kk == k) & (pos < length)
        behind = r0 - (c0 - keys)
        in_fresh = (c0 >= keys) & (behind >= 0) & (behind <= step_r)
        allowed = (in_prompt | in_fresh)[None]
        parts = []
        for odd, k_ref in enumerate((k_even, k_odd)):
            starts = [2 * entry * p + odd * (2 * entry - padded) for p in range(half_heads)]
            query = jnp.concatenate(
                [qp[hop * tile : (hop + 1) * tile, s : s + padded] for s in starts], axis=0
            )
            scores = dot_t(query, k_ref[...]).reshape(half_heads, tile, cols) * scale
            scores = jnp.where(allowed, scores, NEG)
            top = jnp.max(scores, axis=-1, keepdims=True)
            raised = jnp.exp(scores - top)
            weights = raised / jnp.sum(raised, axis=-1, keepdims=True)
            parts.append(weights.reshape(half_heads * tile, cols).astype(BF16))
        weights = jnp.concatenate(parts, axis=0)
        context = dot(weights, k_even[:, :rank]).astype(BF16)
        for at in range(heads):
            ctx[at, hop * tile : (hop + 1) * tile, :] = context[at * tile : (at + 1) * tile]
    for h in range(heads):
        at = (h % 2) * half_heads + h // 2
        out = dot(ctx[at], w_ref[h]).astype(BF16)
        out = dot(back, out).astype(BF16)
        for s, o_ref in enumerate(o_refs):
            o_ref[:, h * dv : (h + 1) * dv] = out[s * n : (s + 1) * n]


def mla_out_kernel(geo, *refs):
    refs, o_ref = refs[:-1], refs[-1]
    me = lax.axis_index("roll")
    _, b = split(me, geo["width"])
    n = geo["per_shift"]
    total, wide = o_ref.shape
    pick = send_pick(geo, (total, n * geo["width"]), 1, b)
    step = geo["chunk"]
    for at in range(0, wide, step):
        part = jnp.concatenate([r[:, at : at + step] for r in refs], axis=0)
        o_ref[:, at : at + step] = dot(pick, part).astype(BF16)


def call(kernel, geo, out, args, smem=0, scratch=()):
    spaces = [pltpu.SMEM] * smem + [pltpu.VMEM] * (len(args) - smem)
    return pl.pallas_call(
        functools.partial(kernel, geo),
        out_shape=out,
        in_specs=[pl.BlockSpec(memory_space=s) for s in spaces],
        scratch_shapes=list(scratch),
        compiler_params=pltpu.CompilerParams(vmem_limit_bytes=48 * 1024 * 1024),
        name=kernel.__name__,
    )(*args)


def pad_to(n, m):
    return -(-n // m) * m


def on_device(
    kda_prefill,
    latent_prefill,
    prompt_len,
    sample_counts,
    kda_q,
    kda_k,
    kda_v,
    kda_decay,
    kda_beta,
    mla_q,
    mla_new,
    w_uv,
):
    group = lax.axis_size("roll")
    halves = lax.axis_size("exp")
    steps, per, kda_width = kda_q.shape
    heads = kda_beta.shape[2]
    prompts, local, entry = latent_prefill.shape
    cache = local * halves
    _, rank, dv = w_uv.shape
    width = 4
    depth = group // width
    slots = -(-per // group)
    per_mate = per // width
    hops = min(depth, per_mate + 1)
    pairs = max(-(-per_mate // depth), -(-16 // (width * steps)))
    padded = pad_to(entry, 128)
    geo = dict(
        group=group,
        halves=halves,
        steps=steps,
        per=per,
        width=width,
        depth=depth,
        slots=slots,
        hops=hops,
        pairs=pairs,
        prompts=prompts,
        cache=cache,
        entry=entry,
        per_shift=hops * pairs * steps,
        tile=width * pairs * steps,
        scale=192.0**-0.5,
        chunk=1152,
    )
    shape = jax.ShapeDtypeStruct

    def mates(sign, s):
        return [(i, i // width * width + (i + sign * s) % width) for i in range(group)]

    coefs = steps * (steps + 1) // 2
    reads, coef = call(
        reads_kernel,
        geo,
        (shape((group * slots * steps, kda_width), BF16), shape((coefs, per, heads), F32)),
        (kda_q, kda_k, kda_decay, kda_beta),
        scratch=[pltpu.VMEM((steps * per, kda_width), BF16)],
    )
    got = lax.all_to_all(reads, "roll", 0, 0, tiled=True)

    own = latent_prefill.reshape(prompts * local, entry)
    column = [own] + [
        lax.ppermute(own, "roll", [(i, (i - width * h) % group) for i in range(group)])
        for h in range(1, hops)
    ]
    column = jnp.concatenate(column, axis=0)
    caches = [column] + [
        lax.ppermute(column, "exp", [(i, (i - e) % halves) for i in range(halves)])
        for e in range(1, halves)
    ]
    wide = mla_q.shape[2]
    parcels = call(
        send_kernel,
        geo,
        tuple(shape((geo["per_shift"], wide + padded), BF16) for _ in range(width)),
        (mla_q.reshape(steps * per, wide), mla_new.reshape(steps * per, entry)),
    )
    queries = [parcels[0]] + [
        lax.ppermute(parcels[s], "roll", mates(1, s)) for s in range(1, width)
    ]
    products = call(
        state_kernel,
        geo,
        shape((group * slots * steps, kda_width), BF16),
        (sample_counts, got, kda_prefill),
        smem=1,
    )
    back = lax.all_to_all(products, "roll", 0, 0, tiled=True)
    cols = pad_to(prompts * cache + geo["tile"], 128)
    results = call(
        latent_kernel,
        geo,
        tuple(shape((geo["per_shift"], heads * dv), BF16) for _ in range(width)),
        (sample_counts, prompt_len, w_uv, *queries, *caches),
        smem=2,
        scratch=[
            pltpu.VMEM((geo["per_shift"] * width, wide + padded), BF16),
            pltpu.VMEM((cols, padded), BF16),
            pltpu.VMEM((cols, padded), BF16),
            pltpu.VMEM((heads, hops * geo["tile"], rank), BF16),
        ],
    )
    returned = [results[0]] + [
        lax.ppermute(results[s], "roll", mates(-1, s)) for s in range(1, width)
    ]
    mla_out = call(mla_out_kernel, geo, shape((steps * per, heads * dv), BF16), returned)
    kda_out = call(
        kda_out_kernel, geo, shape((steps, per, kda_width), BF16), (back, coef, kda_v)
    )
    return (kda_out, mla_out.reshape(steps, per, heads * dv))


def solution(mesh):
    return jax.shard_map(
        on_device,
        mesh=mesh,
        in_specs=(
            P("roll", "exp", None, None),
            P("roll", "exp", None),
            P(),
            P(),
            P(None, "roll", "exp"),
            P(None, "roll", "exp"),
            P(None, "roll", "exp"),
            P(None, "roll", "exp"),
            P(None, "roll", "exp"),
            P(None, "roll", "exp"),
            P(None, "roll", None),
            P("exp", None, None),
        ),
        out_specs=(P(None, "roll", "exp"), P(None, "roll", "exp")),
        check_vma=False,
    )
```

time: 538 us -> 92.4 us (0.17)
  the two profiles are of different devices: /device:TPU:28 before, /device:TPU:0 now
where the time goes in v1:
time: 92.4 us; the launch traced here: 91.8 us
  waiting for transfers between devices  35.5 us (38%)
  starting transfers between devices  25.4 us (27%)
  Pallas kernels  17 us (18%)
  local copies, waits for them, and re-layouts  13 us (14%)
    ppermute x3, waiting for transfers between devices, on_device(): lax.ppermute(own, 'roll', [(i, (i - width * h) % group) for i in range(gr...  17.9 us
    pallas_call x6, Pallas kernels, call(): pl.pallas_call(functools.partial(kernel, geo), out_shape=out, in_specs=[p...  17 us
    ppermute x3, waiting for transfers between devices, on_device(): lax.ppermute(parcels[s], 'roll', mates(1, s))  12.8 us
    all_to_all x1, starting transfers between devices, on_device(): got = lax.all_to_all(reads, 'roll', 0, 0, tiled=True)  8.31 us
    unnamed x28, local copies, waits for them, and re-layouts  7.92 us
    ppermute x3, starting transfers between devices, on_device(): lax.ppermute(own, 'roll', [(i, (i - width * h) % group) for i in range(gr...  4.9 us
    ppermute x3, waiting for transfers between devices, on_device(): lax.ppermute(results[s], 'roll', mates(-1, s))  4.79 us
    ppermute x3, starting transfers between devices, on_device(): lax.ppermute(parcels[s], 'roll', mates(1, s))  4.68 us
  transfers between devices with their start and end apart: 12, of which 8 were waited for; matrix products, arithmetic and copies ran while one was open for 3% of the time, Pallas kernels for 12%

profile of v1, /device:TPU:0, one launch (start us, length us, event | category | flops | bytes accessed | tf_op | source)
XLA Modules:
  0.0 91.8 jit_solution(1145672199145273565)
XLA Ops:
  0.6 0.8 copy.17.b_ref
  1.4 1.0 %copy-done.3 = f32[2,32,2048]{2,1,0:T(8,128)S(1)} copy-done((f32[2,32,2048]{2,1,0:T(8,128)S(1)}, f32[2,32,2048]{2,1,0:T(8,128)}, u32[]{:S(2)}) %copy-start.3) | copy-done | bytes 524312
  2.5 0.9 %copy-done.7 = bf16[2,32,2048]{2,1,0:T(8,128)(2,1)S(1)} copy-done((bf16[2,32,2048]{2,1,0:T(8,128)(2,1)S(1)}, bf16[2,32,2048]{2,1,0:T(8,128)(2,1)}, u32[]{:S(2)}) %copy-start.7) | copy-done | bytes 262168
  3.4 0.9 %copy-done.8 = bf16[2,32,2048]{2,1,0:T(8,128)(2,1)S(1)} copy-done((bf16[2,32,2048]{2,1,0:T(8,128)(2,1)S(1)}, bf16[2,32,2048]{2,1,0:T(8,128)(2,1)}, u32[]{:S(2)}) %copy-start.8) | copy-done | bytes 262168
  4.4 5.1 %reads_kernel.1 = (bf16[64,2048]{1,0:T(8,128)(2,1)S(1)}, f32[3,32,16]{2,1,0:T(8,128)S(1)}) custom-call(bf16[2,32,2048]{2,1,0:T(8,128)(2,1)S(1)} %copy-done.7, bf16[2,32,2048]{2,1,0:T(8,128)(2,1)S(1)} %copy-done.8, f32[2,32,2048]{2,1,0:T(8,128)S(1)} %copy-done.3, f32[2,32,16]{2,1,0:T(8,128)S(1)} %copy.17.b_ref), custom_call_target="tpu_custom_call" | custom-call | tf_op jit(solution)/shard_map/reads_kernel/pallas_call | solution.py:268
  9.5 0.8 all_to_all.14
  10.3 8.3 %all-to-all-start = ((bf16[16,4,2048]{2,1,0:T(4,128)(2,1)}), bf16[16,4,2048]{2,1,0:T(4,128)(2,1)S(1)}, u32[]{:S(2)}, u32[]{:S(2)}) async-start(bf16[16,4,2048]{2,1,0:T(4,128)(2,1)} %all_to_all.14), calls=%async_computation | async-start | bytes 524288 | tf_op jit(solution)/shard_map/all_to_all | solution.py:341
  18.6 0.0 copy-start.12
  18.6 0.0 copy-start
  18.6 3.8 %collective-permute-start.3 = (bf16[128,576]{1,0:T(8,128)(2,1)S(1)}, bf16[128,576]{1,0:T(8,128)(2,1)S(1)}, u32[]{:S(2)}, u32[]{:S(2)}) collective-permute-start(bf16[128,576]{1,0:T(8,128)(2,1)S(1)} %bitcast.7), channel_id=1, source_target_pairs={{0,24},{2,26},{4,28},{6,30},{8,0},{10,2},{12,4},{14,6},{16,8},{18,... | collective-permute-start | bytes 442376 | tf_op jit(solution)/shard_map/ppermute | solution.py:345
  22.4 0.0 collective-permute-start.4
  22.4 1.1 %collective-permute-start.5 = (bf16[128,576]{1,0:T(8,128)(2,1)S(1)}, bf16[128,576]{1,0:T(8,128)(2,1)S(1)}, u32[]{:S(2)}, u32[]{:S(2)}) collective-permute-start(bf16[128,576]{1,0:T(8,128)(2,1)S(1)} %bitcast.9), channel_id=1, source_target_pairs={{0,8},{2,10},{4,12},{6,14},{8,16},{10,18},{12,20},{14,22},{16,24},... | collective-permute-start | bytes 442376 | tf_op jit(solution)/shard_map/ppermute | solution.py:345
  23.5 5.0 %collective-permute-done.3 = bf16[128,576]{1,0:T(8,128)(2,1)S(1)} collective-permute-done((bf16[128,576]{1,0:T(8,128)(2,1)S(1)}, bf16[128,576]{1,0:T(8,128)(2,1)S(1)}, u32[]{:S(2)}, u32[]{:S(2)}) %collective-permute-start.3) | collective-permute-done | bytes 147488 | tf_op jit(solution)/shard_map/ppermute | solution.py:345
  28.6 12.8 %collective-permute-done.4 = bf16[128,576]{1,0:T(8,128)(2,1)S(1)} collective-permute-done((bf16[128,576]{1,0:T(8,128)(2,1)S(1)}, bf16[128,576]{1,0:T(8,128)(2,1)S(1)}, u32[]{:S(2)}, u32[]{:S(2)}) %collective-permute-start.4) | collective-permute-done | bytes 147488 | tf_op jit(solution)/shard_map/ppermute | solution.py:345
  41.4 0.0 collective-permute-done.5
  41.4 0.1 pad_maximum_fusion.refs_4_
  41.5 1.1 %copy.19 = bf16[512,576]{0,1:T(8,128)(2,1)} copy(bf16[512,576]{1,0:T(8,128)(2,1)S(1)} %pad_maximum_fusion.refs_4_) | data formatting | bytes 1179648 | tf_op jit(solution)/shard_map/concatenate | solution.py:348
  42.6 0.1 copy.18.counts_ref
  42.6 0.1 all_to_all.16.r_ref
  42.7 0.0 copy-start.9
  42.7 1.3 %state_kernel.1 = bf16[64,2048]{1,0:T(8,128)(2,1)S(1)} custom-call(s32[16,4]{1,0:T(8,128)S(1)} %copy.18.counts_ref, bf16[64,2048]{1,0:T(8,128)(2,1)S(1)} %all_to_all.16.r_ref, bf16[4,16,128,128]{3,2,1,0:T(8,128)(2,1)S(1)} %copy-done), custom_call_target="tpu_custom_call" | custom-call | tf_op jit(solution)/shard_map/state_kernel/pallas_call | solution.py:268
  44.1 0.8 all_to_all.17
  44.9 4.3 %all-to-all-start.1 = ((bf16[16,4,2048]{2,1,0:T(4,128)(2,1)}), bf16[16,4,2048]{2,1,0:T(4,128)(2,1)}, u32[]{:S(2)}, u32[]{:S(2)}) async-start(bf16[16,4,2048]{2,1,0:T(4,128)(2,1)} %all_to_all.17), calls=%async_computation.1 | async-start | bytes 524288 | tf_op jit(solution)/shard_map/all_to_all | solution.py:370
  49.2 0.0 copy-start.1
  49.3 0.0 copy-start.2
  49.3 1.4 %copy-done.2 = bf16[2,32,9216]{2,1,0:T(8,128)(2,1)S(1)} copy-done((bf16[2,32,9216]{2,1,0:T(8,128)(2,1)S(1)}, bf16[2,32,9216]{2,1,0:T(8,128)(2,1)}, u32[]{:S(2)}) %copy-start.2) | copy-done | bytes 1179672
  50.7 1.5 %send_kernel.1 = (bf16[16,9856]{1,0:T(8,128)(2,1)S(1)}, bf16[16,9856]{1,0:T(8,128)(2,1)}, bf16[16,9856]{1,0:T(8,128)(2,1)}, bf16[16,9856]{1,0:T(8,128)(2,1)}) custom-call(bf16[64,9216]{1,0:T(8,128)(2,1)S(1)} %bitcast.4, bf16[64,576]{1,0:T(8,128)(2,1)S(1)} %bitcast.5), custom_call_target="tpu_custom_call" | custom-call | tf_op jit(solution)/shard_map/send_kernel/pallas_call | solution.py:268
  52.1 0.7 copy-done.4
  52.9 1.7 %collective-permute-start = (bf16[16,9856]{1,0:T(8,128)(2,1)}, bf16[16,9856]{1,0:T(8,128)(2,1)}, u32[]{:S(2)}, u32[]{:S(2)}) collective-permute-start(bf16[16,9856]{1,0:T(8,128)(2,1)} %get-tuple-element.15), channel_id=1, source_target_pairs={{0,2},{2,4},{4,6},{6,0},{8,10},{10,12},{12,14},{14,8},{16,18},{18,... | collective-permute-start | bytes 946184 | tf_op jit(solution)/shard_map/ppermute | solution.py:361
  54.6 1.5 %collective-permute-start.1 = (bf16[16,9856]{1,0:T(8,128)(2,1)}, bf16[16,9856]{1,0:T(8,128)(2,1)}, u32[]{:S(2)}, u32[]{:S(2)}) collective-permute-start(bf16[16,9856]{1,0:T(8,128)(2,1)} %get-tuple-element.16), channel_id=1, source_target_pairs={{0,4},{2,6},{4,0},{6,2},{8,12},{10,14},{12,8},{14,10},{16,20},{18,... | collective-permute-start | bytes 946184 | tf_op jit(solution)/shard_map/ppermute | solution.py:361
  56.1 1.5 %collective-permute-start.2 = (bf16[16,9856]{1,0:T(8,128)(2,1)}, bf16[16,9856]{1,0:T(8,128)(2,1)}, u32[]{:S(2)}, u32[]{:S(2)}) collective-permute-start(bf16[16,9856]{1,0:T(8,128)(2,1)} %get-tuple-element.17), channel_id=1, source_target_pairs={{0,6},{2,0},{4,2},{6,4},{8,14},{10,8},{12,10},{14,12},{16,22},{18,... | collective-permute-start | bytes 946184 | tf_op jit(solution)/shard_map/ppermute | solution.py:361
  57.6 1.4 %copy.21.refs_5_ = bf16[512,576]{1,0:T(8,128)(2,1)S(1)} copy(bf16[512,576]{0,1:T(8,128)(2,1)} %collective-permute-done.6) | data formatting | bytes 1179648 | tf_op jit(solution)/shard_map/ppermute | solution.py:350
  58.9 6.7 %collective-permute-done.refs_1_ = bf16[16,9856]{1,0:T(8,128)(2,1)} collective-permute-done((bf16[16,9856]{1,0:T(8,128)(2,1)}, bf16[16,9856]{1,0:T(8,128)(2,1)}, u32[]{:S(2)}, u32[]{:S(2)}) %collective-permute-start) | collective-permute-done | bytes 315424 | tf_op jit(solution)/shard_map/ppermute | solution.py:361
  65.6 6.1 %collective-permute-done.1.refs_2_ = bf16[16,9856]{1,0:T(8,128)(2,1)} collective-permute-done((bf16[16,9856]{1,0:T(8,128)(2,1)}, bf16[16,9856]{1,0:T(8,128)(2,1)}, u32[]{:S(2)}, u32[]{:S(2)}) %collective-permute-start.1) | collective-permute-done | bytes 315424 | tf_op jit(solution)/shard_map/ppermute | solution.py:361
  71.7 0.1 collective-permute-done.2.refs_3_
  71.8 1.0 %copy-done.5 = bf16[16,9856]{1,0:T(8,128)(2,1)S(1)} copy-done((bf16[16,9856]{1,0:T(8,128)(2,1)S(1)}, bf16[16,9856]{1,0:T(8,128)(2,1)}, u32[]{:S(2)}) %copy-start.5) | copy-done | bytes 315416
  72.7 7.1 %latent_kernel.1 = (bf16[16,2048]{1,0:T(8,128)(2,1)S(1)}, bf16[16,2048]{1,0:T(8,128)(2,1)S(1)}, bf16[16,2048]{1,0:T(8,128)(2,1)S(1)}, bf16[16,2048]{1,0:T(8,128)(2,1)S(1)}) custom-call(s32[16,4]{1,0:T(8,128)S(1)} %copy.18.counts_ref, s32[64]{0:T(128)S(1)} %copy-done.10, bf16[16,512,128]{2,1,0:T(8,128)(2,1)S(1)} %copy-done.1, bf16[16,9856]{1,0:T(8,128)(2,1)S(1)} %copy-done.5, ...), custom_call_target="tpu_custom_call" | custom-call | tf_op jit(solution)/shard_map/latent_kernel/pallas_call | solution.py:268
  79.9 1.5 %collective-permute-start.7 = (bf16[16,2048]{1,0:T(8,128)(2,1)S(1)}, bf16[16,2048]{1,0:T(8,128)(2,1)S(1)}, u32[]{:S(2)}, u32[]{:S(2)}) collective-permute-start(bf16[16,2048]{1,0:T(8,128)(2,1)S(1)} %get-tuple-element.19), channel_id=1, source_target_pairs={{0,6},{2,0},{4,2},{6,4},{8,14},{10,8},{12,10},{14,12},{16,22},{18,... | collective-permute-start | bytes 196616 | tf_op jit(solution)/shard_map/ppermute | solution.py:386
  81.4 1.3 %collective-permute-start.8 = (bf16[16,2048]{1,0:T(8,128)(2,1)S(1)}, bf16[16,2048]{1,0:T(8,128)(2,1)S(1)}, u32[]{:S(2)}, u32[]{:S(2)}) collective-permute-start(bf16[16,2048]{1,0:T(8,128)(2,1)S(1)} %get-tuple-element.20), channel_id=1, source_target_pairs={{0,4},{2,6},{4,0},{6,2},{8,12},{10,14},{12,8},{14,10},{16,20},{18,... | collective-permute-start | bytes 196616 | tf_op jit(solution)/shard_map/ppermute | solution.py:386
  82.7 0.4 collective-permute-start.9
  83.0 1.1 %collective-permute-done.7.refs_1_ = bf16[16,2048]{1,0:T(8,128)(2,1)S(1)} collective-permute-done((bf16[16,2048]{1,0:T(8,128)(2,1)S(1)}, bf16[16,2048]{1,0:T(8,128)(2,1)S(1)}, u32[]{:S(2)}, u32[]{:S(2)}) %collective-permute-start.7) | collective-permute-done | bytes 65568 | tf_op jit(solution)/shard_map/ppermute | solution.py:386
  84.2 2.2 %collective-permute-done.8.refs_2_ = bf16[16,2048]{1,0:T(8,128)(2,1)S(1)} collective-permute-done((bf16[16,2048]{1,0:T(8,128)(2,1)S(1)}, bf16[16,2048]{1,0:T(8,128)(2,1)S(1)}, u32[]{:S(2)}, u32[]{:S(2)}) %collective-permute-start.8) | collective-permute-done | bytes 65568 | tf_op jit(solution)/shard_map/ppermute | solution.py:386
  86.3 1.5 %collective-permute-done.9.refs_3_ = bf16[16,2048]{1,0:T(8,128)(2,1)S(1)} collective-permute-done((bf16[16,2048]{1,0:T(8,128)(2,1)S(1)}, bf16[16,2048]{1,0:T(8,128)(2,1)S(1)}, u32[]{:S(2)}, u32[]{:S(2)}) %collective-permute-start.9) | collective-permute-done | bytes 65568 | tf_op jit(solution)/shard_map/ppermute | solution.py:386
  87.8 0.9 mla_out_kernel.1
  88.8 1.0 %all_to_all.19.y_ref = bf16[64,2048]{1,0:T(8,128)(2,1)S(1)} reshape(bf16[16,4,2048]{2,1,0:T(4,128)(2,1)} %all-to-all-done.1) | data formatting | bytes 524288 | tf_op jit(solution)/shard_map/all_to_all | solution.py:370
  89.8 0.0 copy-start.6
  89.8 0.9 %copy-done.6 = bf16[2,32,2048]{2,1,0:T(8,128)(2,1)S(1)} copy-done((bf16[2,32,2048]{2,1,0:T(8,128)(2,1)S(1)}, bf16[2,32,2048]{2,1,0:T(8,128)(2,1)}, u32[]{:S(2)}) %copy-start.6) | copy-done | bytes 262168
  90.7 1.0 %kda_out_kernel.1 = bf16[2,32,2048]{2,1,0:T(8,128)(2,1)} custom-call(bf16[64,2048]{1,0:T(8,128)(2,1)S(1)} %all_to_all.19.y_ref, f32[3,32,16]{2,1,0:T(8,128)S(1)} %get-tuple-element.13.a_ref, bf16[2,32,2048]{2,1,0:T(8,128)(2,1)S(1)} %copy-done.6), custom_call_target="tpu_custom_call" | custom-call | tf_op jit(solution)/shard_map/kda_out_kernel/pallas_call | solution.py:268
  (17 shorter events, 0.0 us)
Async XLA Ops:
  1.4 1.0 %copy-start.3 = (f32[2,32,2048]{2,1,0:T(8,128)S(1)}, f32[2,32,2048]{2,1,0:T(8,128)}, u32[]{:S(2)}) copy-start(f32[2,32,2048]{2,1,0:T(8,128)} %g_ref.1) | copy-start | bytes 1572868
  2.5 0.9 %copy-start.7 = (bf16[2,32,2048]{2,1,0:T(8,128)(2,1)S(1)}, bf16[2,32,2048]{2,1,0:T(8,128)(2,1)}, u32[]{:S(2)}) copy-start(bf16[2,32,2048]{2,1,0:T(8,128)(2,1)} %q_ref.1) | copy-start | bytes 786436
  3.4 0.9 %copy-start.8 = (bf16[2,32,2048]{2,1,0:T(8,128)(2,1)S(1)}, bf16[2,32,2048]{2,1,0:T(8,128)(2,1)}, u32[]{:S(2)}) copy-start(bf16[2,32,2048]{2,1,0:T(8,128)(2,1)} %k_ref.1) | copy-start | bytes 786436
  4.4 14.2 %copy-start.11 = (bf16[4,32,576]{2,1,0:T(8,128)(2,1)S(1)}, bf16[4,32,576]{2,1,0:T(8,128)(2,1)}, u32[]{:S(2)}) copy-start(bf16[4,32,576]{2,1,0:T(8,128)(2,1)} %param.13) | copy-start | bytes 442372
  10.3 32.4 %all-to-all-start = ((bf16[16,4,2048]{2,1,0:T(4,128)(2,1)}), bf16[16,4,2048]{2,1,0:T(4,128)(2,1)S(1)}, u32[]{:S(2)}, u32[]{:S(2)}) async-start(bf16[16,4,2048]{2,1,0:T(4,128)(2,1)} %all_to_all.14), calls=%async_computation | async-start | bytes 524288 | tf_op jit(solution)/shard_map/all_to_all | solution.py:341
  18.6 24.0 %copy-start.12 = (s32[16,4]{0,1:T(4,128)S(1)}, s32[16,4]{0,1:T(4,128)}, u32[]{:S(2)}) copy-start(s32[16,4]{0,1:T(4,128)} %param.15) | copy-start | bytes 772
  18.6 24.1 %copy-start = (bf16[4,16,128,128]{3,2,1,0:T(8,128)(2,1)S(1)}, bf16[4,16,128,128]{3,2,1,0:T(8,128)(2,1)}, u32[]{:S(2)}) copy-start(bf16[4,16,128,128]{3,2,1,0:T(8,128)(2,1)} %s_ref.1) | copy-start | bytes 6291460
  18.6 9.9 %collective-permute-start.3 = (bf16[128,576]{1,0:T(8,128)(2,1)S(1)}, bf16[128,576]{1,0:T(8,128)(2,1)S(1)}, u32[]{:S(2)}, u32[]{:S(2)}) collective-permute-start(bf16[128,576]{1,0:T(8,128)(2,1)S(1)} %bitcast.7), channel_id=1, source_target_pairs={{0,24},{2,26},{4,28},{6,30},{8,0},{10,2},{12,4},{14,6},{16,8},{18,... | collective-permute-start | bytes 442376 | tf_op jit(solution)/shard_map/ppermute | solution.py:345
  22.4 19.0 %collective-permute-start.4 = (bf16[128,576]{1,0:T(8,128)(2,1)S(1)}, bf16[128,576]{1,0:T(8,128)(2,1)S(1)}, u32[]{:S(2)}, u32[]{:S(2)}) collective-permute-start(bf16[128,576]{1,0:T(8,128)(2,1)S(1)} %bitcast.8), channel_id=1, source_target_pairs={{0,16},{2,18},{4,20},{6,22},{8,24},{10,26},{12,28},{14,30},{16,0},... | collective-permute-start | bytes 442376 | tf_op jit(solution)/shard_map/ppermute | solution.py:345
  22.4 19.0 %collective-permute-start.5 = (bf16[128,576]{1,0:T(8,128)(2,1)S(1)}, bf16[128,576]{1,0:T(8,128)(2,1)S(1)}, u32[]{:S(2)}, u32[]{:S(2)}) collective-permute-start(bf16[128,576]{1,0:T(8,128)(2,1)S(1)} %bitcast.9), channel_id=1, source_target_pairs={{0,8},{2,10},{4,12},{6,14},{8,16},{10,18},{12,20},{14,22},{16,24},... | collective-permute-start | bytes 442376 | tf_op jit(solution)/shard_map/ppermute | solution.py:345
  42.6 15.0 %collective-permute-start.6 = (bf16[512,576]{0,1:T(8,128)(2,1)}, bf16[512,576]{0,1:T(8,128)(2,1)}, u32[]{:S(2)}, u32[]{:S(2)}) collective-permute-start(bf16[512,576]{0,1:T(8,128)(2,1)} %copy.19), channel_id=1, source_target_pairs={{0,1},{1,0},{2,3},{3,2},{4,5},{5,4},{6,7},{7,6},{8,9},{9,8},{10,11... | collective-permute-start | bytes 1769480 | tf_op jit(solution)/shard_map/ppermute | solution.py:350
  42.7 6.5 %copy-start.9 = (bf16[2,32,576]{2,1,0:T(8,128)(2,1)S(1)}, bf16[2,32,576]{2,1,0:T(8,128)(2,1)}, u32[]{:S(2)}) copy-start(bf16[2,32,576]{2,1,0:T(8,128)(2,1)} %param.22) | copy-start | bytes 221188
  44.9 26.9 %copy-start.10 = (s32[64]{0:T(128)S(1)}, s32[64]{0:T(128)}, u32[]{:S(2)}) copy-start(s32[64]{0:T(128)} %len_ref.1) | copy-start | bytes 772
  44.9 43.9 %all-to-all-start.1 = ((bf16[16,4,2048]{2,1,0:T(4,128)(2,1)}), bf16[16,4,2048]{2,1,0:T(4,128)(2,1)}, u32[]{:S(2)}, u32[]{:S(2)}) async-start(bf16[16,4,2048]{2,1,0:T(4,128)(2,1)} %all_to_all.17), calls=%async_computation.1 | async-start | bytes 524288 | tf_op jit(solution)/shard_map/all_to_all | solution.py:370
  49.2 22.5 %copy-start.1 = (bf16[16,512,128]{2,1,0:T(8,128)(2,1)S(1)}, bf16[16,512,128]{2,1,0:T(8,128)(2,1)}, u32[]{:S(2)}) copy-start(bf16[16,512,128]{2,1,0:T(8,128)(2,1)} %w_ref.1) | copy-start | bytes 6291460
  49.3 1.4 %copy-start.2 = (bf16[2,32,9216]{2,1,0:T(8,128)(2,1)S(1)}, bf16[2,32,9216]{2,1,0:T(8,128)(2,1)}, u32[]{:S(2)}) copy-start(bf16[2,32,9216]{2,1,0:T(8,128)(2,1)} %param.21) | copy-start | bytes 3538948
  52.1 0.7 copy-start.4
  52.9 12.7 %collective-permute-start = (bf16[16,9856]{1,0:T(8,128)(2,1)}, bf16[16,9856]{1,0:T(8,128)(2,1)}, u32[]{:S(2)}, u32[]{:S(2)}) collective-permute-start(bf16[16,9856]{1,0:T(8,128)(2,1)} %get-tuple-element.15), channel_id=1, source_target_pairs={{0,2},{2,4},{4,6},{6,0},{8,10},{10,12},{12,14},{14,8},{16,18},{18,... | collective-permute-start | bytes 946184 | tf_op jit(solution)/shard_map/ppermute | solution.py:361
  54.6 17.1 %collective-permute-start.1 = (bf16[16,9856]{1,0:T(8,128)(2,1)}, bf16[16,9856]{1,0:T(8,128)(2,1)}, u32[]{:S(2)}, u32[]{:S(2)}) collective-permute-start(bf16[16,9856]{1,0:T(8,128)(2,1)} %get-tuple-element.16), channel_id=1, source_target_pairs={{0,4},{2,6},{4,0},{6,2},{8,12},{10,14},{12,8},{14,10},{16,20},{18,... | collective-permute-start | bytes 946184 | tf_op jit(solution)/shard_map/ppermute | solution.py:361
  56.1 15.7 %collective-permute-start.2 = (bf16[16,9856]{1,0:T(8,128)(2,1)}, bf16[16,9856]{1,0:T(8,128)(2,1)}, u32[]{:S(2)}, u32[]{:S(2)}) collective-permute-start(bf16[16,9856]{1,0:T(8,128)(2,1)} %get-tuple-element.17), channel_id=1, source_target_pairs={{0,6},{2,0},{4,2},{6,4},{8,14},{10,8},{12,10},{14,12},{16,22},{18,... | collective-permute-start | bytes 946184 | tf_op jit(solution)/shard_map/ppermute | solution.py:361
  71.8 1.0 %copy-start.5 = (bf16[16,9856]{1,0:T(8,128)(2,1)S(1)}, bf16[16,9856]{1,0:T(8,128)(2,1)}, u32[]{:S(2)}) copy-start(bf16[16,9856]{1,0:T(8,128)(2,1)} %copy-done.4) | copy-start | bytes 946180
  79.9 4.3 %collective-permute-start.7 = (bf16[16,2048]{1,0:T(8,128)(2,1)S(1)}, bf16[16,2048]{1,0:T(8,128)(2,1)S(1)}, u32[]{:S(2)}, u32[]{:S(2)}) collective-permute-start(bf16[16,2048]{1,0:T(8,128)(2,1)S(1)} %get-tuple-element.19), channel_id=1, source_target_pairs={{0,6},{2,0},{4,2},{6,4},{8,14},{10,8},{12,10},{14,12},{16,22},{18,... | collective-permute-start | bytes 196616 | tf_op jit(solution)/shard_map/ppermute | solution.py:386
  81.4 5.0 %collective-permute-start.8 = (bf16[16,2048]{1,0:T(8,128)(2,1)S(1)}, bf16[16,2048]{1,0:T(8,128)(2,1)S(1)}, u32[]{:S(2)}, u32[]{:S(2)}) collective-permute-start(bf16[16,2048]{1,0:T(8,128)(2,1)S(1)} %get-tuple-element.20), channel_id=1, source_target_pairs={{0,4},{2,6},{4,0},{6,2},{8,12},{10,14},{12,8},{14,10},{16,20},{18,... | collective-permute-start | bytes 196616 | tf_op jit(solution)/shard_map/ppermute | solution.py:386
  82.7 5.2 %collective-permute-start.9 = (bf16[16,2048]{1,0:T(8,128)(2,1)S(1)}, bf16[16,2048]{1,0:T(8,128)(2,1)S(1)}, u32[]{:S(2)}, u32[]{:S(2)}) collective-permute-start(bf16[16,2048]{1,0:T(8,128)(2,1)S(1)} %get-tuple-element.21), channel_id=1, source_target_pairs={{0,2},{2,4},{4,6},{6,0},{8,10},{10,12},{12,14},{14,8},{16,18},{18,... | collective-permute-start | bytes 196616 | tf_op jit(solution)/shard_map/ppermute | solution.py:386
  89.8 1.0 %copy-start.6 = (bf16[2,32,2048]{2,1,0:T(8,128)(2,1)S(1)}, bf16[2,32,2048]{2,1,0:T(8,128)(2,1)}, u32[]{:S(2)}) copy-start(bf16[2,32,2048]{2,1,0:T(8,128)(2,1)} %v_ref.1) | copy-start | bytes 786436

commit v2 on v0

v2 whole, which is shorter than its diff:
```python
import functools

import jax
import jax.numpy as jnp
from jax import lax
from jax.experimental import pallas as pl
from jax.experimental.pallas import tpu as pltpu
from jax.sharding import PartitionSpec as P

F32 = jnp.float32
BF16 = jnp.bfloat16
NEG = -1e30


def split(x, n):
    if n & (n - 1) == 0:
        return lax.shift_right_logical(x, jnp.full_like(x, n.bit_length() - 1)), x & (n - 1)
    return lax.div(x, jnp.full_like(x, n)), lax.rem(x, jnp.full_like(x, n))


def wrap(x, n):
    return jnp.where(x < 0, x + n, x)


def lanes(shape, dim):
    return lax.broadcasted_iota(jnp.int32, shape, dim)


def prompt_at(counts_ref, owner, j):
    bound = jnp.int32(0)
    k = jnp.zeros_like(j)
    for i in range(counts_ref.shape[0]):
        bound = bound + counts_ref[i, owner]
        k = k + (bound <= j).astype(jnp.int32)
    return k


def fan_rows(geo, shape, dim, me):
    group, slots, steps, parts, per = (geo[n] for n in ("group", "slots", "steps", "parts", "per"))
    other, rest = split(lanes(shape, dim), parts * slots * steps)
    part, rest = split(rest, slots * steps)
    slot, step = split(rest, steps)
    j = wrap(other - me, group) + group * slot
    return part, jnp.where(j < per, step * per + j, -1)


def one_hot(hit):
    return hit.astype(F32).astype(BF16)


def dot(a, b):
    return lax.dot_general(a, b, (((1,), (0,)), ((), ())), preferred_element_type=F32)


def dot_first(a, b):
    return lax.dot_general(a, b, (((0,), (0,)), ((), ())), preferred_element_type=F32)


def dot_t(a, b):
    return lax.dot_general(a, b, (((1,), (1,)), ((), ())), preferred_element_type=F32)


def row_sums(x, ones):
    return dot(x.astype(BF16), ones)


def reads_kernel(geo, q_hbm, k_hbm, g_hbm, b_hbm, r_ref, a_ref, q_ref, k_ref, g_ref, b_ref, raw, sems):
    _, per, width = q_ref.shape
    heads = geo["heads"]
    dk = width // heads
    parts = geo["parts"]
    wide = width // parts
    beta_copy = pltpu.make_async_copy(b_hbm, b_ref, sems.at[parts, 0])
    beta_copy.start()
    copies = []
    for c in range(parts):
        sl = pl.ds(c * wide, wide)
        for n, (src, dst) in enumerate(((q_hbm, q_ref), (k_hbm, k_ref), (g_hbm, g_ref))):
            copies.append(pltpu.make_async_copy(src.at[:, :, sl], dst.at[:, :, sl], sems.at[c, n]))
            copies[-1].start()
    me = lax.axis_index("roll")
    unit = 2 * dk
    ones = one_hot(split(lanes((unit, unit), 0), dk)[0] == split(lanes((unit, unit), 1), dk)[0])
    rows, rows_in = r_ref.shape[0], raw.shape[0]
    part, place = fan_rows(geo, (rows, rows_in), 0, me)
    pick = one_hot((lanes((rows, rows_in), 1) == part * (2 * per) + place) & (place >= 0))
    lane = lanes((per, a_ref.shape[2]), 1)
    coef = [jnp.zeros((per, a_ref.shape[2]), F32) for _ in range(3)]
    spread = one_hot(lanes((heads, width), 0) == split(lanes((heads, width), 1), dk)[0])
    betas = []
    beta_copy.wait()
    for t in range(2):
        beta = b_ref[t]
        high = beta.astype(BF16)
        low = (beta - high.astype(F32)).astype(BF16)
        betas.append(dot_first(high, spread) + dot_first(low, spread))
    for c in range(parts):
        for copy in copies[3 * c : 3 * c + 3]:
            copy.wait()
        for at in range(c * wide, (c + 1) * wide, unit):
            sl = slice(at, at + unit)
            q1, q2 = q_ref[0, :, sl].astype(F32), q_ref[1, :, sl].astype(F32)
            k1, k2 = k_ref[0, :, sl].astype(F32), k_ref[1, :, sl].astype(F32)
            d1, d2 = jnp.exp(-g_ref[0, :, sl]), jnp.exp(-g_ref[1, :, sl])
            h = at // dk

            dq2, dk2 = d2 * q2, d2 * k2
            terms = (q1 * q1, k1 * k1, q2 * q2, k2 * k2, k1 * q1, k2 * q2, k1 * dq2, k1 * dk2)
            sums = row_sums(jnp.concatenate(terms, axis=0), ones)
            s = [sums[n * per : (n + 1) * per] for n in range(8)]
            rq1, rk1, rq2, rk2 = (lax.rsqrt(x + 1e-06) for x in s[:4])
            b1, b2 = betas[0][:, sl], betas[1][:, sl]
            a11 = b1 * (s[4] * rk1 * rq1)
            a22 = b2 * (s[5] * rk2 * rq2)
            a22k = a22 * rk2
            a21 = b1 * (rk1 * (rq2 * s[6] - a22k * s[7]))
            r1 = d1 * (rq1 * q1 - (a11 * rk1) * k1)
            r2 = d1 * (rq2 * dq2 - a22k * dk2 - (a21 * rk1) * k1)
            to = slice(at - c * wide, at - c * wide + unit)
            raw[2 * c * per : (2 * c + 1) * per, to] = r1.astype(BF16)
            raw[(2 * c + 1) * per : (2 * c + 2) * per, to] = r2.astype(BF16)
            for n, a in enumerate((a11, a22, a21)):
                for m in range(2):
                    coef[n] = jnp.where(lane == h + m, a[:, m * dk : (m + 1) * dk], coef[n])
    for n in range(3):
        a_ref[n] = coef[n]
    r_ref[...] = dot(pick, raw[...]).astype(BF16)


def state_kernel(geo, s_hbm, c_hbm, *refs):
    r_ref, y_ref, s_ref, r_all, y_all, counts_ref, sems = refs[-7:]
    rows, wide = r_ref.shape
    prompts, heads, dk, dv = s_ref.shape
    me = lax.axis_index("roll")
    group, slots, steps, parts = geo["group"], geo["slots"], geo["steps"], geo["parts"]
    copies = [pltpu.make_async_copy(c_hbm, counts_ref, sems.at[parts])]
    for c in range(parts):
        sl = pl.ds(c * (heads // parts), heads // parts)
        copies.append(pltpu.make_async_copy(s_hbm.at[:, sl], s_ref.at[:, sl], sems.at[c]))
    for copy in copies:
        copy.start()
    few, own = rows // parts, slots * steps
    part, rest = split(lanes((rows, rows), 0), few)
    other, rest = split(rest, own)
    sort = one_hot(lanes((rows, rows), 1) == (other * parts + part) * own + rest)
    part, rest = split(lanes((rows, rows), 1), few)
    other, rest = split(rest, own)
    back = one_hot(lanes((rows, rows), 0) == (other * parts + part) * own + rest)
    r_all[...] = dot(sort, r_ref[...]).astype(BF16)
    copies[0].wait()
    other, rest = split(lanes((few, dk), 0), own)
    j = wrap(me - other, group) + group * split(rest, steps)[0]
    k = prompt_at(counts_ref, me, j)
    keep = [one_hot(k == p) for p in range(prompts)]
    for c in range(parts):
        copies[1 + c].wait()
        for at in range(wide // dk):
            h = c * (wide // dk) + at
            r = r_all[c * few : (c + 1) * few, at * dk : (at + 1) * dk]
            acc = dot(r * keep[0], s_ref[0, h])
            for p in range(1, prompts):
                acc = acc + dot(r * keep[p], s_ref[p, h])
            y_all[c * few : (c + 1) * few, at * dv : (at + 1) * dv] = acc.astype(BF16)
    y_ref[...] = dot(back, y_all[...]).astype(BF16)


def kda_out_kernel(geo, v_hbm, _, y_ref, a_ref, o_ref, v_ref, sem):
    copy = pltpu.make_async_copy(v_hbm, v_ref, sem)
    copy.start()
    _, per, width = v_ref.shape
    rows, wide = y_ref.shape
    heads = geo["heads"]
    dv = width // heads
    me = lax.axis_index("roll")
    parts = geo["parts"]
    shape = (2 * per * parts, rows)
    part, place = fan_rows(geo, shape, 1, me)
    pick = one_hot((lanes(shape, 0) == part * (2 * per) + place) & (place >= 0))
    y_all = dot(pick, y_ref[...])
    copy.wait()
    for c in range(parts):
        y = y_all[c * 2 * per : (c + 1) * 2 * per]
        for at in range(wide // dv):
            h = c * (wide // dv) + at
            sl = slice(h * dv, (h + 1) * dv)
            v1, v2 = v_ref[0, :, sl].astype(F32), v_ref[1, :, sl].astype(F32)
            a11, a22, a21 = (a_ref[n, :, h : h + 1] for n in range(3))
            here = y[:, at * dv : (at + 1) * dv]
            o_ref[0, :, sl] = (here[:per] + a11 * v1).astype(BF16)
            o_ref[1, :, sl] = (here[per:] + a21 * v1 + a22 * v2).astype(BF16)


def select_kernel(geo, c_hbm, *refs):
    width, depth, hops, prompts, per_mate = (
        geo[n] for n in ("width", "depth", "hops", "prompts", "per_mate")
    )
    refs, (pool, counts_ref, sem) = refs[1:-3], refs[-3:]
    pieces, o_refs = refs[:hops], refs[hops:]
    copy = pltpu.make_async_copy(c_hbm, counts_ref, sem)
    copy.start()
    _, local, padded = pool.shape
    entry = geo["entry"]
    pool[:, :, entry:] = jnp.zeros((hops * prompts, local, padded - entry), BF16)
    for h, piece in enumerate(pieces):
        pool[h * prompts : (h + 1) * prompts, :, :entry] = piece[...]
    copy.wait()
    a, b = split(lax.axis_index("roll"), width)
    for s, o_ref in enumerate(o_refs):
        carry = (b < s).astype(jnp.int32)
        for i in range(per_mate):
            hop = wrap(i + carry - i // depth * depth - depth, depth)
            owner = wrap(a + hop - depth, depth) * width + b
            k = prompt_at(counts_ref, owner, jnp.int32(s + width * i))
            o_ref[i * local : (i + 1) * local, :] = pool[hop * prompts + k]


def query_kernel(geo, q_hbm, f_hbm, _, o_ref, n_ref, q_ref, f_ref, sems):
    total, wide = q_ref.shape
    width, per, steps, entry = geo["width"], geo["per"], geo["steps"], geo["entry"]
    padded = o_ref.shape[1]
    heads = wide // entry
    unit = 2 * entry
    n = total // width
    fresh_copy = pltpu.make_async_copy(f_hbm, f_ref, sems.at[heads // 2])
    fresh_copy.start()
    copies = []
    for c in range(heads // 2):
        sl = pl.ds(c * unit, unit)
        copies.append(pltpu.make_async_copy(q_hbm.at[:, sl], q_ref.at[:, sl], sems.at[c]))
        copies[-1].start()
    row, col = lanes((total, total), 0), lanes((total, total), 1)
    shift, rest = split(row, n)
    i, step = split(rest, steps)
    pick = one_hot(col == step * per + shift + width * i)
    fresh_copy.wait()
    n_ref[:, :entry] = dot(pick, f_ref[...]).astype(BF16)
    n_ref[:, entry:] = jnp.zeros((total, padded - entry), BF16)
    for c, copy in enumerate(copies):
        copy.wait()
        out = dot(pick, q_ref[:, c * unit : (c + 1) * unit])
        even = out[:, :padded].astype(BF16)
        odd = pltpu.roll(out[:, unit - padded :], entry, 1).astype(BF16)
        for s in range(width):
            at = (s * heads + 2 * c) * n
            o_ref[at : at + n, :] = even[s * n : (s + 1) * n]
            o_ref[at + n : at + 2 * n, :] = odd[s * n : (s + 1) * n]


def latent_kernel(geo, w_hbm, c_hbm, l_hbm, _, q_ref, n_ref, *refs):
    width, steps, per, group = geo["width"], geo["steps"], geo["per"], geo["group"]
    halves, cache, prompts, per_mate = (
        geo[n] for n in ("halves", "cache", "prompts", "per_mate")
    )
    k_refs = refs[: width * halves]
    o_ref, keys, ctx, out, w_ref, counts_ref, len_ref, sems = refs[width * halves :]
    copies = [
        pltpu.make_async_copy(src, dst, sems.at[n])
        for n, (src, dst) in enumerate(((c_hbm, counts_ref), (l_hbm, len_ref), (w_hbm, w_ref)))
    ]
    for copy in copies:
        copy.start()
    heads, rank, dv = w_ref.shape
    me = lax.axis_index("roll")
    half = lax.axis_index("exp")
    local = cache // halves
    piece = per_mate * local
    total = per_mate * cache
    n = per_mate * steps
    cols = keys.shape[0]
    keys[total + n :, :] = jnp.zeros((cols - total - n, keys.shape[1]), BF16)
    row, col = lanes((n, cols), 0), lanes((n, cols), 1)
    sample, step = split(row, steps)
    e, rest = split(col, piece)
    other, pos = split(rest, local)
    e = e + half
    pos = jnp.where(e >= halves, e - halves, e) * local + pos
    pos = jnp.where((col < total) & (other == sample), pos, cache)
    behind = row - (col - total)
    in_fresh = (col >= total) & (behind >= 0) & (behind <= step)
    copies[0].wait()
    copies[1].wait()
    for s in range(width):
        length = jnp.zeros_like(pos)
        for i in range(per_mate):
            j = s + width * i
            owner = split(me + j, group)[1]
            k = prompt_at(counts_ref, owner, jnp.int32(j))
            length = jnp.where(sample == i, len_ref[owner * prompts + k], length)
        allowed = ((pos < length) | in_fresh)[None]
        for e in range(halves):
            keys[e * piece : (e + 1) * piece, :] = k_refs[s * halves + e][...]
        keys[total : total + n, :] = n_ref[s * n : (s + 1) * n, :]
        query = q_ref[s * heads * n : (s + 1) * heads * n, :]
        scores = dot_t(query, keys[...]).reshape(heads, n, cols) * geo["scale"]
        scores = jnp.where(allowed, scores, NEG)
        top = jnp.max(scores, axis=-1, keepdims=True)
        raised = jnp.exp(scores - top)
        weights = raised / jnp.sum(raised, axis=-1, keepdims=True)
        weights = weights.reshape(heads * n, cols).astype(BF16)
        context = dot(weights, keys[:, :rank]).astype(BF16)
        for h in range(heads):
            ctx[h, s * n : (s + 1) * n, :] = context[h * n : (h + 1) * n]
    copies[2].wait()
    for h in range(heads):
        out[:, h * dv : (h + 1) * dv] = dot(ctx[h], w_ref[h]).astype(BF16)
    rows = steps * per
    shift, rest = split(lanes((rows, rows), 1), n)
    sample, step = split(rest, steps)
    place = step * per + shift + width * sample
    pick = one_hot(lanes((rows, rows), 0) == place)
    o_ref[...] = dot(pick, out[...]).astype(BF16)


def cost(us):
    return pl.CostEstimate(
        flops=2_000_000_000 * us, bytes_accessed=3_000_000 * us, transcendentals=20_000_000 * us
    )


def call(kernel, geo, out, args, hbm=0, after=0, scratch=(), mib=16, us=0):
    spaces = [pltpu.HBM] * hbm + [pl.ANY] * after + [pltpu.VMEM] * (len(args) - hbm - after)
    args = [
        pltpu.with_memory_space_constraint(x, pltpu.HBM) if s == pltpu.HBM else x
        for x, s in zip(args, spaces, strict=True)
    ]
    return pl.pallas_call(
        functools.partial(kernel, geo),
        out_shape=out,
        in_specs=[pl.BlockSpec(memory_space=s) for s in spaces],
        scratch_shapes=list(scratch),
        cost_estimate=cost(us),
        compiler_params=pltpu.CompilerParams(vmem_limit_bytes=mib * 1024 * 1024),
        name=kernel.__name__,
    )(*args)


def hold(x, first):
    return pl.pallas_call(
        lambda *refs: None,
        out_shape=tuple(jax.ShapeDtypeStruct(a.shape, a.dtype) for a in x),
        in_specs=[pl.BlockSpec(memory_space=pl.ANY)] * (len(x) + 1),
        out_specs=[pl.BlockSpec(memory_space=pl.ANY)] * len(x),
        input_output_aliases={n + 1: n for n in range(len(x))},
        cost_estimate=cost(20),
        name="hold",
    )(first, *x)


def pad_to(n, m):
    return -(-n // m) * m


def on_device(
    kda_prefill,
    latent_prefill,
    prompt_len,
    sample_counts,
    kda_q,
    kda_k,
    kda_v,
    kda_decay,
    kda_beta,
    mla_q,
    mla_new,
    w_uv,
):
    group = lax.axis_size("roll")
    halves = lax.axis_size("exp")
    steps, per, kda_width = kda_q.shape
    heads = kda_beta.shape[2]
    prompts, local, entry = latent_prefill.shape
    cache = local * halves
    _, rank, dv = w_uv.shape
    width = 4
    depth = group // width
    slots = -(-per // group)
    per_mate = per // width
    hops = min(depth, per_mate + 1)
    padded = pad_to(entry, 128)
    parts = max(1, min(16 // (slots * steps), heads // 2))
    geo = dict(
        group=group,
        halves=halves,
        steps=steps,
        per=per,
        width=width,
        depth=depth,
        slots=slots,
        hops=hops,
        prompts=prompts,
        cache=cache,
        entry=entry,
        per_mate=per_mate,
        scale=192.0**-0.5,
        heads=heads,
        parts=parts,
    )
    shape = jax.ShapeDtypeStruct

    def mates(sign, s):
        return [(i, i // width * width + (i + sign * s) % width) for i in range(group)]

    counts = sample_counts.T
    fan = (group * parts * slots * steps, kda_width // parts)
    reads, coef = call(
        reads_kernel,
        geo,
        (shape(fan, BF16), shape((3, per, 128), F32)),
        (kda_q, kda_k, kda_decay, jnp.swapaxes(kda_beta, 1, 2)),
        hbm=4,
        scratch=[
            pltpu.VMEM(kda_q.shape, BF16),
            pltpu.VMEM(kda_q.shape, BF16),
            pltpu.VMEM(kda_q.shape, F32),
            pltpu.VMEM((steps, heads, per), F32),
            pltpu.VMEM((steps * per * parts, kda_width // parts), BF16),
            pltpu.SemaphoreType.DMA((parts + 1, 3)),
        ],
    )
    got = lax.all_to_all(reads, "roll", 0, 0, tiled=True)

    column = [latent_prefill] + [
        lax.ppermute(latent_prefill, "roll", [(i, (i - width * h) % group) for i in range(group)])
        for h in range(1, hops)
    ]
    wide = mla_q.shape[2]
    rows = steps * per
    queries, fresh = call(
        query_kernel,
        geo,
        (shape((heads * rows, padded), BF16), shape((rows, padded), BF16)),
        (mla_q.reshape(rows, wide), mla_new.reshape(rows, entry), reads),
        hbm=2,
        after=1,
        scratch=[
            pltpu.VMEM((rows, wide), BF16),
            pltpu.VMEM((rows, entry), BF16),
            pltpu.SemaphoreType.DMA((heads // 2 + 1,)),
        ],
    )
    chosen = call(
        select_kernel,
        geo,
        tuple(shape((per_mate * local, padded), BF16) for _ in range(width)),
        (counts, fresh, *column),
        hbm=1,
        after=1,
        us=20,
        scratch=[
            pltpu.VMEM((hops * prompts, local, padded), BF16),
            pltpu.SMEM(counts.shape, jnp.int32),
            pltpu.SemaphoreType.DMA(()),
        ],
    )
    products = call(
        state_kernel,
        geo,
        shape(fan, BF16),
        (kda_prefill, counts, *chosen, got),
        hbm=2,
        after=width,
        us=20,
        scratch=[
            pltpu.VMEM(kda_prefill.shape, BF16),
            pltpu.VMEM(fan, BF16),
            pltpu.VMEM(fan, BF16),
            pltpu.SMEM(counts.shape, jnp.int32),
            pltpu.SemaphoreType.DMA((parts + 1,)),
        ],
    )
    back = lax.all_to_all(products, "roll", 0, 0, tiled=True)
    taken = [lax.ppermute(chosen[s], "roll", mates(-1, s)) for s in range(1, width)]
    taken = [chosen[0], *hold(taken, products)]
    caches = []
    for piece in taken:
        caches.append(piece)
        for e in range(1, halves):
            caches.append(
                lax.ppermute(piece, "exp", [(i, (i - e) % halves) for i in range(halves)])
            )
    cols = pad_to(per_mate * (cache + steps), 128)
    mla_out = call(
        latent_kernel,
        geo,
        shape((rows, heads * dv), BF16),
        (w_uv, counts, prompt_len, products, queries, fresh, *caches),
        hbm=3,
        after=1,
        us=0,
        mib=32,
        scratch=[
            pltpu.VMEM((cols, padded), BF16),
            pltpu.VMEM((heads, rows, rank), BF16),
            pltpu.VMEM((rows, heads * dv), BF16),
            pltpu.VMEM(w_uv.shape, BF16),
            pltpu.SMEM(counts.shape, jnp.int32),
            pltpu.SMEM(prompt_len.shape, jnp.int32),
            pltpu.SemaphoreType.DMA((3,)),
        ],
    )
    kda_out = call(
        kda_out_kernel, geo, shape((steps, per, kda_width), BF16), (kda_v, mla_out, back, coef), hbm=1, after=1,
        scratch=[pltpu.VMEM(kda_v.shape, BF16), pltpu.SemaphoreType.DMA(())],
    )
    return (kda_out, mla_out.reshape(steps, per, heads * dv))


def solution(mesh):
    return jax.shard_map(
        on_device,
        mesh=mesh,
        in_specs=(
            P("roll", "exp", None, None),
            P("roll", "exp", None),
            P(),
            P(),
            P(None, "roll", "exp"),
            P(None, "roll", "exp"),
            P(None, "roll", "exp"),
            P(None, "roll", "exp"),
            P(None, "roll", "exp"),
            P(None, "roll", "exp"),
            P(None, "roll", None),
            P("exp", None, None),
        ),
        out_specs=(P(None, "roll", "exp"), P(None, "roll", "exp")),
        check_vma=False,
    )
```

time: 538 us -> 57.6 us (0.11)
  the two profiles are of different devices: /device:TPU:28 before, /device:TPU:17 now
where the time goes in v2:
time: 57.6 us; the launch traced here: 57 us
  starting transfers between devices  26.6 us (46%)
  Pallas kernels  22.4 us (39%)
  waiting for transfers between devices  6.27 us (11%)
  local copies, waits for them, and re-layouts  0.96 us (2%)
  between operations  0.75 us (1%)
    pallas_call x6, Pallas kernels, call(): pl.pallas_call(functools.partial(kernel, geo), out_shape=out, in_specs=[p...  22.4 us
    ppermute x4, starting transfers between devices, on_device(): lax.ppermute(piece, 'exp', [(i, (i - e) % halves) for i in range(halves)])  8.49 us
    all_to_all x1, starting transfers between devices, on_device(): got = lax.all_to_all(reads, 'roll', 0, 0, tiled=True)  6.44 us
    all_to_all x1, starting transfers between devices, on_device(): back = lax.all_to_all(products, 'roll', 0, 0, tiled=True)  5.49 us
    ppermute x3, waiting for transfers between devices, on_device(): lax.ppermute(latent_prefill, 'roll', [(i, (i - width * h) % group) for i...  4.05 us
    ppermute x3, starting transfers between devices, on_device(): lax.ppermute(latent_prefill, 'roll', [(i, (i - width * h) % group) for i...  3.43 us
    ppermute x3, starting transfers between devices, on_device(): lax.ppermute(chosen[s], 'roll', mates(-1, s))  2.76 us
    ppermute x4, waiting for transfers between devices, on_device(): lax.ppermute(piece, 'exp', [(i, (i - e) % halves) for i in range(halves)])  1.89 us
  transfers between devices with their start and end apart: 12, of which 5 were waited for; matrix products, arithmetic and copies ran while one was open for 0% of the time, Pallas kernels for 34%

profile of v2, /device:TPU:17, one launch (start us, length us, event | category | flops | bytes accessed | tf_op | source)
XLA Modules:
  0.0 57.0 jit_solution(6780753408943100554)
XLA Ops:
  0.6 0.0 copy-start.3
  0.6 0.2 collective-permute-start
  0.9 3.2 %collective-permute-start.1 = (bf16[4,32,576]{2,1,0:T(8,128)(2,1)}, bf16[4,32,576]{2,1,0:T(8,128)(2,1)S(1)}, u32[]{:S(2)}, u32[]{:S(2)}) collective-permute-start(bf16[4,32,576]{2,1,0:T(8,128)(2,1)} %refs_1_.1), channel_id=1, source_target_pairs={{0,16},{2,18},{4,20},{6,22},{8,24},{10,26},{12,28},{14,30},{16,0},... | collective-permute-start | bytes 442376 | tf_op jit(solution)/shard_map/ppermute | solution.py:423
  4.1 0.0 collective-permute-start.2
  4.1 3.2 %reads_kernel.1 = (bf16[256,512]{1,0:T(8,128)(2,1)}, f32[3,32,128]{2,1,0:T(8,128)S(1)}) custom-call(bf16[2,32,2048]{2,1,0:T(8,128)(2,1)} %q_hbm.1, bf16[2,32,2048]{2,1,0:T(8,128)(2,1)} %k_hbm.1, f32[2,32,2048]{2,1,0:T(8,128)} %g_hbm.1, f32[2,16,32]{2,1,0:T(8,128)} %bitcast.12), custom_call_target="tpu_custom_call" | custom-call | tf_op jit(solution)/shard_map/reads_kernel/pallas_call | solution.py:326
  7.2 6.4 %all-to-all-start = ((bf16[16,16,512]{2,1,0:T(8,128)(2,1)}), bf16[16,16,512]{2,1,0:T(8,128)(2,1)}, u32[]{:S(2)}, u32[]{:S(2)}) async-start(bf16[16,16,512]{2,1,0:T(8,128)(2,1)} %bitcast.4), calls=%async_computation | async-start | bytes 524288 | tf_op jit(solution)/shard_map/all_to_all | solution.py:420
  13.7 3.1 %query_kernel.1 = (bf16[1024,640]{1,0:T(8,128)(2,1)S(1)}, bf16[64,640]{1,0:T(8,128)(2,1)S(1)}) custom-call(bf16[64,9216]{1,0:T(8,128)(2,1)} %bitcast.10, bf16[64,576]{1,0:T(8,128)(2,1)} %bitcast.11, bf16[256,512]{1,0:T(8,128)(2,1)} %get-tuple-element.13._), custom_call_target="tpu_custom_call" | custom-call | tf_op jit(solution)/shard_map/query_kernel/pallas_call | solution.py:326
  16.8 0.0 copy-start.1
  16.8 0.0 collective-permute-done.refs_2_
  16.9 0.0 collective-permute-done.1.refs_3_
  16.9 4.0 %collective-permute-done.2.refs_4_ = bf16[4,32,576]{2,1,0:T(8,128)(2,1)S(1)} collective-permute-done((bf16[4,32,576]{2,1,0:T(8,128)(2,1)}, bf16[4,32,576]{2,1,0:T(8,128)(2,1)S(1)}, u32[]{:S(2)}, u32[]{:S(2)}) %collective-permute-start.2) | collective-permute-done | bytes 147488 | tf_op jit(solution)/shard_map/ppermute | solution.py:423
  20.9 0.0 copy-done.3
  20.9 2.1 %select_kernel.1 = (bf16[256,640]{1,0:T(8,128)(2,1)}, bf16[256,640]{1,0:T(8,128)(2,1)}, bf16[256,640]{1,0:T(8,128)(2,1)}, bf16[256,640]{1,0:T(8,128)(2,1)}) custom-call(s32[4,16]{1,0:T(4,128)} %bitcast.13, bf16[64,640]{1,0:T(8,128)(2,1)S(1)} %get-tuple-element.14.refs_0_.n_ref, bf16[4,32,576]{2,1,0:T(8,128)(2,1)S(1)} %copy-done.3, ...), custom_call_target="tpu_custom_call" | custom-call | flops 40000000000 | bytes 60000000 | tf_op jit(solution)/shard_map/select_kernel/pallas_call | solution.py:326
  23.0 0.0 copy-done.1
  23.0 2.1 %collective-permute-start.4 = (bf16[256,640]{1,0:T(8,128)(2,1)}, bf16[256,640]{1,0:T(8,128)(2,1)}, u32[]{:S(2)}, u32[]{:S(2)}) collective-permute-start(bf16[256,640]{1,0:T(8,128)(2,1)} %get-tuple-element.16.refs_1_), channel_id=1, source_target_pairs={{0,6},{2,0},{4,2},{6,4},{8,14},{10,8},{12,10},{14,12},{16,22},{18,... | collective-permute-start | bytes 983048 | tf_op jit(solution)/shard_map/ppermute | solution.py:472
  25.1 0.3 collective-permute-start.5
  25.5 0.3 collective-permute-start.6
  25.8 2.9 %collective-permute-start.3 = (bf16[256,640]{1,0:T(8,128)(2,1)}, bf16[256,640]{1,0:T(8,128)(2,1)}, u32[]{:S(2)}, u32[]{:S(2)}) collective-permute-start(bf16[256,640]{1,0:T(8,128)(2,1)} %get-tuple-element.15.refs_0_), channel_id=1, source_target_pairs={{0,1},{1,0},{2,3},{3,2},{4,5},{5,4},{6,7},{7,6},{8,9},{9,8},{10,11... | collective-permute-start | bytes 983048 | tf_op jit(solution)/shard_map/ppermute | solution.py:479
  28.7 0.0 all-to-all-done
  28.7 4.1 %state_kernel.1.refs_0_._ = bf16[256,512]{1,0:T(8,128)(2,1)} custom-call(bf16[4,16,128,128]{3,2,1,0:T(8,128)(2,1)} %s_hbm.1, s32[4,16]{1,0:T(4,128)} %bitcast.14, bf16[256,640]{1,0:T(8,128)(2,1)} %get-tuple-element.15.refs_0_, bf16[256,640]{1,0:T(8,128)(2,1)} %get-tuple-element.16.refs_1_, bf16[256,640]{1,0:T(8,128)(2,1)} %get-tuple-element.17.refs_2_, ...), custom_call_target="tpu_custom_call" | custom-call | flops 40000000000 | bytes 60000000 | tf_op jit(solution)/shard_map/state_kernel/pallas_call | solution.py:326
  32.8 5.5 %all-to-all-start.1 = ((bf16[16,16,512]{2,1,0:T(8,128)(2,1)}), bf16[16,16,512]{2,1,0:T(8,128)(2,1)}, u32[]{:S(2)}, u32[]{:S(2)}) async-start(bf16[16,16,512]{2,1,0:T(8,128)(2,1)} %bitcast.6), calls=%async_computation.1 | async-start | bytes 524288 | tf_op jit(solution)/shard_map/all_to_all | solution.py:471
  38.2 0.0 collective-permute-done.4.refs_1_
  38.3 0.0 collective-permute-done.5.refs_2_
  38.3 0.3 collective-permute-done.6.refs_3_
  38.6 0.0 copy-start.2
  38.6 5.1 %collective-permute-start.7 = (bf16[256,640]{1,0:T(8,128)(2,1)}, bf16[256,640]{1,0:T(8,128)(2,1)S(1)}, u32[]{:S(2)}, u32[]{:S(2)}) collective-permute-start(bf16[256,640]{1,0:T(8,128)(2,1)} %get-tuple-element.20.refs_2_), channel_id=1, source_target_pairs={{0,1},{1,0},{2,3},{3,2},{4,5},{5,4},{6,7},{7,6},{8,9},{9,8},{10,11... | collective-permute-start | bytes 983048 | tf_op jit(solution)/shard_map/ppermute | solution.py:479
  43.7 0.1 collective-permute-start.8
  43.7 0.4 collective-permute-start.9
  44.2 0.0 collective-permute-done.3.refs_1_
  44.2 1.0 %collective-permute-done.7.refs_3_ = bf16[256,640]{1,0:T(8,128)(2,1)S(1)} collective-permute-done((bf16[256,640]{1,0:T(8,128)(2,1)}, bf16[256,640]{1,0:T(8,128)(2,1)S(1)}, u32[]{:S(2)}, u32[]{:S(2)}) %collective-permute-start.7) | collective-permute-done | bytes 327712 | tf_op jit(solution)/shard_map/ppermute | solution.py:479
  45.1 0.5 collective-permute-done.8.refs_5_
  45.6 0.5 collective-permute-done.9.refs_7_
  46.1 0.0 copy-done.2
  46.1 7.1 %latent_kernel.1._ = bf16[64,2048]{1,0:T(8,128)(2,1)} custom-call(bf16[16,512,128]{2,1,0:T(8,128)(2,1)} %w_hbm.1, s32[4,16]{1,0:T(4,128)} %bitcast.15, s32[64]{0:T(128)} %l_hbm.1, bf16[256,512]{1,0:T(8,128)(2,1)} %state_kernel.1.refs_0_._, bf16[1024,640]{1,0:T(8,128)(2,1)S(1)} %get-tuple-element.19.q_ref, bf16[64,640]{1,0:T(8,128)(2,1)S(1)} %copy-done.2, ...), custom_call_target="tpu_custom_call" | custom-call | tf_op jit(solution)/shard_map/latent_kernel/pallas_call | solution.py:326
  53.1 0.0 all-to-all-done.1
  53.2 0.0 copy-start
  53.2 0.9 %copy-done = bf16[64,2048]{1,0:T(8,128)(2,1)S(1)} copy-done((bf16[64,2048]{1,0:T(8,128)(2,1)S(1)}, bf16[64,2048]{1,0:T(8,128)(2,1)}, u32[]{:S(2)}) %copy-start) | copy-done | bytes 262168
  54.1 2.9 %kda_out_kernel.1 = bf16[2,32,2048]{2,1,0:T(8,128)(2,1)} custom-call(bf16[2,32,2048]{2,1,0:T(8,128)(2,1)} %v_hbm.1, bf16[64,2048]{1,0:T(8,128)(2,1)S(1)} %copy-done, bf16[256,512]{1,0:T(8,128)(2,1)} %bitcast.7.y_ref, f32[3,32,128]{2,1,0:T(8,128)S(1)} %get-tuple-element.23.a_ref), custom_call_target="tpu_custom_call" | custom-call | tf_op jit(solution)/shard_map/kda_out_kernel/pallas_call | solution.py:326
  (1 shorter events, 0.0 us)
Async XLA Ops:
  0.6 20.3 %copy-start.3 = (bf16[4,32,576]{2,1,0:T(8,128)(2,1)S(1)}, bf16[4,32,576]{2,1,0:T(8,128)(2,1)}, u32[]{:S(2)}) copy-start(bf16[4,32,576]{2,1,0:T(8,128)(2,1)} %refs_1_.1) | copy-start | bytes 442372
  0.6 16.2 %collective-permute-start = (bf16[4,32,576]{2,1,0:T(8,128)(2,1)}, bf16[4,32,576]{2,1,0:T(8,128)(2,1)S(1)}, u32[]{:S(2)}, u32[]{:S(2)}) collective-permute-start(bf16[4,32,576]{2,1,0:T(8,128)(2,1)} %refs_1_.1), channel_id=1, source_target_pairs={{0,24},{2,26},{4,28},{6,30},{8,0},{10,2},{12,4},{14,6},{16,8},{18,... | collective-permute-start | bytes 442376 | tf_op jit(solution)/shard_map/ppermute | solution.py:423
  0.9 16.0 %collective-permute-start.1 = (bf16[4,32,576]{2,1,0:T(8,128)(2,1)}, bf16[4,32,576]{2,1,0:T(8,128)(2,1)S(1)}, u32[]{:S(2)}, u32[]{:S(2)}) collective-permute-start(bf16[4,32,576]{2,1,0:T(8,128)(2,1)} %refs_1_.1), channel_id=1, source_target_pairs={{0,16},{2,18},{4,20},{6,22},{8,24},{10,26},{12,28},{14,30},{16,0},... | collective-permute-start | bytes 442376 | tf_op jit(solution)/shard_map/ppermute | solution.py:423
  4.1 16.8 %collective-permute-start.2 = (bf16[4,32,576]{2,1,0:T(8,128)(2,1)}, bf16[4,32,576]{2,1,0:T(8,128)(2,1)S(1)}, u32[]{:S(2)}, u32[]{:S(2)}) collective-permute-start(bf16[4,32,576]{2,1,0:T(8,128)(2,1)} %refs_1_.1), channel_id=1, source_target_pairs={{0,8},{2,10},{4,12},{6,14},{8,16},{10,18},{12,20},{14,22},{16,24},... | collective-permute-start | bytes 442376 | tf_op jit(solution)/shard_map/ppermute | solution.py:423
  7.2 21.4 %all-to-all-start = ((bf16[16,16,512]{2,1,0:T(8,128)(2,1)}), bf16[16,16,512]{2,1,0:T(8,128)(2,1)}, u32[]{:S(2)}, u32[]{:S(2)}) async-start(bf16[16,16,512]{2,1,0:T(8,128)(2,1)} %bitcast.4), calls=%async_computation | async-start | bytes 524288 | tf_op jit(solution)/shard_map/all_to_all | solution.py:420
  16.8 6.2 %copy-start.1 = (bf16[64,640]{1,0:T(8,128)(2,1)}, bf16[64,640]{1,0:T(8,128)(2,1)S(1)}, u32[]{:S(2)}) copy-start(bf16[64,640]{1,0:T(8,128)(2,1)S(1)} %get-tuple-element.14.refs_0_.n_ref) | copy-start | bytes 245764
  23.0 15.2 %collective-permute-start.4 = (bf16[256,640]{1,0:T(8,128)(2,1)}, bf16[256,640]{1,0:T(8,128)(2,1)}, u32[]{:S(2)}, u32[]{:S(2)}) collective-permute-start(bf16[256,640]{1,0:T(8,128)(2,1)} %get-tuple-element.16.refs_1_), channel_id=1, source_target_pairs={{0,6},{2,0},{4,2},{6,4},{8,14},{10,8},{12,10},{14,12},{16,22},{18,... | collective-permute-start | bytes 983048 | tf_op jit(solution)/shard_map/ppermute | solution.py:472
  25.1 13.1 %collective-permute-start.5 = (bf16[256,640]{1,0:T(8,128)(2,1)}, bf16[256,640]{1,0:T(8,128)(2,1)}, u32[]{:S(2)}, u32[]{:S(2)}) collective-permute-start(bf16[256,640]{1,0:T(8,128)(2,1)} %get-tuple-element.17.refs_2_), channel_id=1, source_target_pairs={{0,4},{2,6},{4,0},{6,2},{8,12},{10,14},{12,8},{14,10},{16,20},{18,... | collective-permute-start | bytes 983048 | tf_op jit(solution)/shard_map/ppermute | solution.py:472
  25.5 13.1 %collective-permute-start.6 = (bf16[256,640]{1,0:T(8,128)(2,1)}, bf16[256,640]{1,0:T(8,128)(2,1)}, u32[]{:S(2)}, u32[]{:S(2)}) collective-permute-start(bf16[256,640]{1,0:T(8,128)(2,1)} %get-tuple-element.18.refs_3_), channel_id=1, source_target_pairs={{0,2},{2,4},{4,6},{6,0},{8,10},{10,12},{12,14},{14,8},{16,18},{18,... | collective-permute-start | bytes 983048 | tf_op jit(solution)/shard_map/ppermute | solution.py:472
  25.8 18.4 %collective-permute-start.3 = (bf16[256,640]{1,0:T(8,128)(2,1)}, bf16[256,640]{1,0:T(8,128)(2,1)}, u32[]{:S(2)}, u32[]{:S(2)}) collective-permute-start(bf16[256,640]{1,0:T(8,128)(2,1)} %get-tuple-element.15.refs_0_), channel_id=1, source_target_pairs={{0,1},{1,0},{2,3},{3,2},{4,5},{5,4},{6,7},{7,6},{8,9},{9,8},{10,11... | collective-permute-start | bytes 983048 | tf_op jit(solution)/shard_map/ppermute | solution.py:479
  32.8 20.4 %all-to-all-start.1 = ((bf16[16,16,512]{2,1,0:T(8,128)(2,1)}), bf16[16,16,512]{2,1,0:T(8,128)(2,1)}, u32[]{:S(2)}, u32[]{:S(2)}) async-start(bf16[16,16,512]{2,1,0:T(8,128)(2,1)} %bitcast.6), calls=%async_computation.1 | async-start | bytes 524288 | tf_op jit(solution)/shard_map/all_to_all | solution.py:471
  38.6 7.5 %copy-start.2 = (bf16[64,640]{1,0:T(8,128)(2,1)S(1)}, bf16[64,640]{1,0:T(8,128)(2,1)}, u32[]{:S(2)}) copy-start(bf16[64,640]{1,0:T(8,128)(2,1)} %copy-done.1) | copy-start | bytes 245764
  38.6 6.6 %collective-permute-start.7 = (bf16[256,640]{1,0:T(8,128)(2,1)}, bf16[256,640]{1,0:T(8,128)(2,1)S(1)}, u32[]{:S(2)}, u32[]{:S(2)}) collective-permute-start(bf16[256,640]{1,0:T(8,128)(2,1)} %get-tuple-element.20.refs_2_), channel_id=1, source_target_pairs={{0,1},{1,0},{2,3},{3,2},{4,5},{5,4},{6,7},{7,6},{8,9},{9,8},{10,11... | collective-permute-start | bytes 983048 | tf_op jit(solution)/shard_map/ppermute | solution.py:479
  43.7 1.9 %collective-permute-start.8 = (bf16[256,640]{1,0:T(8,128)(2,1)}, bf16[256,640]{1,0:T(8,128)(2,1)S(1)}, u32[]{:S(2)}, u32[]{:S(2)}) collective-permute-start(bf16[256,640]{1,0:T(8,128)(2,1)} %get-tuple-element.21.refs_4_), channel_id=1, source_target_pairs={{0,1},{1,0},{2,3},{3,2},{4,5},{5,4},{6,7},{7,6},{8,9},{9,8},{10,11... | collective-permute-start | bytes 983048 | tf_op jit(solution)/shard_map/ppermute | solution.py:479
  43.7 2.3 %collective-permute-start.9 = (bf16[256,640]{1,0:T(8,128)(2,1)}, bf16[256,640]{1,0:T(8,128)(2,1)S(1)}, u32[]{:S(2)}, u32[]{:S(2)}) collective-permute-start(bf16[256,640]{1,0:T(8,128)(2,1)} %get-tuple-element.22.refs_6_), channel_id=1, source_target_pairs={{0,1},{1,0},{2,3},{3,2},{4,5},{5,4},{6,7},{7,6},{8,9},{9,8},{10,11... | collective-permute-start | bytes 983048 | tf_op jit(solution)/shard_map/ppermute | solution.py:479
  53.2 1.0 %copy-start = (bf16[64,2048]{1,0:T(8,128)(2,1)S(1)}, bf16[64,2048]{1,0:T(8,128)(2,1)}, u32[]{:S(2)}) copy-start(bf16[64,2048]{1,0:T(8,128)(2,1)} %latent_kernel.1._) | copy-start | bytes 786436

commit v3 on v2

v3 whole, which is shorter than its diff:
```python
import functools

import jax
import jax.numpy as jnp
from jax import lax
from jax.experimental import pallas as pl
from jax.experimental.pallas import tpu as pltpu
from jax.sharding import PartitionSpec as P

F32 = jnp.float32
BF16 = jnp.bfloat16
NEG = -1e30


def split(x, n):
    if n & (n - 1) == 0:
        return lax.shift_right_logical(x, jnp.full_like(x, n.bit_length() - 1)), x & (n - 1)
    return lax.div(x, jnp.full_like(x, n)), lax.rem(x, jnp.full_like(x, n))


def wrap(x, n):
    return jnp.where(x < 0, x + n, x)


def lanes(shape, dim):
    return lax.broadcasted_iota(jnp.int32, shape, dim)


def prompt_at(counts_ref, owner, j):
    bound = jnp.int32(0)
    k = jnp.zeros_like(j)
    for i in range(counts_ref.shape[0]):
        bound = bound + counts_ref[i, owner]
        k = k + (bound <= j).astype(jnp.int32)
    return k


def fan_rows(geo, shape, dim, me):
    group, slots, steps, parts, per = (geo[n] for n in ("group", "slots", "steps", "parts", "per"))
    other, rest = split(lanes(shape, dim), parts * slots * steps)
    part, rest = split(rest, slots * steps)
    slot, step = split(rest, steps)
    j = wrap(other - me, group) + group * slot
    return part, jnp.where(j < per, step * per + j, -1)


def one_hot(hit):
    return hit.astype(F32).astype(BF16)


def dot(a, b):
    return lax.dot_general(a, b, (((1,), (0,)), ((), ())), preferred_element_type=F32)


def dot_first(a, b):
    return lax.dot_general(a, b, (((0,), (0,)), ((), ())), preferred_element_type=F32)


def dot_t(a, b):
    return lax.dot_general(a, b, (((1,), (1,)), ((), ())), preferred_element_type=F32)


def row_sums(x, ones):
    return dot(x.astype(BF16), ones)


def slot_sample(geo, hop, pair, carry):
    return wrap(hop - carry, geo["depth"]) + geo["depth"] * pair


def fill_table(geo, counts_ref, table_ref):
    width, depth, prompts, pairs = (geo[n] for n in ("width", "depth", "prompts", "pairs"))
    a, b = split(lax.axis_index("roll"), width)
    at = 0
    for s in range(width):
        for hop in geo["order"]:
            if hop == 0:
                column = wrap(b + s - width, width)
                carry = (b + s >= width).astype(jnp.int32)
                owner, piece = a * width + column, s
            else:
                carry = (b < s).astype(jnp.int32)
                owner = wrap(a + hop - depth, depth) * width + b
                piece = hop - 1
            for pair in range(pairs):
                j = s + width * slot_sample(geo, hop, pair, carry)
                k = jnp.minimum(prompt_at(counts_ref, owner, j), prompts - 1)
                table_ref[at] = piece * prompts + k
                at += 1


def reads_kernel(geo, q_hbm, k_hbm, g_hbm, v_hbm, b_hbm, c_hbm, r_ref, a_ref, table_ref, *scratch):
    q_ref, k_ref, g_ref, v_ref, b_ref, raw, counts_ref, sems = scratch
    _, per, width = q_ref.shape
    heads = geo["heads"]
    dk = width // heads
    parts = geo["parts"]
    wide = width // parts
    unit = 2 * dk
    chunk = width // 2
    beta_copy = pltpu.make_async_copy(b_hbm, b_ref, sems.at[2, 0])
    beta_copy.start()
    counts_copy = pltpu.make_async_copy(c_hbm, counts_ref, sems.at[2, 1])
    counts_copy.start()
    copies = []
    for c in range(2):
        sl = pl.ds(c * chunk, chunk)
        pairs = ((q_hbm, q_ref), (k_hbm, k_ref), (g_hbm, g_ref), (v_hbm, v_ref))
        for n, (src, dst) in enumerate(pairs):
            copies.append(pltpu.make_async_copy(src.at[:, :, sl], dst.at[:, :, sl], sems.at[c, n]))
            copies[-1].start()
    me = lax.axis_index("roll")
    ones = one_hot(split(lanes((unit, unit), 0), dk)[0] == split(lanes((unit, unit), 1), dk)[0])
    rows, rows_in = r_ref.shape[0], raw.shape[0]
    part, place = fan_rows(geo, (rows, rows_in), 0, me)
    pick = one_hot((lanes((rows, rows_in), 1) == part * (2 * per) + place) & (place >= 0))
    spread = one_hot(lanes((heads, width), 0) == split(lanes((heads, width), 1), dk)[0])
    betas = []
    beta_copy.wait()
    for t in range(2):
        beta = b_ref[t]
        high = beta.astype(BF16)
        low = (beta - high.astype(F32)).astype(BF16)
        betas.append(dot_first(high, spread) + dot_first(low, spread))
    for c in range(parts):
        for at in range(c * wide, (c + 1) * wide, unit):
            if at % chunk == 0:
                for copy in copies[4 * (at // chunk) : 4 * (at // chunk) + 4]:
                    copy.wait()
            sl = slice(at, at + unit)
            q1, q2 = q_ref[0, :, sl].astype(F32), q_ref[1, :, sl].astype(F32)
            k1, k2 = k_ref[0, :, sl].astype(F32), k_ref[1, :, sl].astype(F32)
            d1, d2 = jnp.exp(-g_ref[0, :, sl]), jnp.exp(-g_ref[1, :, sl])
            dq2, dk2 = d2 * q2, d2 * k2
            terms = (q1 * q1, k1 * k1, q2 * q2, k2 * k2, k1 * q1, k2 * q2, k1 * dq2, k1 * dk2)
            sums = row_sums(jnp.concatenate(terms, axis=0), ones)
            s = [sums[n * per : (n + 1) * per] for n in range(8)]
            rq1, rk1, rq2, rk2 = (lax.rsqrt(x + 1e-06) for x in s[:4])
            b1, b2 = betas[0][:, sl], betas[1][:, sl]
            a11 = b1 * (s[4] * rk1 * rq1)
            a22 = b2 * (s[5] * rk2 * rq2)
            a22k = a22 * rk2
            a21 = b1 * (rk1 * (rq2 * s[6] - a22k * s[7]))
            r1 = d1 * (rq1 * q1 - (a11 * rk1) * k1)
            r2 = d1 * (rq2 * dq2 - a22k * dk2 - (a21 * rk1) * k1)
            to = slice(at - c * wide, at - c * wide + unit)
            raw[2 * c * per : (2 * c + 1) * per, to] = r1.astype(BF16)
            raw[(2 * c + 1) * per : (2 * c + 2) * per, to] = r2.astype(BF16)
            v1, v2 = v_ref[0, :, sl].astype(F32), v_ref[1, :, sl].astype(F32)
            a_ref[0, :, sl] = a11 * v1
            a_ref[1, :, sl] = a21 * v1 + a22 * v2
    r_ref[...] = dot(pick, raw[...]).astype(BF16)
    counts_copy.wait()
    fill_table(geo, counts_ref, table_ref)


def state_kernel(geo, s_hbm, c_hbm, *refs):
    r_hbm, y_ref, r_ref, s_ref, r_all, y_all, counts_ref, sems = refs[-8:]
    rows, wide = r_ref.shape
    prompts, heads, dk, dv = s_ref.shape
    me = lax.axis_index("roll")
    group, slots, steps, parts = geo["group"], geo["slots"], geo["steps"], geo["parts"]
    first = pltpu.make_async_copy(r_hbm, r_ref, sems.at[parts + 1])
    first.start()
    copies = [pltpu.make_async_copy(c_hbm, counts_ref, sems.at[parts])]
    for c in range(parts):
        sl = pl.ds(c * (heads // parts), heads // parts)
        copies.append(pltpu.make_async_copy(s_hbm.at[:, sl], s_ref.at[:, sl], sems.at[c]))
    for copy in copies:
        copy.start()
    few, own = rows // parts, slots * steps
    part, rest = split(lanes((rows, rows), 0), few)
    other, rest = split(rest, own)
    sort = one_hot(lanes((rows, rows), 1) == (other * parts + part) * own + rest)
    part, rest = split(lanes((rows, rows), 1), few)
    other, rest = split(rest, own)
    back = one_hot(lanes((rows, rows), 0) == (other * parts + part) * own + rest)
    first.wait()
    r_all[...] = dot(sort, r_ref[...]).astype(BF16)
    copies[0].wait()
    other, rest = split(lanes((few, dk), 0), own)
    j = wrap(me - other, group) + group * split(rest, steps)[0]
    k = prompt_at(counts_ref, me, j)
    keep = [one_hot(k == p) for p in range(prompts)]
    for c in range(parts):
        copies[1 + c].wait()
        for at in range(wide // dk):
            h = c * (wide // dk) + at
            r = r_all[c * few : (c + 1) * few, at * dk : (at + 1) * dk]
            acc = dot(r * keep[0], s_ref[0, h])
            for p in range(1, prompts):
                acc = acc + dot(r * keep[p], s_ref[p, h])
            y_all[c * few : (c + 1) * few, at * dv : (at + 1) * dv] = acc.astype(BF16)
    y_ref[...] = dot(back, y_all[...]).astype(BF16)


def kda_out_kernel(geo, y_hbm, _, a_ref, o_hbm, y_ref, o_ref, sems):
    per, parts = geo["per"], geo["parts"]
    rows, wide = y_ref.shape
    copy = pltpu.make_async_copy(y_hbm, y_ref, sems.at[0])
    copy.start()
    me = lax.axis_index("roll")
    shape = (2 * per * parts, rows)
    part, place = fan_rows(geo, shape, 1, me)
    pick = one_hot((lanes(shape, 0) == part * (2 * per) + place) & (place >= 0))
    copy.wait()
    send = []
    for c in range(parts):
        sl = pl.ds(c * wide, wide)
        y = dot(pick[2 * c * per : 2 * (c + 1) * per], y_ref[...])
        for t in range(2):
            o_ref[t, :, sl] = (y[t * per : (t + 1) * per] + a_ref[t, :, sl]).astype(BF16)
        send.append(pltpu.make_async_copy(o_ref.at[:, :, sl], o_hbm.at[:, :, sl], sems.at[1 + c]))
        send[c].start()
    for copy in send:
        copy.wait()


def select_kernel(geo, table_ref, *refs):
    width, order, prompts, pairs, entry = (
        geo[n] for n in ("width", "order", "prompts", "pairs", "entry")
    )
    o_refs, plane_pool, column_pool = refs[-2 - width : -2], *refs[-2:]
    column, plane = refs[: -2 - 2 * width], refs[-2 - 2 * width : -2 - width]
    for pool, pieces in ((plane_pool, plane), (column_pool, column)):
        pool[:, :, entry:] = jnp.zeros(pool.shape[:2] + (pool.shape[2] - entry,), BF16)
        for n, piece in enumerate(pieces):
            pool[n * prompts : (n + 1) * prompts, :, :entry] = piece[...]
    local = plane_pool.shape[1]
    sent = len(column) * pairs * local
    at = 0
    for s in range(width):
        to = 0
        for hop in order:
            for pair in range(pairs):
                if hop == 0:
                    o_ref, rows, pool = o_refs[0], sent + (s * pairs + pair) * local, plane_pool
                else:
                    o_ref, rows, pool = o_refs[s], to * local, column_pool
                    to += 1
                o_ref[rows : rows + local, :] = pool[table_ref[at]]
                at += 1


def query_kernel(geo, q_hbm, f_hbm, c_hbm, l_hbm, _, o_ref, n_ref, length_ref, *scratch):
    q_ref, f_ref, counts_ref, len_ref, sems = scratch
    total, wide = q_ref.shape
    width, per, steps, entry = geo["width"], geo["per"], geo["steps"], geo["entry"]
    group, prompts, per_mate = (geo[n] for n in ("group", "prompts", "per_mate"))
    padded = o_ref.shape[1]
    heads = wide // entry
    unit = 2 * entry
    n = total // width
    small = [
        pltpu.make_async_copy(src, dst, sems.at[heads // 2 + x])
        for x, (src, dst) in enumerate(((f_hbm, f_ref), (c_hbm, counts_ref), (l_hbm, len_ref)))
    ]
    copies = []
    for c in range(heads // 2):
        sl = pl.ds(c * unit, unit)
        copies.append(pltpu.make_async_copy(q_hbm.at[:, sl], q_ref.at[:, sl], sems.at[c]))
    for copy in small + copies:
        copy.start()
    row, col = lanes((total, total), 0), lanes((total, total), 1)
    shift, rest = split(row, n)
    i, step = split(rest, steps)
    pick = one_hot(col == step * per + shift + width * i)
    block = n_ref.shape[0] // width
    n_ref[...] = jnp.zeros(n_ref.shape, BF16)
    me = lax.axis_index("roll")
    sample = split(lanes((n, length_ref.shape[1]), 0), steps)[0]
    for copy in small:
        copy.wait()
    for s in range(width):
        length = jnp.zeros(sample.shape, jnp.int32)
        for i in range(per_mate):
            j = jnp.int32(s + width * i)
            owner = split(me + j, group)[1]
            k = prompt_at(counts_ref, owner, j)
            length = jnp.where(sample == i, len_ref[owner * prompts + k], length)
        length_ref[s * n : (s + 1) * n, :] = length
    out = dot(pick, f_ref[...]).astype(BF16)
    for s in range(width):
        n_ref[s * block : s * block + n, :entry] = out[s * n : (s + 1) * n]
    for c, copy in enumerate(copies):
        copy.wait()
        out = dot(pick, q_ref[:, c * unit : (c + 1) * unit])
        even = out[:, :padded].astype(BF16)
        odd = pltpu.roll(out[:, unit - padded :], entry, 1).astype(BF16)
        for s in range(width):
            at = (s * heads + 2 * c) * n
            o_ref[at : at + n, :] = even[s * n : (s + 1) * n]
            o_ref[at + n : at + 2 * n, :] = odd[s * n : (s + 1) * n]


def latent_kernel(geo, w_hbm, *refs):
    width, steps, per, per_mate = (geo[n] for n in ("width", "steps", "per", "per_mate"))
    halves, local, pairs, order = (geo[n] for n in ("halves", "local", "pairs", "order"))
    arrays = halves * width
    k_hbm, refs = refs[:arrays], refs[arrays:]
    _, q_ref, n_ref, length_ref, o_hbm, keys, ctx, out, w_ref, o_ref, sems = refs
    heads, rank, dv = w_ref.shape
    half = lax.axis_index("exp")
    few = pairs * local
    sent = (len(order) - 1) * few
    piece = sent + few
    old = halves * piece
    n = per_mate * steps
    block = n_ref.shape[0] // width
    copies = []
    for s in range(width):
        for e in range(halves):
            first = k_hbm[e].at[pl.ds(sent + s * few, few)], keys.at[s, pl.ds(e * piece + sent, few)]
            rest = k_hbm[s * halves + e].at[pl.ds(0, sent)], keys.at[s, pl.ds(e * piece, sent)]
            for src, dst in (rest, first):
                copies.append(pltpu.make_async_copy(src, dst, sems.at[len(copies)]))
    each = len(copies) // width
    copies.append(pltpu.make_async_copy(w_hbm, w_ref, sems.at[len(copies)]))
    for copy in copies:
        copy.start()
    _, b = split(lax.axis_index("roll"), width)
    row, col = lanes((n, old), 0), lanes((n, old), 1)
    e, rest = split(col, piece)
    rest, pos = split(rest, local)
    place, pair = split(rest, pairs)
    hop = jnp.zeros_like(place)
    for x, h in enumerate(order):
        hop = jnp.where(place == x, h, hop)
    e = e + half
    pos = jnp.where(e >= halves, e - halves, e) * local + pos
    of_carry = []
    for carry in range(2):
        other = slot_sample(geo, hop, pair, carry)
        mine = (other == split(row, steps)[0]) & (other < per_mate)
        of_carry.append(jnp.where(mine, pos, halves * local))
    row, col = lanes((n, block), 0), lanes((n, block), 1)
    behind = row - col
    allowed_new = ((behind >= 0) & (behind <= split(row, steps)[1]))[None]
    scores = []
    for s in range(width):
        query = q_ref[s * heads * n : (s + 1) * heads * n, :]
        keys[s, old:, :] = n_ref[s * block : (s + 1) * block, :]
        for copy in copies[s * each : (s + 1) * each]:
            copy.wait()
        scores.append(dot_t(query, keys[s]).reshape(heads, n, old + block) * geo["scale"])
    weights = []
    for s in range(width):
        length = length_ref[s * n : (s + 1) * n, :]
        length = jnp.concatenate([length] * -(-old // length.shape[1]), axis=1)[:, :old]
        pos = jnp.where(b + s >= width, of_carry[1], of_carry[0])
        allowed_old = (pos < length)[None]
        part = jnp.concatenate(
            [
                jnp.where(allowed_old, scores[s][:, :, :old], NEG),
                jnp.where(allowed_new, scores[s][:, :, old:], NEG),
            ],
            axis=-1,
        )
        top = jnp.max(part, axis=-1, keepdims=True)
        raised = jnp.exp(part - top)
        part = raised / jnp.sum(raised, axis=-1, keepdims=True)
        weights.append(part.reshape(heads * n, old + block).astype(BF16))
    for s in range(width):
        context = dot(weights[s], keys[s, :, :rank]).astype(BF16)
        for h in range(heads):
            ctx[h, s * n : (s + 1) * n, :] = context[h * n : (h + 1) * n]
    copies[-1].wait()
    for h in range(heads):
        out[:, h * dv : (h + 1) * dv] = dot(ctx[h], w_ref[h]).astype(BF16)
    rows = steps * per
    shift, rest = split(lanes((rows, rows), 1), n)
    sample, step = split(rest, steps)
    place = step * per + shift + width * sample
    pick = one_hot(lanes((rows, rows), 0) == place)
    send = []
    for c in range(2):
        sl = pl.ds(c * (heads * dv // 2), heads * dv // 2)
        o_ref[:, sl] = dot(pick, out[:, sl]).astype(BF16)
        send.append(pltpu.make_async_copy(o_ref.at[:, sl], o_hbm.at[:, sl], sems.at[c]))
        send[c].start()
    for copy in send:
        copy.wait()


def cost(us):
    return pl.CostEstimate(
        flops=2_000_000_000 * us, bytes_accessed=3_000_000 * us, transcendentals=20_000_000 * us
    )


def call(kernel, geo, out, args, smem=0, hbm=0, after=0, scratch=(), mib=16, us=0):
    spaces = [pltpu.SMEM] * smem + [pltpu.HBM] * hbm + [pl.ANY] * after
    spaces += [pltpu.VMEM] * (len(args) - len(spaces))

    def place(x):
        if isinstance(x, jax.ShapeDtypeStruct):
            return pl.BlockSpec(memory_space=pltpu.SMEM if len(x.shape) == 1 else pltpu.VMEM)
        return pl.BlockSpec(memory_space=pltpu.HBM)

    outs = jax.tree.map(place, out)
    args = [
        pltpu.with_memory_space_constraint(x, pltpu.HBM) if s == pltpu.HBM else x
        for x, s in zip(args, spaces, strict=True)
    ]
    return pl.pallas_call(
        functools.partial(kernel, geo),
        out_shape=out,
        in_specs=[pl.BlockSpec(memory_space=s) for s in spaces],
        out_specs=outs,
        scratch_shapes=list(scratch),
        cost_estimate=cost(us),
        compiler_params=pltpu.CompilerParams(vmem_limit_bytes=mib * 1024 * 1024),
        name=kernel.__name__,
    )(*args)


def hold(x, first):
    return pl.pallas_call(
        lambda *refs: None,
        out_shape=tuple(jax.ShapeDtypeStruct(a.shape, a.dtype) for a in x),
        in_specs=[pl.BlockSpec(memory_space=pl.ANY)] * (len(x) + 1),
        out_specs=[pl.BlockSpec(memory_space=pl.ANY)] * len(x),
        input_output_aliases={n + 1: n for n in range(len(x))},
        cost_estimate=cost(20),
        name="hold",
    )(first, *x)


def pad_to(n, m):
    return -(-n // m) * m


def on_device(
    kda_prefill,
    latent_prefill,
    prompt_len,
    sample_counts,
    kda_q,
    kda_k,
    kda_v,
    kda_decay,
    kda_beta,
    mla_q,
    mla_new,
    w_uv,
):
    group = lax.axis_size("roll")
    halves = lax.axis_size("exp")
    steps, per, kda_width = kda_q.shape
    heads = kda_beta.shape[2]
    prompts, local, entry = latent_prefill.shape
    cache = local * halves
    _, rank, dv = w_uv.shape
    width = 4
    depth = group // width
    slots = -(-per // group)
    per_mate = per // width
    hops = min(depth, per_mate + 1)
    padded = pad_to(entry, 128)
    parts = max(1, min(16 // (slots * steps), heads // 2))
    geo = dict(
        group=group,
        halves=halves,
        steps=steps,
        per=per,
        width=width,
        depth=depth,
        slots=slots,
        hops=hops,
        prompts=prompts,
        cache=cache,
        entry=entry,
        per_mate=per_mate,
        local=local,
        pairs=max(-(-per_mate // depth), -(-16 // local)),
        order=[*range(1, hops), 0],
        scale=192.0**-0.5,
        heads=heads,
        parts=parts,
    )
    shape = jax.ShapeDtypeStruct

    def mates(sign, s):
        return [(i, i // width * width + (i + sign * s) % width) for i in range(group)]

    counts = sample_counts.T
    fan = (group * parts * slots * steps, kda_width // parts)
    reads, coef, table = call(
        reads_kernel,
        geo,
        (
            shape(fan, BF16),
            shape((steps, per, kda_width), F32),
            shape((width * hops * geo["pairs"],), jnp.int32),
        ),
        (kda_q, kda_k, kda_decay, kda_v, jnp.swapaxes(kda_beta, 1, 2), counts),
        hbm=6,
        scratch=[
            pltpu.VMEM(kda_q.shape, BF16),
            pltpu.VMEM(kda_q.shape, BF16),
            pltpu.VMEM(kda_q.shape, F32),
            pltpu.VMEM(kda_q.shape, BF16),
            pltpu.VMEM((steps, heads, per), F32),
            pltpu.VMEM((steps * per * parts, kda_width // parts), BF16),
            pltpu.SMEM(counts.shape, jnp.int32),
            pltpu.SemaphoreType.DMA((3, 4)),
        ],
    )
    got = lax.all_to_all(reads, "roll", 0, 0, tiled=True)

    plane = [latent_prefill] + [
        lax.ppermute(latent_prefill, "roll", mates(-1, s)) for s in range(1, width)
    ]
    column = [
        lax.ppermute(latent_prefill, "roll", [(i, (i - width * h) % group) for i in range(group)])
        for h in range(1, hops)
    ]
    few = geo["pairs"] * local
    sent = (hops - 1) * few
    wide = mla_q.shape[2]
    rows = steps * per
    few = geo["pairs"] * local
    sent = (hops - 1) * few
    wide = mla_q.shape[2]
    rows = steps * per
    queries, fresh, lengths = call(
        query_kernel,
        geo,
        (
            shape((heads * rows, padded), BF16),
            shape((width * pad_to(per_mate * steps, 128), padded), BF16),
            shape((rows, 128), jnp.int32),
        ),
        (mla_q.reshape(rows, wide), mla_new.reshape(rows, entry), counts, prompt_len, reads),
        hbm=4,
        after=1,
        scratch=[
            pltpu.VMEM((rows, wide), BF16),
            pltpu.VMEM((rows, entry), BF16),
            pltpu.SMEM(counts.shape, jnp.int32),
            pltpu.SMEM(prompt_len.shape, jnp.int32),
            pltpu.SemaphoreType.DMA((heads // 2 + 3,)),
        ],
    )
    chosen = call(
        select_kernel,
        geo,
        tuple(shape((sent + (s == 0) * width * few, padded), BF16) for s in range(width)),
        (table, *column, *plane),
        smem=1,
        us=20,
        scratch=[
            pltpu.VMEM((width * prompts, local, padded), BF16),
            pltpu.VMEM(((hops - 1) * prompts, local, padded), BF16),
        ],
    )
    products = call(
        state_kernel,
        geo,
        shape(fan, BF16),
        (kda_prefill, counts, *chosen, got),
        hbm=2,
        after=len(chosen) + 1,
        us=20,
        scratch=[
            pltpu.VMEM(fan, BF16),
            pltpu.VMEM(kda_prefill.shape, BF16),
            pltpu.VMEM(fan, BF16),
            pltpu.VMEM(fan, BF16),
            pltpu.SMEM(counts.shape, jnp.int32),
            pltpu.SemaphoreType.DMA((parts + 2,)),
        ],
    )
    back = lax.all_to_all(products, "roll", 0, 0, tiled=True)
    taken = [lax.ppermute(chosen[s], "roll", mates(-1, s)) for s in range(1, width)]
    taken = [chosen[0], *hold(taken, products)]
    caches = []
    for piece in taken:
        caches.append(piece)
        for e in range(1, halves):
            caches.append(
                lax.ppermute(piece, "exp", [(i, (i - e) % halves) for i in range(halves)])
            )
    mla_out = call(
        latent_kernel,
        geo,
        pltpu.HBM((rows, heads * dv), BF16),
        (w_uv, *caches, products, queries, fresh, lengths),
        hbm=1,
        after=1 + len(caches),
        scratch=[
            pltpu.VMEM((width, fresh.shape[0] // width + hops * few * halves, padded), BF16),
            pltpu.VMEM((heads, rows, rank), BF16),
            pltpu.VMEM((rows, heads * dv), BF16),
            pltpu.VMEM(w_uv.shape, BF16),
            pltpu.VMEM((rows, heads * dv), BF16),
            pltpu.SemaphoreType.DMA((width * halves * 2 + 1,)),
        ],
    )
    kda_out = call(
        kda_out_kernel,
        geo,
        pltpu.HBM((steps, per, kda_width), BF16),
        (back, mla_out, coef),
        hbm=2,
        scratch=[
            pltpu.VMEM(fan, BF16),
            pltpu.VMEM((steps, per, kda_width), BF16),
            pltpu.SemaphoreType.DMA((parts + 1,)),
        ],
    )
    return (kda_out, mla_out.reshape(steps, per, heads * dv))


def solution(mesh):
    return jax.shard_map(
        on_device,
        mesh=mesh,
        in_specs=(
            P("roll", "exp", None, None),
            P("roll", "exp", None),
            P(),
            P(),
            P(None, "roll", "exp"),
            P(None, "roll", "exp"),
            P(None, "roll", "exp"),
            P(None, "roll", "exp"),
            P(None, "roll", "exp"),
            P(None, "roll", "exp"),
            P(None, "roll", None),
            P("exp", None, None),
        ),
        out_specs=(P(None, "roll", "exp"), P(None, "roll", "exp")),
        check_vma=False,
    )
```

time: 57.6 us -> 51.3 us (0.89)
  the two profiles are of different devices: /device:TPU:17 before, /device:TPU:0 now
where the time goes in v3:
time: 51.3 us; the launch traced here: 50.9 us
  starting transfers between devices  26.1 us (51%)
  Pallas kernels  19.3 us (38%)
  waiting for transfers between devices  3.73 us (7%)
  local copies, waits for them, and re-layouts  0.91 us (2%)
  between operations  0.78 us (2%)
    pallas_call x6, Pallas kernels, call(): pl.pallas_call(functools.partial(kernel, geo), out_shape=out, in_specs=[p...  19.3 us
    all_to_all x1, starting transfers between devices, on_device(): got = lax.all_to_all(reads, 'roll', 0, 0, tiled=True)  6.63 us
    ppermute x3, starting transfers between devices, on_device(): lax.ppermute(latent_prefill, 'roll', [(i, (i - width * h) % group) for i...  6.11 us
    all_to_all x1, starting transfers between devices, on_device(): back = lax.all_to_all(products, 'roll', 0, 0, tiled=True)  4.47 us
    ppermute x3, starting transfers between devices, on_device(): lax.ppermute(latent_prefill, 'roll', mates(-1, s))  4.44 us
    ppermute x3, starting transfers between devices, on_device(): lax.ppermute(chosen[s], 'roll', mates(-1, s))  3.9 us
    all_to_all x1, waiting for transfers between devices, on_device(): got = lax.all_to_all(reads, 'roll', 0, 0, tiled=True)  2.04 us
  transfers between devices with their start and end apart: 15, of which 4 were waited for; matrix products, arithmetic and copies ran while one was open for 0% of the time, Pallas kernels for 34%

profile of v3, /device:TPU:0, one launch (start us, length us, event | category | flops | bytes accessed | tf_op | source)
XLA Modules:
  0.0 50.9 jit_solution(3276132654835262048)
XLA Ops:
  0.6 5.1 %collective-permute-start = (bf16[4,32,576]{2,1,0:T(8,128)(2,1)}, bf16[4,32,576]{2,1,0:T(8,128)(2,1)S(1)}, u32[]{:S(2)}, u32[]{:S(2)}) collective-permute-start(bf16[4,32,576]{2,1,0:T(8,128)(2,1)} %refs_3_.1), channel_id=1, source_target_pairs={{0,24},{2,26},{4,28},{6,30},{8,0},{10,2},{12,4},{14,6},{16,8},{18,... | collective-permute-start | bytes 442376 | tf_op jit(solution)/shard_map/ppermute | solution.py:515
  5.7 0.0 collective-permute-start.1
  5.7 1.0 %collective-permute-start.2 = (bf16[4,32,576]{2,1,0:T(8,128)(2,1)}, bf16[4,32,576]{2,1,0:T(8,128)(2,1)S(1)}, u32[]{:S(2)}, u32[]{:S(2)}) collective-permute-start(bf16[4,32,576]{2,1,0:T(8,128)(2,1)} %refs_3_.1), channel_id=1, source_target_pairs={{0,8},{2,10},{4,12},{6,14},{8,16},{10,18},{12,20},{14,22},{16,24},... | collective-permute-start | bytes 442376 | tf_op jit(solution)/shard_map/ppermute | solution.py:515
  6.7 2.4 %collective-permute-start.3 = (bf16[4,32,576]{2,1,0:T(8,128)(2,1)}, bf16[4,32,576]{2,1,0:T(8,128)(2,1)S(1)}, u32[]{:S(2)}, u32[]{:S(2)}) collective-permute-start(bf16[4,32,576]{2,1,0:T(8,128)(2,1)} %refs_3_.1), channel_id=1, source_target_pairs={{0,6},{2,0},{4,2},{6,4},{8,14},{10,8},{12,10},{14,12},{16,22},{18,... | collective-permute-start | bytes 442376 | tf_op jit(solution)/shard_map/ppermute | solution.py:512
  9.2 0.5 collective-permute-start.4
  9.7 1.0 %collective-permute-done.refs_0_ = bf16[4,32,576]{2,1,0:T(8,128)(2,1)S(1)} collective-permute-done((bf16[4,32,576]{2,1,0:T(8,128)(2,1)}, bf16[4,32,576]{2,1,0:T(8,128)(2,1)S(1)}, u32[]{:S(2)}, u32[]{:S(2)}) %collective-permute-start) | collective-permute-done | bytes 147488 | tf_op jit(solution)/shard_map/ppermute | solution.py:515
  10.7 1.5 %collective-permute-start.5 = (bf16[4,32,576]{2,1,0:T(8,128)(2,1)}, bf16[4,32,576]{2,1,0:T(8,128)(2,1)S(1)}, u32[]{:S(2)}, u32[]{:S(2)}) collective-permute-start(bf16[4,32,576]{2,1,0:T(8,128)(2,1)} %refs_3_.1), channel_id=1, source_target_pairs={{0,2},{2,4},{4,6},{6,0},{8,10},{10,12},{12,14},{14,8},{16,18},{18,... | collective-permute-start | bytes 442376 | tf_op jit(solution)/shard_map/ppermute | solution.py:512
  12.2 3.1 %reads_kernel.1 = (bf16[256,512]{1,0:T(8,128)(2,1)}, f32[2,32,2048]{2,1,0:T(8,128)S(1)}, s32[32]{0:T(128)S(1)}) custom-call(bf16[2,32,2048]{2,1,0:T(8,128)(2,1)} %q_hbm.1, bf16[2,32,2048]{2,1,0:T(8,128)(2,1)} %k_hbm.1, f32[2,32,2048]{2,1,0:T(8,128)} %g_hbm.1, bf16[2,32,2048]{2,1,0:T(8,128)(2,1)} %v_hbm.1, f32[2,16,32]{2,1,0:T(8,128)} %bitcast.12, ...), custom_call_target="tpu_custom_call" | custom-call | tf_op jit(solution)/shard_map/reads_kernel/pallas_call | solution.py:405
  15.3 6.6 %all-to-all-start = ((bf16[16,16,512]{2,1,0:T(8,128)(2,1)}), bf16[16,16,512]{2,1,0:T(8,128)(2,1)}, u32[]{:S(2)}, u32[]{:S(2)}) async-start(bf16[16,16,512]{2,1,0:T(8,128)(2,1)} %bitcast.2), calls=%async_computation | async-start | bytes 524288 | tf_op jit(solution)/shard_map/all_to_all | solution.py:509
  21.9 0.0 collective-permute-done.1.refs_1_
  21.9 0.0 collective-permute-done.2.refs_2_
  22.0 0.0 collective-permute-done.3.refs_4_
  22.0 0.0 collective-permute-done.4.refs_5_
  22.0 0.0 collective-permute-done.5.refs_6_
  22.0 0.0 copy-start
  22.0 0.9 %copy-done = bf16[4,32,576]{2,1,0:T(8,128)(2,1)S(1)} copy-done((bf16[4,32,576]{2,1,0:T(8,128)(2,1)S(1)}, bf16[4,32,576]{2,1,0:T(8,128)(2,1)}, u32[]{:S(2)}) %copy-start) | copy-done | bytes 147480
  22.9 1.7 %select_kernel.1 = (bf16[448,640]{1,0:T(8,128)(2,1)}, bf16[192,640]{1,0:T(8,128)(2,1)}, bf16[192,640]{1,0:T(8,128)(2,1)}, bf16[192,640]{1,0:T(8,128)(2,1)}) custom-call(s32[32]{0:T(128)S(1)} %get-tuple-element.15.table_ref, bf16[4,32,576]{2,1,0:T(8,128)(2,1)S(1)} %collective-permute-done.refs_0_, bf16[4,32,576]{2,1,0:T(8,128)(2,1)S(1)} %collective-permute-done.1.refs_1_, ...), custom_call_target="tpu_custom_call" | custom-call | flops 40000000000 | bytes 60000000 | tf_op jit(solution)/shard_map/select_kernel/pallas_call | solution.py:405
  24.7 2.8 %collective-permute-start.7 = (bf16[192,640]{1,0:T(8,128)(2,1)}, bf16[192,640]{1,0:T(8,128)(2,1)}, u32[]{:S(2)}, u32[]{:S(2)}) collective-permute-start(bf16[192,640]{1,0:T(8,128)(2,1)} %get-tuple-element.17.refs_1_), channel_id=1, source_target_pairs={{0,6},{2,0},{4,2},{6,4},{8,14},{10,8},{12,10},{14,12},{16,22},{18,... | collective-permute-start | bytes 737288 | tf_op jit(solution)/shard_map/ppermute | solution.py:575
  27.4 0.6 %collective-permute-start.8 = (bf16[192,640]{1,0:T(8,128)(2,1)}, bf16[192,640]{1,0:T(8,128)(2,1)}, u32[]{:S(2)}, u32[]{:S(2)}) collective-permute-start(bf16[192,640]{1,0:T(8,128)(2,1)} %get-tuple-element.18.refs_2_), channel_id=1, source_target_pairs={{0,4},{2,6},{4,0},{6,2},{8,12},{10,14},{12,8},{14,10},{16,20},{18,... | collective-permute-start | bytes 737288 | tf_op jit(solution)/shard_map/ppermute | solution.py:575
  28.0 0.6 %collective-permute-start.9 = (bf16[192,640]{1,0:T(8,128)(2,1)}, bf16[192,640]{1,0:T(8,128)(2,1)}, u32[]{:S(2)}, u32[]{:S(2)}) collective-permute-start(bf16[192,640]{1,0:T(8,128)(2,1)} %get-tuple-element.19.refs_3_), channel_id=1, source_target_pairs={{0,2},{2,4},{4,6},{6,0},{8,10},{10,12},{12,14},{14,8},{16,18},{18,... | collective-permute-start | bytes 737288 | tf_op jit(solution)/shard_map/ppermute | solution.py:575
  28.6 0.0 collective-permute-start.6
  28.6 2.0 %all-to-all-done = bf16[16,16,512]{2,1,0:T(8,128)(2,1)} async-done(((bf16[16,16,512]{2,1,0:T(8,128)(2,1)}), bf16[16,16,512]{2,1,0:T(8,128)(2,1)}, u32[]{:S(2)}, u32[]{:S(2)}) %all-to-all-start) | async-done | bytes 262176 | tf_op jit(solution)/shard_map/all_to_all | solution.py:509
  30.6 3.3 %state_kernel.1.refs_0_.refs_8_ = bf16[256,512]{1,0:T(8,128)(2,1)} custom-call(bf16[4,16,128,128]{3,2,1,0:T(8,128)(2,1)} %s_hbm.1, s32[4,16]{1,0:T(4,128)} %bitcast.14, bf16[448,640]{1,0:T(8,128)(2,1)} %get-tuple-element.16.refs_0_, bf16[192,640]{1,0:T(8,128)(2,1)} %get-tuple-element.17.refs_1_, bf16[192,640]{1,0:T(8,128)(2,1)} %get-tuple-element.18.refs_2_, ...), custom_call_target="tpu_custom_call" | custom-call | flops 40000000000 | bytes 60000000 | tf_op jit(solution)/shard_map/state_kernel/pallas_call | solution.py:405
  33.9 4.5 %all-to-all-start.1 = ((bf16[16,16,512]{2,1,0:T(8,128)(2,1)}), bf16[16,16,512]{2,1,0:T(8,128)(2,1)}, u32[]{:S(2)}, u32[]{:S(2)}) async-start(bf16[16,16,512]{2,1,0:T(8,128)(2,1)} %bitcast.4), calls=%async_computation.1 | async-start | bytes 524288 | tf_op jit(solution)/shard_map/all_to_all | solution.py:574
  38.4 0.0 collective-permute-done.7.refs_1_
  38.4 0.4 collective-permute-done.8.refs_2_
  38.8 0.0 collective-permute-done.9.refs_3_
  38.8 0.0 collective-permute-start.10
  38.8 0.5 collective-permute-start.11
  39.3 0.1 collective-permute-start.12
  39.4 3.3 %query_kernel.1 = (bf16[1024,640]{1,0:T(8,128)(2,1)S(1)}, bf16[512,640]{1,0:T(8,128)(2,1)S(1)}, s32[64,128]{1,0:T(8,128)S(1)}) custom-call(bf16[64,9216]{1,0:T(8,128)(2,1)} %bitcast.9, bf16[64,576]{1,0:T(8,128)(2,1)} %bitcast.11, s32[4,16]{1,0:T(4,128)} %bitcast.15, s32[64]{0:T(128)} %l_hbm.1, bf16[256,512]{1,0:T(8,128)(2,1)} %get-tuple-element.20._), custom_call_target="tpu_custom_call" | custom-call | tf_op jit(solution)/shard_map/query_kernel/pallas_call | solution.py:405
  42.7 0.0 collective-permute-done.6.refs_1_
  42.7 0.0 collective-permute-done.10.refs_3_
  42.7 0.0 collective-permute-done.11.refs_5_
  42.7 0.0 collective-permute-done.12.refs_7_
  42.7 6.0 %latent_kernel.1._ = bf16[64,2048]{1,0:T(8,128)(2,1)} custom-call(bf16[16,512,128]{2,1,0:T(8,128)(2,1)} %w_hbm.1, bf16[448,640]{1,0:T(8,128)(2,1)} %get-tuple-element.16.refs_0_, bf16[448,640]{1,0:T(8,128)(2,1)} %collective-permute-done.6.refs_1_, bf16[192,640]{1,0:T(8,128)(2,1)} %get-tuple-element.21.refs_2_, ...), custom_call_target="tpu_custom_call" | custom-call | tf_op jit(solution)/shard_map/latent_kernel/pallas_call | solution.py:405
  48.7 0.2 all-to-all-done.1
  49.0 1.9 %kda_out_kernel.1 = bf16[2,32,2048]{2,1,0:T(8,128)(2,1)} custom-call(bf16[256,512]{1,0:T(8,128)(2,1)} %bitcast.5.y_hbm, bf16[64,2048]{1,0:T(8,128)(2,1)} %latent_kernel.1._, f32[2,32,2048]{2,1,0:T(8,128)S(1)} %get-tuple-element.27.a_ref), custom_call_target="tpu_custom_call" | custom-call | tf_op jit(solution)/shard_map/kda_out_kernel/pallas_call | solution.py:405
  (1 shorter events, 0.0 us)
Async XLA Ops:
  0.6 10.1 %collective-permute-start = (bf16[4,32,576]{2,1,0:T(8,128)(2,1)}, bf16[4,32,576]{2,1,0:T(8,128)(2,1)S(1)}, u32[]{:S(2)}, u32[]{:S(2)}) collective-permute-start(bf16[4,32,576]{2,1,0:T(8,128)(2,1)} %refs_3_.1), channel_id=1, source_target_pairs={{0,24},{2,26},{4,28},{6,30},{8,0},{10,2},{12,4},{14,6},{16,8},{18,... | collective-permute-start | bytes 442376 | tf_op jit(solution)/shard_map/ppermute | solution.py:515
  5.7 16.2 %collective-permute-start.1 = (bf16[4,32,576]{2,1,0:T(8,128)(2,1)}, bf16[4,32,576]{2,1,0:T(8,128)(2,1)S(1)}, u32[]{:S(2)}, u32[]{:S(2)}) collective-permute-start(bf16[4,32,576]{2,1,0:T(8,128)(2,1)} %refs_3_.1), channel_id=1, source_target_pairs={{0,16},{2,18},{4,20},{6,22},{8,24},{10,26},{12,28},{14,30},{16,0},... | collective-permute-start | bytes 442376 | tf_op jit(solution)/shard_map/ppermute | solution.py:515
  5.7 16.2 %collective-permute-start.2 = (bf16[4,32,576]{2,1,0:T(8,128)(2,1)}, bf16[4,32,576]{2,1,0:T(8,128)(2,1)S(1)}, u32[]{:S(2)}, u32[]{:S(2)}) collective-permute-start(bf16[4,32,576]{2,1,0:T(8,128)(2,1)} %refs_3_.1), channel_id=1, source_target_pairs={{0,8},{2,10},{4,12},{6,14},{8,16},{10,18},{12,20},{14,22},{16,24},... | collective-permute-start | bytes 442376 | tf_op jit(solution)/shard_map/ppermute | solution.py:515
  6.7 15.2 %collective-permute-start.3 = (bf16[4,32,576]{2,1,0:T(8,128)(2,1)}, bf16[4,32,576]{2,1,0:T(8,128)(2,1)S(1)}, u32[]{:S(2)}, u32[]{:S(2)}) collective-permute-start(bf16[4,32,576]{2,1,0:T(8,128)(2,1)} %refs_3_.1), channel_id=1, source_target_pairs={{0,6},{2,0},{4,2},{6,4},{8,14},{10,8},{12,10},{14,12},{16,22},{18,... | collective-permute-start | bytes 442376 | tf_op jit(solution)/shard_map/ppermute | solution.py:512
  9.2 12.8 %collective-permute-start.4 = (bf16[4,32,576]{2,1,0:T(8,128)(2,1)}, bf16[4,32,576]{2,1,0:T(8,128)(2,1)S(1)}, u32[]{:S(2)}, u32[]{:S(2)}) collective-permute-start(bf16[4,32,576]{2,1,0:T(8,128)(2,1)} %refs_3_.1), channel_id=1, source_target_pairs={{0,4},{2,6},{4,0},{6,2},{8,12},{10,14},{12,8},{14,10},{16,20},{18,... | collective-permute-start | bytes 442376 | tf_op jit(solution)/shard_map/ppermute | solution.py:512
  10.7 11.3 %collective-permute-start.5 = (bf16[4,32,576]{2,1,0:T(8,128)(2,1)}, bf16[4,32,576]{2,1,0:T(8,128)(2,1)S(1)}, u32[]{:S(2)}, u32[]{:S(2)}) collective-permute-start(bf16[4,32,576]{2,1,0:T(8,128)(2,1)} %refs_3_.1), channel_id=1, source_target_pairs={{0,2},{2,4},{4,6},{6,0},{8,10},{10,12},{12,14},{14,8},{16,18},{18,... | collective-permute-start | bytes 442376 | tf_op jit(solution)/shard_map/ppermute | solution.py:512
  15.3 15.3 %all-to-all-start = ((bf16[16,16,512]{2,1,0:T(8,128)(2,1)}), bf16[16,16,512]{2,1,0:T(8,128)(2,1)}, u32[]{:S(2)}, u32[]{:S(2)}) async-start(bf16[16,16,512]{2,1,0:T(8,128)(2,1)} %bitcast.2), calls=%async_computation | async-start | bytes 524288 | tf_op jit(solution)/shard_map/all_to_all | solution.py:509
  22.0 0.9 %copy-start = (bf16[4,32,576]{2,1,0:T(8,128)(2,1)S(1)}, bf16[4,32,576]{2,1,0:T(8,128)(2,1)}, u32[]{:S(2)}) copy-start(bf16[4,32,576]{2,1,0:T(8,128)(2,1)} %refs_3_.1) | copy-start | bytes 442372
  24.7 13.7 %collective-permute-start.7 = (bf16[192,640]{1,0:T(8,128)(2,1)}, bf16[192,640]{1,0:T(8,128)(2,1)}, u32[]{:S(2)}, u32[]{:S(2)}) collective-permute-start(bf16[192,640]{1,0:T(8,128)(2,1)} %get-tuple-element.17.refs_1_), channel_id=1, source_target_pairs={{0,6},{2,0},{4,2},{6,4},{8,14},{10,8},{12,10},{14,12},{16,22},{18,... | collective-permute-start | bytes 737288 | tf_op jit(solution)/shard_map/ppermute | solution.py:575
  27.4 11.4 %collective-permute-start.8 = (bf16[192,640]{1,0:T(8,128)(2,1)}, bf16[192,640]{1,0:T(8,128)(2,1)}, u32[]{:S(2)}, u32[]{:S(2)}) collective-permute-start(bf16[192,640]{1,0:T(8,128)(2,1)} %get-tuple-element.18.refs_2_), channel_id=1, source_target_pairs={{0,4},{2,6},{4,0},{6,2},{8,12},{10,14},{12,8},{14,10},{16,20},{18,... | collective-permute-start | bytes 737288 | tf_op jit(solution)/shard_map/ppermute | solution.py:575
  28.0 10.8 %collective-permute-start.9 = (bf16[192,640]{1,0:T(8,128)(2,1)}, bf16[192,640]{1,0:T(8,128)(2,1)}, u32[]{:S(2)}, u32[]{:S(2)}) collective-permute-start(bf16[192,640]{1,0:T(8,128)(2,1)} %get-tuple-element.19.refs_3_), channel_id=1, source_target_pairs={{0,2},{2,4},{4,6},{6,0},{8,10},{10,12},{12,14},{14,8},{16,18},{18,... | collective-permute-start | bytes 737288 | tf_op jit(solution)/shard_map/ppermute | solution.py:575
  28.6 14.1 %collective-permute-start.6 = (bf16[448,640]{1,0:T(8,128)(2,1)}, bf16[448,640]{1,0:T(8,128)(2,1)}, u32[]{:S(2)}, u32[]{:S(2)}) collective-permute-start(bf16[448,640]{1,0:T(8,128)(2,1)} %get-tuple-element.16.refs_0_), channel_id=1, source_target_pairs={{0,1},{1,0},{2,3},{3,2},{4,5},{5,4},{6,7},{7,6},{8,9},{9,8},{10,11... | collective-permute-start | bytes 1720328 | tf_op jit(solution)/shard_map/ppermute | solution.py:582
  33.9 15.1 %all-to-all-start.1 = ((bf16[16,16,512]{2,1,0:T(8,128)(2,1)}), bf16[16,16,512]{2,1,0:T(8,128)(2,1)}, u32[]{:S(2)}, u32[]{:S(2)}) async-start(bf16[16,16,512]{2,1,0:T(8,128)(2,1)} %bitcast.4), calls=%async_computation.1 | async-start | bytes 524288 | tf_op jit(solution)/shard_map/all_to_all | solution.py:574
  38.8 3.9 %collective-permute-start.10 = (bf16[192,640]{1,0:T(8,128)(2,1)}, bf16[192,640]{1,0:T(8,128)(2,1)S(1)}, u32[]{:S(2)}, u32[]{:S(2)}) collective-permute-start(bf16[192,640]{1,0:T(8,128)(2,1)} %get-tuple-element.21.refs_2_), channel_id=1, source_target_pairs={{0,1},{1,0},{2,3},{3,2},{4,5},{5,4},{6,7},{7,6},{8,9},{9,8},{10,11... | collective-permute-start | bytes 737288 | tf_op jit(solution)/shard_map/ppermute | solution.py:582
  38.8 3.9 %collective-permute-start.11 = (bf16[192,640]{1,0:T(8,128)(2,1)}, bf16[192,640]{1,0:T(8,128)(2,1)S(1)}, u32[]{:S(2)}, u32[]{:S(2)}) collective-permute-start(bf16[192,640]{1,0:T(8,128)(2,1)} %get-tuple-element.22.refs_4_), channel_id=1, source_target_pairs={{0,1},{1,0},{2,3},{3,2},{4,5},{5,4},{6,7},{7,6},{8,9},{9,8},{10,11... | collective-permute-start | bytes 737288 | tf_op jit(solution)/shard_map/ppermute | solution.py:582
  39.3 3.4 %collective-permute-start.12 = (bf16[192,640]{1,0:T(8,128)(2,1)}, bf16[192,640]{1,0:T(8,128)(2,1)S(1)}, u32[]{:S(2)}, u32[]{:S(2)}) collective-permute-start(bf16[192,640]{1,0:T(8,128)(2,1)} %get-tuple-element.23.refs_6_), channel_id=1, source_target_pairs={{0,1},{1,0},{2,3},{3,2},{4,5},{5,4},{6,7},{7,6},{8,9},{9,8},{10,11... | collective-permute-start | bytes 737288 | tf_op jit(solution)/shard_map/ppermute | solution.py:582

commit v4 on v3

--- a/solution.py
+++ b/solution.py
@@ -154,8 +154,21 @@
     fill_table(geo, counts_ref, table_ref)
 
 
-def state_kernel(geo, s_hbm, c_hbm, *refs):
-    r_hbm, y_ref, r_ref, s_ref, r_all, y_all, counts_ref, sems = refs[-8:]
+def fill_pool(pool, pieces, prompts):
+    local, entry = pieces[0].shape[1:]
+    pool[:, :, entry:] = jnp.zeros(pool.shape[:2] + (pool.shape[2] - entry,), BF16)
+    for n, piece in enumerate(pieces):
+        pool[n * prompts : (n + 1) * prompts, :, :entry] = piece[...]
+
+
+def state_kernel(geo, table_ref, s_hbm, c_hbm, own_hbm, *refs):
+    pieces, refs = refs[: geo["width"] - 1], refs[-14:]
+    r_hbm, y_hbm, o_hbm, y_ref, o_ref, r_ref, s_ref, r_all, y_all, pool = refs[:10]
+    parts_ref, counts_ref, sems, piece_sems = refs[10:]
+    pieces = [
+        pltpu.make_async_copy(piece, parts_ref.at[n], piece_sems.at[n])
+        for n, piece in enumerate((own_hbm, *pieces))
+    ]
     rows, wide = r_ref.shape
     prompts, heads, dk, dv = s_ref.shape
     me = lax.axis_index("roll")
@@ -166,7 +179,7 @@
     for c in range(parts):
         sl = pl.ds(c * (heads // parts), heads // parts)
         copies.append(pltpu.make_async_copy(s_hbm.at[:, sl], s_ref.at[:, sl], sems.at[c]))
-    for copy in copies:
+    for copy in copies + pieces:
         copy.start()
     few, own = rows // parts, slots * steps
     part, rest = split(lanes((rows, rows), 0), few)
@@ -187,23 +200,35 @@
         for at in range(wide // dk):
             h = c * (wide // dk) + at
             r = r_all[c * few : (c + 1) * few, at * dk : (at + 1) * dk]
-            acc = dot(r * keep[0], s_ref[0, h])
-            for p in range(1, prompts):
-                acc = acc + dot(r * keep[p], s_ref[p, h])
+            wide_r = jnp.concatenate([r * k for k in keep], axis=1)
+            acc = dot(wide_r, s_ref[:, h].reshape(prompts * dk, dv))
             y_all[c * few : (c + 1) * few, at * dv : (at + 1) * dv] = acc.astype(BF16)
     y_ref[...] = dot(back, y_all[...]).astype(BF16)
-
-
-def kda_out_kernel(geo, y_hbm, _, a_ref, o_hbm, y_ref, o_ref, sems):
+    send = [pltpu.make_async_copy(y_ref, y_hbm, sems.at[0])]
+    send[0].start()
+    for copy in pieces:
+        copy.wait()
+    width, hops, pairs = geo["width"], geo["hops"], geo["pairs"]
+    fill_pool(pool, [parts_ref.at[n] for n in range(width)], prompts)
+    local = pool.shape[1]
+    for s in range(width):
+        for pair in range(pairs):
+            at = (s * hops + hops - 1) * pairs + pair
+            to = (s * pairs + pair) * local
+            o_ref[to : to + local, :] = pool[table_ref[at]]
+    send.append(pltpu.make_async_copy(o_ref, o_hbm, piece_sems.at[1]))
+    send[1].start()
+    for copy in send:
+        copy.wait()
+
+
+def kda_out_kernel(geo, _, y_ref, a_ref, o_hbm, o_ref, sems):
     per, parts = geo["per"], geo["parts"]
     rows, wide = y_ref.shape
-    copy = pltpu.make_async_copy(y_hbm, y_ref, sems.at[0])
-    copy.start()
     me = lax.axis_index("roll")
     shape = (2 * per * parts, rows)
     part, place = fan_rows(geo, shape, 1, me)
     pick = one_hot((lanes(shape, 0) == part * (2 * per) + place) & (place >= 0))
-    copy.wait()
     send = []
     for c in range(parts):
         sl = pl.ds(c * wide, wide)
@@ -216,34 +241,19 @@
         copy.wait()
 
 
-def select_kernel(geo, table_ref, *refs):
-    width, order, prompts, pairs, entry = (
-        geo[n] for n in ("width", "order", "prompts", "pairs", "entry")
-    )
-    o_refs, plane_pool, column_pool = refs[-2 - width : -2], *refs[-2:]
-    column, plane = refs[: -2 - 2 * width], refs[-2 - 2 * width : -2 - width]
-    for pool, pieces in ((plane_pool, plane), (column_pool, column)):
-        pool[:, :, entry:] = jnp.zeros(pool.shape[:2] + (pool.shape[2] - entry,), BF16)
-        for n, piece in enumerate(pieces):
-            pool[n * prompts : (n + 1) * prompts, :, :entry] = piece[...]
-    local = plane_pool.shape[1]
-    sent = len(column) * pairs * local
-    at = 0
-    for s in range(width):
-        to = 0
-        for hop in order:
-            for pair in range(pairs):
-                if hop == 0:
-                    o_ref, rows, pool = o_refs[0], sent + (s * pairs + pair) * local, plane_pool
-                else:
-                    o_ref, rows, pool = o_refs[s], to * local, column_pool
-                    to += 1
-                o_ref[rows : rows + local, :] = pool[table_ref[at]]
-                at += 1
+def select_kernel(geo, table_ref, _, *refs):
+    width, hops, prompts, pairs = (geo[n] for n in ("width", "hops", "prompts", "pairs"))
+    pieces, o_refs, pool = refs[: hops - 1], refs[hops - 1 : -1], refs[-1]
+    fill_pool(pool, [pieces[geo["column"].index(h)] for h in range(1, hops)], prompts)
+    local = pool.shape[1]
+    for s, o_ref in enumerate(o_refs):
+        for to in range((hops - 1) * pairs):
+            at = s * hops * pairs + to
+            o_ref[to * local : (to + 1) * local, :] = pool[table_ref[at]]
 
 
 def query_kernel(geo, q_hbm, f_hbm, c_hbm, l_hbm, _, o_ref, n_ref, length_ref, *scratch):
-    q_ref, f_ref, counts_ref, len_ref, sems = scratch
+    q_ref, tall, f_ref, counts_ref, len_ref, sems = scratch
     total, wide = q_ref.shape
     width, per, steps, entry = geo["width"], geo["per"], geo["steps"], geo["entry"]
     group, prompts, per_mate = (geo[n] for n in ("group", "prompts", "per_mate"))
@@ -263,12 +273,11 @@
         copy.start()
     row, col = lanes((total, total), 0), lanes((total, total), 1)
     shift, rest = split(row, n)
-    i, step = split(rest, steps)
+    step, i = split(rest, per_mate)
     pick = one_hot(col == step * per + shift + width * i)
-    block = n_ref.shape[0] // width
-    n_ref[...] = jnp.zeros(n_ref.shape, BF16)
+    n_ref[:, entry:] = jnp.zeros((total, padded - entry), BF16)
     me = lax.axis_index("roll")
-    sample = split(lanes((n, length_ref.shape[1]), 0), steps)[0]
+    sample = split(lanes((n, length_ref.shape[1]), 0), per_mate)[1]
     for copy in small:
         copy.wait()
     for s in range(width):
@@ -279,24 +288,30 @@
             k = prompt_at(counts_ref, owner, j)
             length = jnp.where(sample == i, len_ref[owner * prompts + k], length)
         length_ref[s * n : (s + 1) * n, :] = length
-    out = dot(pick, f_ref[...]).astype(BF16)
-    for s in range(width):
-        n_ref[s * block : s * block + n, :entry] = out[s * n : (s + 1) * n]
+    n_ref[:, :entry] = dot(pick, f_ref[...]).astype(BF16)
     for c, copy in enumerate(copies):
         copy.wait()
-        out = dot(pick, q_ref[:, c * unit : (c + 1) * unit])
-        even = out[:, :padded].astype(BF16)
-        odd = pltpu.roll(out[:, unit - padded :], entry, 1).astype(BF16)
+        tiles = range(c * unit // 128, (c + 1) * unit // 128)
+        for k in tiles:
+            tall[k] = q_ref[:, k * 128 : (k + 1) * 128].astype(F32)
         for s in range(width):
+            out = [
+                jnp.concatenate(
+                    [tall[k, pl.ds(t * per + s, per_mate, width), :] for t in range(steps)], axis=0
+                )
+                for k in tiles
+            ]
             at = (s * heads + 2 * c) * n
-            o_ref[at : at + n, :] = even[s * n : (s + 1) * n]
-            o_ref[at + n : at + 2 * n, :] = odd[s * n : (s + 1) * n]
+            even = jnp.concatenate(out[: padded // 128], axis=1)
+            odd = pltpu.roll(jnp.concatenate(out[-padded // 128 :], axis=1), entry, 1)
+            o_ref[at : at + n, :] = even.astype(BF16)
+            o_ref[at + n : at + 2 * n, :] = odd.astype(BF16)
 
 
 def latent_kernel(geo, w_hbm, *refs):
     width, steps, per, per_mate = (geo[n] for n in ("width", "steps", "per", "per_mate"))
     halves, local, pairs, order = (geo[n] for n in ("halves", "local", "pairs", "order"))
-    arrays = halves * width
+    arrays = halves * (width + 1)
     k_hbm, refs = refs[:arrays], refs[arrays:]
     _, q_ref, n_ref, length_ref, o_hbm, keys, ctx, out, w_ref, o_ref, sems = refs
     heads, rank, dv = w_ref.shape
@@ -306,17 +321,17 @@
     piece = sent + few
     old = halves * piece
     n = per_mate * steps
-    block = n_ref.shape[0] // width
+    block = keys.shape[1] - old
     copies = []
     for s in range(width):
         for e in range(halves):
-            first = k_hbm[e].at[pl.ds(sent + s * few, few)], keys.at[s, pl.ds(e * piece + sent, few)]
-            rest = k_hbm[s * halves + e].at[pl.ds(0, sent)], keys.at[s, pl.ds(e * piece, sent)]
+            first = k_hbm[e * (width + 1) + width].at[pl.ds(s * few, few)], keys.at[s, pl.ds(e * piece + sent, few)]
+            rest = k_hbm[e * (width + 1) + s], keys.at[s, pl.ds(e * piece, sent)]
             for src, dst in (rest, first):
                 copies.append(pltpu.make_async_copy(src, dst, sems.at[len(copies)]))
     each = len(copies) // width
     copies.append(pltpu.make_async_copy(w_hbm, w_ref, sems.at[len(copies)]))
-    for copy in copies:
+    for copy in copies[:-1]:
         copy.start()
     _, b = split(lax.axis_index("roll"), width)
     row, col = lanes((n, old), 0), lanes((n, old), 1)
@@ -331,17 +346,20 @@
     of_carry = []
     for carry in range(2):
         other = slot_sample(geo, hop, pair, carry)
-        mine = (other == split(row, steps)[0]) & (other < per_mate)
+        mine = (other == split(row, per_mate)[1]) & (other < per_mate)
         of_carry.append(jnp.where(mine, pos, halves * local))
     row, col = lanes((n, block), 0), lanes((n, block), 1)
-    behind = row - col
-    allowed_new = ((behind >= 0) & (behind <= split(row, steps)[1]))[None]
+    (step, sample), (step_of, sample_of) = split(row, per_mate), split(col, per_mate)
+    allowed_new = ((sample == sample_of) & (step_of <= step))[None]
     scores = []
     for s in range(width):
         query = q_ref[s * heads * n : (s + 1) * heads * n, :]
-        keys[s, old:, :] = n_ref[s * block : (s + 1) * block, :]
+        keys[s, old : old + n, :] = n_ref[s * n : (s + 1) * n, :]
+        keys[s, old + n :, :] = jnp.zeros((block - n, keys.shape[2]), BF16)
         for copy in copies[s * each : (s + 1) * each]:
             copy.wait()
+        if s == 0:
+            copies[-1].start()
         scores.append(dot_t(query, keys[s]).reshape(heads, n, old + block) * geo["scale"])
     weights = []
     for s in range(width):
@@ -369,7 +387,7 @@
         out[:, h * dv : (h + 1) * dv] = dot(ctx[h], w_ref[h]).astype(BF16)
     rows = steps * per
     shift, rest = split(lanes((rows, rows), 1), n)
-    sample, step = split(rest, steps)
+    step, sample = split(rest, per_mate)
     place = step * per + shift + width * sample
     pick = one_hot(lanes((rows, rows), 0) == place)
     send = []
@@ -474,6 +492,7 @@
         local=local,
         pairs=max(-(-per_mate // depth), -(-16 // local)),
         order=[*range(1, hops), 0],
+        column=[h for h in (3, 1, 2, *range(4, hops)) if h < hops],
         scale=192.0**-0.5,
         heads=heads,
         parts=parts,
@@ -508,12 +527,10 @@
     )
     got = lax.all_to_all(reads, "roll", 0, 0, tiled=True)
 
-    plane = [latent_prefill] + [
-        lax.ppermute(latent_prefill, "roll", mates(-1, s)) for s in range(1, width)
-    ]
+    plane = [lax.ppermute(latent_prefill, "roll", mates(-1, s)) for s in range(1, width)]
     column = [
         lax.ppermute(latent_prefill, "roll", [(i, (i - width * h) % group) for i in range(group)])
-        for h in range(1, hops)
+        for h in geo["column"]
     ]
     few = geo["pairs"] * local
     sent = (hops - 1) * few
@@ -528,14 +545,15 @@
         geo,
         (
             shape((heads * rows, padded), BF16),
-            shape((width * pad_to(per_mate * steps, 128), padded), BF16),
+            shape((rows, padded), BF16),
             shape((rows, 128), jnp.int32),
         ),
-        (mla_q.reshape(rows, wide), mla_new.reshape(rows, entry), counts, prompt_len, reads),
+        (mla_q.reshape(rows, wide), mla_new.reshape(rows, entry), counts, prompt_len, column[0]),
         hbm=4,
         after=1,
         scratch=[
             pltpu.VMEM((rows, wide), BF16),
+            pltpu.VMEM((wide // 128, rows, 128), F32),
             pltpu.VMEM((rows, entry), BF16),
             pltpu.SMEM(counts.shape, jnp.int32),
             pltpu.SMEM(prompt_len.shape, jnp.int32),
@@ -545,51 +563,52 @@
     chosen = call(
         select_kernel,
         geo,
-        tuple(shape((sent + (s == 0) * width * few, padded), BF16) for s in range(width)),
-        (table, *column, *plane),
+        tuple(shape((sent, padded), BF16) for s in range(width)),
+        (table, lengths, *column),
         smem=1,
+        after=1,
+        us=20,
+        scratch=[pltpu.VMEM(((hops - 1) * prompts, local, padded), BF16)],
+    )
+    products, own = call(
+        state_kernel,
+        geo,
+        (pltpu.HBM(fan, BF16), pltpu.HBM((width * few, padded), BF16)),
+        (table, kda_prefill, counts, latent_prefill, *plane, *chosen, got),
+        smem=1,
+        hbm=3,
+        after=len(plane) + len(chosen) + 1,
         us=20,
         scratch=[
-            pltpu.VMEM((width * prompts, local, padded), BF16),
-            pltpu.VMEM(((hops - 1) * prompts, local, padded), BF16),
-        ],
-    )
-    products = call(
-        state_kernel,
-        geo,
-        shape(fan, BF16),
-        (kda_prefill, counts, *chosen, got),
-        hbm=2,
-        after=len(chosen) + 1,
-        us=20,
-        scratch=[
+            pltpu.VMEM(fan, BF16),
+            pltpu.VMEM((width * few, padded), BF16),
             pltpu.VMEM(fan, BF16),
             pltpu.VMEM(kda_prefill.shape, BF16),
             pltpu.VMEM(fan, BF16),
             pltpu.VMEM(fan, BF16),
+            pltpu.VMEM((width * prompts, local, padded), BF16),
+            pltpu.VMEM((width,) + latent_prefill.shape, BF16),
             pltpu.SMEM(counts.shape, jnp.int32),
             pltpu.SemaphoreType.DMA((parts + 2,)),
+            pltpu.SemaphoreType.DMA((width,)),
         ],
     )
     back = lax.all_to_all(products, "roll", 0, 0, tiled=True)
     taken = [lax.ppermute(chosen[s], "roll", mates(-1, s)) for s in range(1, width)]
-    taken = [chosen[0], *hold(taken, products)]
-    caches = []
-    for piece in taken:
-        caches.append(piece)
-        for e in range(1, halves):
-            caches.append(
-                lax.ppermute(piece, "exp", [(i, (i - e) % halves) for i in range(halves)])
-            )
+    taken = [*hold([chosen[0], *taken], products), own]
+    caches = list(taken)
+    for e in range(1, halves):
+        pairs = [(i, (i - e) % halves) for i in range(halves)]
+        caches += [lax.ppermute(piece, "exp", pairs) for piece in taken]
     mla_out = call(
         latent_kernel,
         geo,
         pltpu.HBM((rows, heads * dv), BF16),
         (w_uv, *caches, products, queries, fresh, lengths),
-        hbm=1,
-        after=1 + len(caches),
+        hbm=2 + width,
+        after=len(caches) - width,
         scratch=[
-            pltpu.VMEM((width, fresh.shape[0] // width + hops * few * halves, padded), BF16),
+            pltpu.VMEM((width, hops * few * halves + pad_to(per_mate * steps, 128), padded), BF16),
             pltpu.VMEM((heads, rows, rank), BF16),
             pltpu.VMEM((rows, heads * dv), BF16),
             pltpu.VMEM(w_uv.shape, BF16),
@@ -601,10 +620,9 @@
         kda_out_kernel,
         geo,
         pltpu.HBM((steps, per, kda_width), BF16),
-        (back, mla_out, coef),
-        hbm=2,
+        (mla_out, pltpu.with_memory_space_constraint(back, pltpu.VMEM), coef),
+        hbm=1,
         scratch=[
-            pltpu.VMEM(fan, BF16),
             pltpu.VMEM((steps, per, kda_width), BF16),
             pltpu.SemaphoreType.DMA((parts + 1,)),
         ],

time: 51.3 us -> 51.4 us (level)
  starting transfers between devices: 26.1 us -> 27.4 us
  local copies, waits for them, and re-layouts: 0.91 us -> 0.02 us
  Pallas kernels: 19.3 us -> 18.7 us
    all_to_all x1, starting transfers between devices: 4.47 us -> 7.15 us  [on_device(): back = lax.all_to_all(products, 'roll', 0, 0, tiled=True)]
    all_to_all x1, starting transfers between devices: 6.63 us -> 4.53 us  [on_device(): got = lax.all_to_all(reads, 'roll', 0, 0, tiled=True)]
    all_to_all x1, waiting for transfers between devices: 2.04 us -> 0.12 us  [on_device(): got = lax.all_to_all(reads, 'roll', 0, 0, tiled=True)]
    ppermute x4 -> x5, waiting for transfers between devices: 0.01 us -> 1.76 us  [on_device(): caches += [lax.ppermute(piece, 'exp', pairs) for piece in taken]]
    unnamed x2 -> x8, local copies, waits for them, and re-layouts: 0.91 us -> 0.02 us
    all_to_all x1, waiting for transfers between devices: 0.24 us -> 0.96 us  [on_device(): back = lax.all_to_all(products, 'roll', 0, 0, tiled=True)]
    pallas_call x6, Pallas kernels: 19.3 us -> 18.7 us  [call(): pl.pallas_call(functools.partial(kernel, geo), out_shape=out, in_specs=[p...]
    ppermute x4 -> x5, starting transfers between devices: 0.58 us -> 1.15 us  [on_device(): caches += [lax.ppermute(piece, 'exp', pairs) for piece in taken]]
  transfers between devices with their start and end apart: 15 -> 16, of which waited for: 4 -> 8; matrix products, arithmetic and copies ran while one was open for 0% -> 0% of each run, Pallas kernels for 34% -> 33%
where the time goes in v4:
time: 51.4 us; the launch traced here: 50.9 us
  starting transfers between devices  27.4 us (53%)
  Pallas kernels  18.7 us (36%)
  waiting for transfers between devices  4.07 us (8%)
  between operations  0.76 us (1%)
    pallas_call x6, Pallas kernels, call(): pl.pallas_call(functools.partial(kernel, geo), out_shape=out, in_specs=[p...  18.7 us
    all_to_all x1, starting transfers between devices, on_device(): back = lax.all_to_all(products, 'roll', 0, 0, tiled=True)  7.15 us
    ppermute x3, starting transfers between devices, on_device(): lax.ppermute(latent_prefill, 'roll', [(i, (i - width * h) % group) for i...  6.11 us
    ppermute x3, starting transfers between devices, on_device(): lax.ppermute(latent_prefill, 'roll', mates(-1, s))  4.88 us
    all_to_all x1, starting transfers between devices, on_device(): got = lax.all_to_all(reads, 'roll', 0, 0, tiled=True)  4.53 us
    ppermute x3, starting transfers between devices, on_device(): lax.ppermute(chosen[s], 'roll', mates(-1, s))  3.55 us
    ppermute x5, waiting for transfers between devices, on_device(): caches += [lax.ppermute(piece, 'exp', pairs) for piece in taken]  1.76 us
    ppermute x5, starting transfers between devices, on_device(): caches += [lax.ppermute(piece, 'exp', pairs) for piece in taken]  1.15 us
  transfers between devices with their start and end apart: 16, of which 8 were waited for; matrix products, arithmetic and copies ran while one was open for 0% of the time, Pallas kernels for 33%

profile of v4, /device:TPU:0, one launch (start us, length us, event | category | flops | bytes accessed | tf_op | source)
XLA Modules:
  0.0 50.9 jit_solution(12451361379950537134)
XLA Ops:
  0.6 3.1 %collective-permute-start.3 = (bf16[4,32,576]{2,1,0:T(8,128)(2,1)}, bf16[4,32,576]{2,1,0:T(8,128)(2,1)S(1)}, u32[]{:S(2)}, u32[]{:S(2)}) collective-permute-start(bf16[4,32,576]{2,1,0:T(8,128)(2,1)} %own_hbm.1), channel_id=1, source_target_pairs={{0,8},{2,10},{4,12},{6,14},{8,16},{10,18},{12,20},{14,22},{16,24},... | collective-permute-start | bytes 442376 | tf_op jit(solution)/shard_map/ppermute | solution.py:532
  3.7 2.1 %collective-permute-start.4 = (bf16[4,32,576]{2,1,0:T(8,128)(2,1)}, bf16[4,32,576]{2,1,0:T(8,128)(2,1)S(1)}, u32[]{:S(2)}, u32[]{:S(2)}) collective-permute-start(bf16[4,32,576]{2,1,0:T(8,128)(2,1)} %own_hbm.1), channel_id=1, source_target_pairs={{0,24},{2,26},{4,28},{6,30},{8,0},{10,2},{12,4},{14,6},{16,8},{18,... | collective-permute-start | bytes 442376 | tf_op jit(solution)/shard_map/ppermute | solution.py:532
  5.8 0.9 %collective-permute-start.5 = (bf16[4,32,576]{2,1,0:T(8,128)(2,1)}, bf16[4,32,576]{2,1,0:T(8,128)(2,1)S(1)}, u32[]{:S(2)}, u32[]{:S(2)}) collective-permute-start(bf16[4,32,576]{2,1,0:T(8,128)(2,1)} %own_hbm.1), channel_id=1, source_target_pairs={{0,16},{2,18},{4,20},{6,22},{8,24},{10,26},{12,28},{14,30},{16,0},... | collective-permute-start | bytes 442376 | tf_op jit(solution)/shard_map/ppermute | solution.py:532
  6.7 2.4 %collective-permute-start = (bf16[4,32,576]{2,1,0:T(8,128)(2,1)}, bf16[4,32,576]{2,1,0:T(8,128)(2,1)}, u32[]{:S(2)}, u32[]{:S(2)}) collective-permute-start(bf16[4,32,576]{2,1,0:T(8,128)(2,1)} %own_hbm.1), channel_id=1, source_target_pairs={{0,6},{2,0},{4,2},{6,4},{8,14},{10,8},{12,10},{14,12},{16,22},{18,... | collective-permute-start | bytes 442376 | tf_op jit(solution)/shard_map/ppermute | solution.py:530
  9.2 0.5 collective-permute-start.1
  9.7 3.1 %reads_kernel.1 = (bf16[256,512]{1,0:T(8,128)(2,1)}, f32[2,32,2048]{2,1,0:T(8,128)S(1)}, s32[32]{0:T(128)S(1)}) custom-call(bf16[2,32,2048]{2,1,0:T(8,128)(2,1)} %q_hbm.1, bf16[2,32,2048]{2,1,0:T(8,128)(2,1)} %k_hbm.1, f32[2,32,2048]{2,1,0:T(8,128)} %g_hbm.1, bf16[2,32,2048]{2,1,0:T(8,128)(2,1)} %v_hbm.1, f32[2,16,32]{2,1,0:T(8,128)} %bitcast.13, ...), custom_call_target="tpu_custom_call" | custom-call | tf_op jit(solution)/shard_map/reads_kernel/pallas_call | solution.py:423
  12.8 4.5 %all-to-all-start = ((bf16[16,16,512]{2,1,0:T(8,128)(2,1)}), bf16[16,16,512]{2,1,0:T(8,128)(2,1)}, u32[]{:S(2)}, u32[]{:S(2)}) async-start(bf16[16,16,512]{2,1,0:T(8,128)(2,1)} %bitcast.4), calls=%async_computation | async-start | bytes 524288 | tf_op jit(solution)/shard_map/all_to_all | solution.py:528
  17.4 0.0 collective-permute-done.3._.refs_0_
  17.4 1.9 %collective-permute-start.2 = (bf16[4,32,576]{2,1,0:T(8,128)(2,1)}, bf16[4,32,576]{2,1,0:T(8,128)(2,1)}, u32[]{:S(2)}, u32[]{:S(2)}) collective-permute-start(bf16[4,32,576]{2,1,0:T(8,128)(2,1)} %own_hbm.1), channel_id=1, source_target_pairs={{0,2},{2,4},{4,6},{6,0},{8,10},{10,12},{12,14},{14,8},{16,18},{18,... | collective-permute-start | bytes 442376 | tf_op jit(solution)/shard_map/ppermute | solution.py:530
  19.3 2.3 %query_kernel.1 = (bf16[1024,640]{1,0:T(8,128)(2,1)S(1)}, bf16[64,640]{1,0:T(8,128)(2,1)S(1)}, s32[64,128]{1,0:T(8,128)S(1)}) custom-call(bf16[64,9216]{1,0:T(8,128)(2,1)} %bitcast.10, bf16[64,576]{1,0:T(8,128)(2,1)} %bitcast.12, s32[4,16]{1,0:T(4,128)} %bitcast.15, s32[64]{0:T(128)} %l_hbm.1, bf16[4,32,576]{2,1,0:T(8,128)(2,1)S(1)} %collective-permute-done.3._.refs_0_), custom_call_target="tpu_custom_call" | custom-call | tf_op jit(solution)/shard_map/query_kernel/pallas_call | solution.py:423
  21.6 0.0 copy-start.2
  21.6 0.0 collective-permute-done.4.refs_1_
  21.6 0.6 %collective-permute-done.5.refs_2_ = bf16[4,32,576]{2,1,0:T(8,128)(2,1)S(1)} collective-permute-done((bf16[4,32,576]{2,1,0:T(8,128)(2,1)}, bf16[4,32,576]{2,1,0:T(8,128)(2,1)S(1)}, u32[]{:S(2)}, u32[]{:S(2)}) %collective-permute-start.5) | collective-permute-done | bytes 147488 | tf_op jit(solution)/shard_map/ppermute | solution.py:532
  22.2 1.5 %select_kernel.1 = (bf16[192,640]{1,0:T(8,128)(2,1)S(1)}, bf16[192,640]{1,0:T(8,128)(2,1)}, bf16[192,640]{1,0:T(8,128)(2,1)}, bf16[192,640]{1,0:T(8,128)(2,1)}) custom-call(s32[32]{0:T(128)S(1)} %get-tuple-element.18.table_ref, s32[64,128]{1,0:T(8,128)S(1)} %get-tuple-element.19._.refs_13_, bf16[4,32,576]{2,1,0:T(8,128)(2,1)S(1)} %collective-permute-done.3._.refs_0_, ...), custom_call_target="tpu_custom_call" | custom-call | flops 40000000000 | bytes 60000000 | tf_op jit(solution)/shard_map/select_kernel/pallas_call | solution.py:423
  23.7 0.0 copy-done.2
  23.7 0.0 copy-start.1
  23.7 2.4 %collective-permute-start.6 = (bf16[192,640]{1,0:T(8,128)(2,1)}, bf16[192,640]{1,0:T(8,128)(2,1)}, u32[]{:S(2)}, u32[]{:S(2)}) collective-permute-start(bf16[192,640]{1,0:T(8,128)(2,1)} %get-tuple-element.21.refs_4_), channel_id=1, source_target_pairs={{0,6},{2,0},{4,2},{6,4},{8,14},{10,8},{12,10},{14,12},{16,22},{18,... | collective-permute-start | bytes 737288 | tf_op jit(solution)/shard_map/ppermute | solution.py:597
  26.1 0.5 collective-permute-start.7
  26.6 0.0 collective-permute-done.refs_0_
  26.7 0.6 %collective-permute-start.8 = (bf16[192,640]{1,0:T(8,128)(2,1)}, bf16[192,640]{1,0:T(8,128)(2,1)}, u32[]{:S(2)}, u32[]{:S(2)}) collective-permute-start(bf16[192,640]{1,0:T(8,128)(2,1)} %get-tuple-element.23.refs_6_), channel_id=1, source_target_pairs={{0,2},{2,4},{4,6},{6,0},{8,10},{10,12},{12,14},{14,8},{16,18},{18,... | collective-permute-start | bytes 737288 | tf_op jit(solution)/shard_map/ppermute | solution.py:597
  27.2 0.0 collective-permute-done.1.refs_1_
  27.2 0.0 collective-permute-done.2.refs_2_
  27.2 0.1 all-to-all-done
  27.4 3.8 %state_kernel.1 = (bf16[256,512]{1,0:T(8,128)(2,1)}, bf16[256,640]{1,0:T(8,128)(2,1)}) custom-call(s32[32]{0:T(128)S(1)} %get-tuple-element.18.table_ref, bf16[4,16,128,128]{3,2,1,0:T(8,128)(2,1)} %s_hbm.1, s32[4,16]{1,0:T(4,128)} %bitcast.16, bf16[4,32,576]{2,1,0:T(8,128)(2,1)} %own_hbm.1, bf16[4,32,576]{2,1,0:T(8,128)(2,1)} %collective-permute-done.refs_0_, ...), custom_call_target="tpu_custom_call" | custom-call | flops 40000000000 | bytes 60000000 | tf_op jit(solution)/shard_map/state_kernel/pallas_call | solution.py:423
  31.2 0.0 copy-done.1
  31.2 0.1 collective-permute-start.13
  31.3 7.2 %all-to-all-start.1 = ((bf16[16,16,512]{2,1,0:T(8,128)(2,1)}), bf16[16,16,512]{2,1,0:T(8,128)(2,1)}, u32[]{:S(2)}, u32[]{:S(2)}) async-start(bf16[16,16,512]{2,1,0:T(8,128)(2,1)} %bitcast.9), calls=%async_computation.1 | async-start | bytes 524288 | tf_op jit(solution)/shard_map/all_to_all | solution.py:596
  38.4 0.0 collective-permute-done.6.refs_2_
  38.4 0.6 %collective-permute-done.7.refs_3_ = bf16[192,640]{1,0:T(8,128)(2,1)} collective-permute-done((bf16[192,640]{1,0:T(8,128)(2,1)}, bf16[192,640]{1,0:T(8,128)(2,1)}, u32[]{:S(2)}, u32[]{:S(2)}) %collective-permute-start.7) | collective-permute-done | bytes 245792 | tf_op jit(solution)/shard_map/ppermute | solution.py:597
  39.1 0.0 collective-permute-done.8.refs_4_
  39.1 0.0 copy-start
  39.1 0.0 copy-start.3
  39.1 0.1 collective-permute-start.10
  39.1 0.5 collective-permute-start.11
  39.6 0.1 collective-permute-start.12
  39.7 0.4 collective-permute-start.9
  40.2 0.7 %collective-permute-done.10.refs_6_ = bf16[192,640]{1,0:T(8,128)(2,1)S(1)} collective-permute-done((bf16[192,640]{1,0:T(8,128)(2,1)}, bf16[192,640]{1,0:T(8,128)(2,1)S(1)}, u32[]{:S(2)}, u32[]{:S(2)}) %collective-permute-start.10) | collective-permute-done | bytes 245792 | tf_op jit(solution)/shard_map/ppermute | solution.py:602
  40.9 0.4 collective-permute-done.11.refs_7_
  41.2 0.4 collective-permute-done.12.refs_8_
  41.6 0.4 collective-permute-done.9.refs_5_
  41.9 0.0 collective-permute-done.13.refs_9_
  41.9 0.0 copy-done
  41.9 0.0 copy-done.3
  41.9 6.1 %latent_kernel.1._ = bf16[64,2048]{1,0:T(8,128)(2,1)} custom-call(bf16[16,512,128]{2,1,0:T(8,128)(2,1)} %w_hbm.1, bf16[192,640]{1,0:T(8,128)(2,1)} %get-tuple-element.26.refs_0_, bf16[192,640]{1,0:T(8,128)(2,1)} %get-tuple-element.27.refs_1_, bf16[192,640]{1,0:T(8,128)(2,1)} %get-tuple-element.28.refs_2_, bf16[192,640]{1,0:T(8,128)(2,1)} %get-tuple-element.29.refs_3_, ...), custom_call_target="tpu_custom_call" | custom-call | tf_op jit(solution)/shard_map/latent_kernel/pallas_call | solution.py:423
  48.0 1.0 %all-to-all-done.1 = bf16[16,16,512]{2,1,0:T(8,128)(2,1)} async-done(((bf16[16,16,512]{2,1,0:T(8,128)(2,1)}), bf16[16,16,512]{2,1,0:T(8,128)(2,1)}, u32[]{:S(2)}, u32[]{:S(2)}) %all-to-all-start.1) | async-done | bytes 262176 | tf_op jit(solution)/shard_map/all_to_all | solution.py:596
  49.0 1.9 %kda_out_kernel.1 = bf16[2,32,2048]{2,1,0:T(8,128)(2,1)} custom-call(bf16[64,2048]{1,0:T(8,128)(2,1)} %latent_kernel.1._, bf16[256,512]{1,0:T(8,128)(2,1)} %bitcast.7.y_ref, f32[2,32,2048]{2,1,0:T(8,128)S(1)} %get-tuple-element.33.a_ref), custom_call_target="tpu_custom_call" | custom-call | tf_op jit(solution)/shard_map/kda_out_kernel/pallas_call | solution.py:423
  (1 shorter events, 0.0 us)
Async XLA Ops:
  0.6 16.7 %collective-permute-start.3 = (bf16[4,32,576]{2,1,0:T(8,128)(2,1)}, bf16[4,32,576]{2,1,0:T(8,128)(2,1)S(1)}, u32[]{:S(2)}, u32[]{:S(2)}) collective-permute-start(bf16[4,32,576]{2,1,0:T(8,128)(2,1)} %own_hbm.1), channel_id=1, source_target_pairs={{0,8},{2,10},{4,12},{6,14},{8,16},{10,18},{12,20},{14,22},{16,24},... | collective-permute-start | bytes 442376 | tf_op jit(solution)/shard_map/ppermute | solution.py:532
  3.7 17.9 %collective-permute-start.4 = (bf16[4,32,576]{2,1,0:T(8,128)(2,1)}, bf16[4,32,576]{2,1,0:T(8,128)(2,1)S(1)}, u32[]{:S(2)}, u32[]{:S(2)}) collective-permute-start(bf16[4,32,576]{2,1,0:T(8,128)(2,1)} %own_hbm.1), channel_id=1, source_target_pairs={{0,24},{2,26},{4,28},{6,30},{8,0},{10,2},{12,4},{14,6},{16,8},{18,... | collective-permute-start | bytes 442376 | tf_op jit(solution)/shard_map/ppermute | solution.py:532
  5.8 16.4 %collective-permute-start.5 = (bf16[4,32,576]{2,1,0:T(8,128)(2,1)}, bf16[4,32,576]{2,1,0:T(8,128)(2,1)S(1)}, u32[]{:S(2)}, u32[]{:S(2)}) collective-permute-start(bf16[4,32,576]{2,1,0:T(8,128)(2,1)} %own_hbm.1), channel_id=1, source_target_pairs={{0,16},{2,18},{4,20},{6,22},{8,24},{10,26},{12,28},{14,30},{16,0},... | collective-permute-start | bytes 442376 | tf_op jit(solution)/shard_map/ppermute | solution.py:532
  6.7 19.9 %collective-permute-start = (bf16[4,32,576]{2,1,0:T(8,128)(2,1)}, bf16[4,32,576]{2,1,0:T(8,128)(2,1)}, u32[]{:S(2)}, u32[]{:S(2)}) collective-permute-start(bf16[4,32,576]{2,1,0:T(8,128)(2,1)} %own_hbm.1), channel_id=1, source_target_pairs={{0,6},{2,0},{4,2},{6,4},{8,14},{10,8},{12,10},{14,12},{16,22},{18,... | collective-permute-start | bytes 442376 | tf_op jit(solution)/shard_map/ppermute | solution.py:530
  9.2 18.1 %collective-permute-start.1 = (bf16[4,32,576]{2,1,0:T(8,128)(2,1)}, bf16[4,32,576]{2,1,0:T(8,128)(2,1)}, u32[]{:S(2)}, u32[]{:S(2)}) collective-permute-start(bf16[4,32,576]{2,1,0:T(8,128)(2,1)} %own_hbm.1), channel_id=1, source_target_pairs={{0,4},{2,6},{4,0},{6,2},{8,12},{10,14},{12,8},{14,10},{16,20},{18,... | collective-permute-start | bytes 442376 | tf_op jit(solution)/shard_map/ppermute | solution.py:530
  12.8 14.6 %all-to-all-start = ((bf16[16,16,512]{2,1,0:T(8,128)(2,1)}), bf16[16,16,512]{2,1,0:T(8,128)(2,1)}, u32[]{:S(2)}, u32[]{:S(2)}) async-start(bf16[16,16,512]{2,1,0:T(8,128)(2,1)} %bitcast.4), calls=%async_computation | async-start | bytes 524288 | tf_op jit(solution)/shard_map/all_to_all | solution.py:528
  17.4 9.9 %collective-permute-start.2 = (bf16[4,32,576]{2,1,0:T(8,128)(2,1)}, bf16[4,32,576]{2,1,0:T(8,128)(2,1)}, u32[]{:S(2)}, u32[]{:S(2)}) collective-permute-start(bf16[4,32,576]{2,1,0:T(8,128)(2,1)} %own_hbm.1), channel_id=1, source_target_pairs={{0,2},{2,4},{4,6},{6,0},{8,10},{10,12},{12,14},{14,8},{16,18},{18,... | collective-permute-start | bytes 442376 | tf_op jit(solution)/shard_map/ppermute | solution.py:530
  21.6 2.1 %copy-start.2 = (s32[64,128]{1,0:T(8,128)}, s32[64,128]{1,0:T(8,128)S(1)}, u32[]{:S(2)}) copy-start(s32[64,128]{1,0:T(8,128)S(1)} %get-tuple-element.19._.refs_13_) | copy-start | bytes 98308
  23.7 7.5 %copy-start.1 = (bf16[192,640]{1,0:T(8,128)(2,1)}, bf16[192,640]{1,0:T(8,128)(2,1)S(1)}, u32[]{:S(2)}) copy-start(bf16[192,640]{1,0:T(8,128)(2,1)S(1)} %get-tuple-element.20.refs_3_.refs_1_) | copy-start | bytes 737284
  23.7 14.7 %collective-permute-start.6 = (bf16[192,640]{1,0:T(8,128)(2,1)}, bf16[192,640]{1,0:T(8,128)(2,1)}, u32[]{:S(2)}, u32[]{:S(2)}) collective-permute-start(bf16[192,640]{1,0:T(8,128)(2,1)} %get-tuple-element.21.refs_4_), channel_id=1, source_target_pairs={{0,6},{2,0},{4,2},{6,4},{8,14},{10,8},{12,10},{14,12},{16,22},{18,... | collective-permute-start | bytes 737288 | tf_op jit(solution)/shard_map/ppermute | solution.py:597
  26.1 12.9 %collective-permute-start.7 = (bf16[192,640]{1,0:T(8,128)(2,1)}, bf16[192,640]{1,0:T(8,128)(2,1)}, u32[]{:S(2)}, u32[]{:S(2)}) collective-permute-start(bf16[192,640]{1,0:T(8,128)(2,1)} %get-tuple-element.22.refs_5_), channel_id=1, source_target_pairs={{0,4},{2,6},{4,0},{6,2},{8,12},{10,14},{12,8},{14,10},{16,20},{18,... | collective-permute-start | bytes 737288 | tf_op jit(solution)/shard_map/ppermute | solution.py:597
  26.7 12.4 %collective-permute-start.8 = (bf16[192,640]{1,0:T(8,128)(2,1)}, bf16[192,640]{1,0:T(8,128)(2,1)}, u32[]{:S(2)}, u32[]{:S(2)}) collective-permute-start(bf16[192,640]{1,0:T(8,128)(2,1)} %get-tuple-element.23.refs_6_), channel_id=1, source_target_pairs={{0,2},{2,4},{4,6},{6,0},{8,10},{10,12},{12,14},{14,8},{16,18},{18,... | collective-permute-start | bytes 737288 | tf_op jit(solution)/shard_map/ppermute | solution.py:597
  31.2 10.7 %collective-permute-start.13 = (bf16[256,640]{1,0:T(8,128)(2,1)}, bf16[256,640]{1,0:T(8,128)(2,1)}, u32[]{:S(2)}, u32[]{:S(2)}) collective-permute-start(bf16[256,640]{1,0:T(8,128)(2,1)} %get-tuple-element.30.refs_4_), channel_id=1, source_target_pairs={{0,1},{1,0},{2,3},{3,2},{4,5},{5,4},{6,7},{7,6},{8,9},{9,8},{10,11... | collective-permute-start | bytes 983048 | tf_op jit(solution)/shard_map/ppermute | solution.py:602
  31.3 17.7 %all-to-all-start.1 = ((bf16[16,16,512]{2,1,0:T(8,128)(2,1)}), bf16[16,16,512]{2,1,0:T(8,128)(2,1)}, u32[]{:S(2)}, u32[]{:S(2)}) async-start(bf16[16,16,512]{2,1,0:T(8,128)(2,1)} %bitcast.9), calls=%async_computation.1 | async-start | bytes 524288 | tf_op jit(solution)/shard_map/all_to_all | solution.py:596
  39.1 2.9 %copy-start = (bf16[256,512]{1,0:T(8,128)(2,1)S(1)}, bf16[256,512]{1,0:T(8,128)(2,1)}, u32[]{:S(2)}) copy-start(bf16[256,512]{1,0:T(8,128)(2,1)} %get-tuple-element.25.refs_0_.refs_10_) | copy-start | bytes 786436
  39.1 2.9 %copy-start.3 = (s32[64,128]{1,0:T(8,128)S(1)}, s32[64,128]{1,0:T(8,128)}, u32[]{:S(2)}) copy-start(s32[64,128]{1,0:T(8,128)} %copy-done.2) | copy-start | bytes 98308
  39.1 1.8 %collective-permute-start.10 = (bf16[192,640]{1,0:T(8,128)(2,1)}, bf16[192,640]{1,0:T(8,128)(2,1)S(1)}, u32[]{:S(2)}, u32[]{:S(2)}) collective-permute-start(bf16[192,640]{1,0:T(8,128)(2,1)} %get-tuple-element.27.refs_1_), channel_id=1, source_target_pairs={{0,1},{1,0},{2,3},{3,2},{4,5},{5,4},{6,7},{7,6},{8,9},{9,8},{10,11... | collective-permute-start | bytes 737288 | tf_op jit(solution)/shard_map/ppermute | solution.py:602
  39.1 2.1 %collective-permute-start.11 = (bf16[192,640]{1,0:T(8,128)(2,1)}, bf16[192,640]{1,0:T(8,128)(2,1)S(1)}, u32[]{:S(2)}, u32[]{:S(2)}) collective-permute-start(bf16[192,640]{1,0:T(8,128)(2,1)} %get-tuple-element.28.refs_2_), channel_id=1, source_target_pairs={{0,1},{1,0},{2,3},{3,2},{4,5},{5,4},{6,7},{7,6},{8,9},{9,8},{10,11... | collective-permute-start | bytes 737288 | tf_op jit(solution)/shard_map/ppermute | solution.py:602
  39.6 1.9 %collective-permute-start.12 = (bf16[192,640]{1,0:T(8,128)(2,1)}, bf16[192,640]{1,0:T(8,128)(2,1)S(1)}, u32[]{:S(2)}, u32[]{:S(2)}) collective-permute-start(bf16[192,640]{1,0:T(8,128)(2,1)} %get-tuple-element.29.refs_3_), channel_id=1, source_target_pairs={{0,1},{1,0},{2,3},{3,2},{4,5},{5,4},{6,7},{7,6},{8,9},{9,8},{10,11... | collective-permute-start | bytes 737288 | tf_op jit(solution)/shard_map/ppermute | solution.py:602
  39.7 2.2 %collective-permute-start.9 = (bf16[192,640]{1,0:T(8,128)(2,1)}, bf16[192,640]{1,0:T(8,128)(2,1)S(1)}, u32[]{:S(2)}, u32[]{:S(2)}) collective-permute-start(bf16[192,640]{1,0:T(8,128)(2,1)} %get-tuple-element.26.refs_0_), channel_id=1, source_target_pairs={{0,1},{1,0},{2,3},{3,2},{4,5},{5,4},{6,7},{7,6},{8,9},{9,8},{10,11... | collective-permute-start | bytes 737288 | tf_op jit(solution)/shard_map/ppermute | solution.py:602

commit v5 on v4

--- a/solution.py
+++ b/solution.py
@@ -548,7 +548,7 @@
             shape((rows, padded), BF16),
             shape((rows, 128), jnp.int32),
         ),
-        (mla_q.reshape(rows, wide), mla_new.reshape(rows, entry), counts, prompt_len, column[0]),
+        (mla_q.reshape(rows, wide), mla_new.reshape(rows, entry), counts, prompt_len, reads),
         hbm=4,
         after=1,
         scratch=[
@@ -564,7 +564,7 @@
         select_kernel,
         geo,
         tuple(shape((sent, padded), BF16) for s in range(width)),
-        (table, lengths, *column),
+        (table, reads, *column),
         smem=1,
         after=1,
         us=20,

time: 51.4 us -> 51.4 us (level)
    ppermute x3, waiting for transfers between devices: 0.59 us -> 2.94 us  [on_device(): lax.ppermute(latent_prefill, 'roll', [(i, (i - width * h) % group) for i...]
    ppermute x5, waiting for transfers between devices: 1.76 us -> 0.01 us  [on_device(): caches += [lax.ppermute(piece, 'exp', pairs) for piece in taken]]
    all_to_all x1, waiting for transfers between devices: 0.96 us -> 0.4 us  [on_device(): back = lax.all_to_all(products, 'roll', 0, 0, tiled=True)]
  transfers between devices with their start and end apart: 16 -> 16, of which waited for: 8 -> 4; matrix products, arithmetic and copies ran while one was open for 0% -> 0% of each run, Pallas kernels for 33% -> 33%
where the time goes in v5:
time: 51.4 us; the launch traced here: 50.9 us
  starting transfers between devices  27.3 us (53%)
  Pallas kernels  18.7 us (36%)
  waiting for transfers between devices  4.11 us (8%)
  between operations  0.78 us (2%)
    pallas_call x6, Pallas kernels, call(): pl.pallas_call(functools.partial(kernel, geo), out_shape=out, in_specs=[p...  18.7 us
    all_to_all x1, starting transfers between devices, on_device(): back = lax.all_to_all(products, 'roll', 0, 0, tiled=True)  7.17 us
    ppermute x3, starting transfers between devices, on_device(): lax.ppermute(latent_prefill, 'roll', [(i, (i - width * h) % group) for i...  6.11 us
    ppermute x3, starting transfers between devices, on_device(): lax.ppermute(latent_prefill, 'roll', mates(-1, s))  4.88 us
    all_to_all x1, starting transfers between devices, on_device(): got = lax.all_to_all(reads, 'roll', 0, 0, tiled=True)  4.53 us
    ppermute x3, starting transfers between devices, on_device(): lax.ppermute(chosen[s], 'roll', mates(-1, s))  3.55 us
    ppermute x3, waiting for transfers between devices, on_device(): lax.ppermute(latent_prefill, 'roll', [(i, (i - width * h) % group) for i...  2.94 us
    ppermute x5, starting transfers between devices, on_device(): caches += [lax.ppermute(piece, 'exp', pairs) for piece in taken]  1.09 us
  transfers between devices with their start and end apart: 16, of which 4 were waited for; matrix products, arithmetic and copies ran while one was open for 0% of the time, Pallas kernels for 33%

profile of v5, /device:TPU:0, one launch (start us, length us, event | category | flops | bytes accessed | tf_op | source)
XLA Modules:
  0.0 50.9 jit_solution(3705942389251118647)
XLA Ops:
  0.6 3.1 %collective-permute-start.3 = (bf16[4,32,576]{2,1,0:T(8,128)(2,1)}, bf16[4,32,576]{2,1,0:T(8,128)(2,1)S(1)}, u32[]{:S(2)}, u32[]{:S(2)}) collective-permute-start(bf16[4,32,576]{2,1,0:T(8,128)(2,1)} %own_hbm.1), channel_id=1, source_target_pairs={{0,8},{2,10},{4,12},{6,14},{8,16},{10,18},{12,20},{14,22},{16,24},... | collective-permute-start | bytes 442376 | tf_op jit(solution)/shard_map/ppermute | solution.py:532
  3.7 2.1 %collective-permute-start.4 = (bf16[4,32,576]{2,1,0:T(8,128)(2,1)}, bf16[4,32,576]{2,1,0:T(8,128)(2,1)S(1)}, u32[]{:S(2)}, u32[]{:S(2)}) collective-permute-start(bf16[4,32,576]{2,1,0:T(8,128)(2,1)} %own_hbm.1), channel_id=1, source_target_pairs={{0,24},{2,26},{4,28},{6,30},{8,0},{10,2},{12,4},{14,6},{16,8},{18,... | collective-permute-start | bytes 442376 | tf_op jit(solution)/shard_map/ppermute | solution.py:532
  5.8 0.9 %collective-permute-start.5 = (bf16[4,32,576]{2,1,0:T(8,128)(2,1)}, bf16[4,32,576]{2,1,0:T(8,128)(2,1)S(1)}, u32[]{:S(2)}, u32[]{:S(2)}) collective-permute-start(bf16[4,32,576]{2,1,0:T(8,128)(2,1)} %own_hbm.1), channel_id=1, source_target_pairs={{0,16},{2,18},{4,20},{6,22},{8,24},{10,26},{12,28},{14,30},{16,0},... | collective-permute-start | bytes 442376 | tf_op jit(solution)/shard_map/ppermute | solution.py:532
  6.7 2.4 %collective-permute-start = (bf16[4,32,576]{2,1,0:T(8,128)(2,1)}, bf16[4,32,576]{2,1,0:T(8,128)(2,1)}, u32[]{:S(2)}, u32[]{:S(2)}) collective-permute-start(bf16[4,32,576]{2,1,0:T(8,128)(2,1)} %own_hbm.1), channel_id=1, source_target_pairs={{0,6},{2,0},{4,2},{6,4},{8,14},{10,8},{12,10},{14,12},{16,22},{18,... | collective-permute-start | bytes 442376 | tf_op jit(solution)/shard_map/ppermute | solution.py:530
  9.2 0.5 collective-permute-start.1
  9.7 3.1 %reads_kernel.1 = (bf16[256,512]{1,0:T(8,128)(2,1)}, f32[2,32,2048]{2,1,0:T(8,128)S(1)}, s32[32]{0:T(128)S(1)}) custom-call(bf16[2,32,2048]{2,1,0:T(8,128)(2,1)} %q_hbm.1, bf16[2,32,2048]{2,1,0:T(8,128)(2,1)} %k_hbm.1, f32[2,32,2048]{2,1,0:T(8,128)} %g_hbm.1, bf16[2,32,2048]{2,1,0:T(8,128)(2,1)} %v_hbm.1, f32[2,16,32]{2,1,0:T(8,128)} %bitcast.13, ...), custom_call_target="tpu_custom_call" | custom-call | tf_op jit(solution)/shard_map/reads_kernel/pallas_call | solution.py:423
  12.8 4.5 %all-to-all-start = ((bf16[16,16,512]{2,1,0:T(8,128)(2,1)}), bf16[16,16,512]{2,1,0:T(8,128)(2,1)}, u32[]{:S(2)}, u32[]{:S(2)}) async-start(bf16[16,16,512]{2,1,0:T(8,128)(2,1)} %bitcast.2), calls=%async_computation | async-start | bytes 524288 | tf_op jit(solution)/shard_map/all_to_all | solution.py:528
  17.4 0.0 collective-permute-done.3.refs_0_
  17.4 1.9 %collective-permute-start.2 = (bf16[4,32,576]{2,1,0:T(8,128)(2,1)}, bf16[4,32,576]{2,1,0:T(8,128)(2,1)}, u32[]{:S(2)}, u32[]{:S(2)}) collective-permute-start(bf16[4,32,576]{2,1,0:T(8,128)(2,1)} %own_hbm.1), channel_id=1, source_target_pairs={{0,2},{2,4},{4,6},{6,0},{8,10},{10,12},{12,14},{14,8},{16,18},{18,... | collective-permute-start | bytes 442376 | tf_op jit(solution)/shard_map/ppermute | solution.py:530
  19.3 0.0 collective-permute-done.4.refs_1_
  19.3 2.9 %collective-permute-done.5.refs_2_ = bf16[4,32,576]{2,1,0:T(8,128)(2,1)S(1)} collective-permute-done((bf16[4,32,576]{2,1,0:T(8,128)(2,1)}, bf16[4,32,576]{2,1,0:T(8,128)(2,1)S(1)}, u32[]{:S(2)}, u32[]{:S(2)}) %collective-permute-start.5) | collective-permute-done | bytes 147488 | tf_op jit(solution)/shard_map/ppermute | solution.py:532
  22.2 1.5 %select_kernel.1 = (bf16[192,640]{1,0:T(8,128)(2,1)S(1)}, bf16[192,640]{1,0:T(8,128)(2,1)}, bf16[192,640]{1,0:T(8,128)(2,1)}, bf16[192,640]{1,0:T(8,128)(2,1)}) custom-call(s32[32]{0:T(128)S(1)} %get-tuple-element.18.table_ref, bf16[256,512]{1,0:T(8,128)(2,1)} %get-tuple-element.19._, bf16[4,32,576]{2,1,0:T(8,128)(2,1)S(1)} %collective-permute-done.3.refs_0_, ...), custom_call_target="tpu_custom_call" | custom-call | flops 40000000000 | bytes 60000000 | tf_op jit(solution)/shard_map/select_kernel/pallas_call | solution.py:423
  23.7 0.0 copy-start.1
  23.7 2.4 %collective-permute-start.6 = (bf16[192,640]{1,0:T(8,128)(2,1)}, bf16[192,640]{1,0:T(8,128)(2,1)}, u32[]{:S(2)}, u32[]{:S(2)}) collective-permute-start(bf16[192,640]{1,0:T(8,128)(2,1)} %get-tuple-element.21.refs_4_), channel_id=1, source_target_pairs={{0,6},{2,0},{4,2},{6,4},{8,14},{10,8},{12,10},{14,12},{16,22},{18,... | collective-permute-start | bytes 737288 | tf_op jit(solution)/shard_map/ppermute | solution.py:597
  26.1 0.5 collective-permute-start.7
  26.7 0.0 collective-permute-done.refs_0_
  26.7 0.6 %collective-permute-start.8 = (bf16[192,640]{1,0:T(8,128)(2,1)}, bf16[192,640]{1,0:T(8,128)(2,1)}, u32[]{:S(2)}, u32[]{:S(2)}) collective-permute-start(bf16[192,640]{1,0:T(8,128)(2,1)} %get-tuple-element.23.refs_6_), channel_id=1, source_target_pairs={{0,2},{2,4},{4,6},{6,0},{8,10},{10,12},{12,14},{14,8},{16,18},{18,... | collective-permute-start | bytes 737288 | tf_op jit(solution)/shard_map/ppermute | solution.py:597
  27.3 0.0 collective-permute-done.1.refs_1_
  27.3 0.0 collective-permute-done.2.refs_2_
  27.3 0.1 all-to-all-done
  27.4 3.8 %state_kernel.1 = (bf16[256,512]{1,0:T(8,128)(2,1)}, bf16[256,640]{1,0:T(8,128)(2,1)}) custom-call(s32[32]{0:T(128)S(1)} %get-tuple-element.18.table_ref, bf16[4,16,128,128]{3,2,1,0:T(8,128)(2,1)} %s_hbm.1, s32[4,16]{1,0:T(4,128)} %bitcast.15, bf16[4,32,576]{2,1,0:T(8,128)(2,1)} %own_hbm.1, bf16[4,32,576]{2,1,0:T(8,128)(2,1)} %collective-permute-done.refs_0_, ...), custom_call_target="tpu_custom_call" | custom-call | flops 40000000000 | bytes 60000000 | tf_op jit(solution)/shard_map/state_kernel/pallas_call | solution.py:423
  31.1 0.0 copy-done.1
  31.2 0.1 collective-permute-start.13
  31.2 7.2 %all-to-all-start.1 = ((bf16[16,16,512]{2,1,0:T(8,128)(2,1)}), bf16[16,16,512]{2,1,0:T(8,128)(2,1)}, u32[]{:S(2)}, u32[]{:S(2)}) async-start(bf16[16,16,512]{2,1,0:T(8,128)(2,1)} %bitcast.9), calls=%async_computation.1 | async-start | bytes 524288 | tf_op jit(solution)/shard_map/all_to_all | solution.py:596
  38.4 0.0 collective-permute-done.6.refs_2_
  38.4 0.6 %collective-permute-done.7.refs_3_ = bf16[192,640]{1,0:T(8,128)(2,1)} collective-permute-done((bf16[192,640]{1,0:T(8,128)(2,1)}, bf16[192,640]{1,0:T(8,128)(2,1)}, u32[]{:S(2)}, u32[]{:S(2)}) %collective-permute-start.7) | collective-permute-done | bytes 245792 | tf_op jit(solution)/shard_map/ppermute | solution.py:597
  39.1 0.0 collective-permute-done.8.refs_4_
  39.1 0.0 copy-start
  39.1 0.0 collective-permute-start.10
  39.1 0.5 collective-permute-start.11
  39.6 0.1 collective-permute-start.12
  39.7 0.4 collective-permute-start.9
  40.1 2.3 %query_kernel.1 = (bf16[1024,640]{1,0:T(8,128)(2,1)S(1)}, bf16[64,640]{1,0:T(8,128)(2,1)S(1)}, s32[64,128]{1,0:T(8,128)S(1)}) custom-call(bf16[64,9216]{1,0:T(8,128)(2,1)} %bitcast.10, bf16[64,576]{1,0:T(8,128)(2,1)} %bitcast.12, s32[4,16]{1,0:T(4,128)} %bitcast.16, s32[64]{0:T(128)} %l_hbm.1, bf16[256,512]{1,0:T(8,128)(2,1)} %get-tuple-element.19._), custom_call_target="tpu_custom_call" | custom-call | tf_op jit(solution)/shard_map/query_kernel/pallas_call | solution.py:423
  42.4 0.0 collective-permute-done.10.refs_6_
  42.4 0.0 collective-permute-done.11.refs_7_
  42.4 0.0 collective-permute-done.12.refs_8_
  42.5 0.0 collective-permute-done.9.refs_5_
  42.5 0.0 collective-permute-done.13.refs_9_
  42.5 0.0 copy-done
  42.5 6.1 %latent_kernel.1._ = bf16[64,2048]{1,0:T(8,128)(2,1)} custom-call(bf16[16,512,128]{2,1,0:T(8,128)(2,1)} %w_hbm.1, bf16[192,640]{1,0:T(8,128)(2,1)} %get-tuple-element.25.refs_0_, bf16[192,640]{1,0:T(8,128)(2,1)} %get-tuple-element.26.refs_1_, bf16[192,640]{1,0:T(8,128)(2,1)} %get-tuple-element.27.refs_2_, bf16[192,640]{1,0:T(8,128)(2,1)} %get-tuple-element.28.refs_3_, ...), custom_call_target="tpu_custom_call" | custom-call | tf_op jit(solution)/shard_map/latent_kernel/pallas_call | solution.py:423
  48.6 0.4 all-to-all-done.1
  49.0 1.9 %kda_out_kernel.1 = bf16[2,32,2048]{2,1,0:T(8,128)(2,1)} custom-call(bf16[64,2048]{1,0:T(8,128)(2,1)} %latent_kernel.1._, bf16[256,512]{1,0:T(8,128)(2,1)} %bitcast.7.y_ref, f32[2,32,2048]{2,1,0:T(8,128)S(1)} %get-tuple-element.33.a_ref), custom_call_target="tpu_custom_call" | custom-call | tf_op jit(solution)/shard_map/kda_out_kernel/pallas_call | solution.py:423
  (1 shorter events, 0.0 us)
Async XLA Ops:
  0.6 16.7 %collective-permute-start.3 = (bf16[4,32,576]{2,1,0:T(8,128)(2,1)}, bf16[4,32,576]{2,1,0:T(8,128)(2,1)S(1)}, u32[]{:S(2)}, u32[]{:S(2)}) collective-permute-start(bf16[4,32,576]{2,1,0:T(8,128)(2,1)} %own_hbm.1), channel_id=1, source_target_pairs={{0,8},{2,10},{4,12},{6,14},{8,16},{10,18},{12,20},{14,22},{16,24},... | collective-permute-start | bytes 442376 | tf_op jit(solution)/shard_map/ppermute | solution.py:532
  3.7 15.6 %collective-permute-start.4 = (bf16[4,32,576]{2,1,0:T(8,128)(2,1)}, bf16[4,32,576]{2,1,0:T(8,128)(2,1)S(1)}, u32[]{:S(2)}, u32[]{:S(2)}) collective-permute-start(bf16[4,32,576]{2,1,0:T(8,128)(2,1)} %own_hbm.1), channel_id=1, source_target_pairs={{0,24},{2,26},{4,28},{6,30},{8,0},{10,2},{12,4},{14,6},{16,8},{18,... | collective-permute-start | bytes 442376 | tf_op jit(solution)/shard_map/ppermute | solution.py:532
  5.8 16.4 %collective-permute-start.5 = (bf16[4,32,576]{2,1,0:T(8,128)(2,1)}, bf16[4,32,576]{2,1,0:T(8,128)(2,1)S(1)}, u32[]{:S(2)}, u32[]{:S(2)}) collective-permute-start(bf16[4,32,576]{2,1,0:T(8,128)(2,1)} %own_hbm.1), channel_id=1, source_target_pairs={{0,16},{2,18},{4,20},{6,22},{8,24},{10,26},{12,28},{14,30},{16,0},... | collective-permute-start | bytes 442376 | tf_op jit(solution)/shard_map/ppermute | solution.py:532
  6.7 19.9 %collective-permute-start = (bf16[4,32,576]{2,1,0:T(8,128)(2,1)}, bf16[4,32,576]{2,1,0:T(8,128)(2,1)}, u32[]{:S(2)}, u32[]{:S(2)}) collective-permute-start(bf16[4,32,576]{2,1,0:T(8,128)(2,1)} %own_hbm.1), channel_id=1, source_target_pairs={{0,6},{2,0},{4,2},{6,4},{8,14},{10,8},{12,10},{14,12},{16,22},{18,... | collective-permute-start | bytes 442376 | tf_op jit(solution)/shard_map/ppermute | solution.py:530
  9.2 18.1 %collective-permute-start.1 = (bf16[4,32,576]{2,1,0:T(8,128)(2,1)}, bf16[4,32,576]{2,1,0:T(8,128)(2,1)}, u32[]{:S(2)}, u32[]{:S(2)}) collective-permute-start(bf16[4,32,576]{2,1,0:T(8,128)(2,1)} %own_hbm.1), channel_id=1, source_target_pairs={{0,4},{2,6},{4,0},{6,2},{8,12},{10,14},{12,8},{14,10},{16,20},{18,... | collective-permute-start | bytes 442376 | tf_op jit(solution)/shard_map/ppermute | solution.py:530
  12.8 14.5 %all-to-all-start = ((bf16[16,16,512]{2,1,0:T(8,128)(2,1)}), bf16[16,16,512]{2,1,0:T(8,128)(2,1)}, u32[]{:S(2)}, u32[]{:S(2)}) async-start(bf16[16,16,512]{2,1,0:T(8,128)(2,1)} %bitcast.2), calls=%async_computation | async-start | bytes 524288 | tf_op jit(solution)/shard_map/all_to_all | solution.py:528
  17.4 9.9 %collective-permute-start.2 = (bf16[4,32,576]{2,1,0:T(8,128)(2,1)}, bf16[4,32,576]{2,1,0:T(8,128)(2,1)}, u32[]{:S(2)}, u32[]{:S(2)}) collective-permute-start(bf16[4,32,576]{2,1,0:T(8,128)(2,1)} %own_hbm.1), channel_id=1, source_target_pairs={{0,2},{2,4},{4,6},{6,0},{8,10},{10,12},{12,14},{14,8},{16,18},{18,... | collective-permute-start | bytes 442376 | tf_op jit(solution)/shard_map/ppermute | solution.py:530
  23.7 7.4 %copy-start.1 = (bf16[192,640]{1,0:T(8,128)(2,1)}, bf16[192,640]{1,0:T(8,128)(2,1)S(1)}, u32[]{:S(2)}) copy-start(bf16[192,640]{1,0:T(8,128)(2,1)S(1)} %get-tuple-element.20.refs_3_.refs_1_) | copy-start | bytes 737284
  23.7 14.7 %collective-permute-start.6 = (bf16[192,640]{1,0:T(8,128)(2,1)}, bf16[192,640]{1,0:T(8,128)(2,1)}, u32[]{:S(2)}, u32[]{:S(2)}) collective-permute-start(bf16[192,640]{1,0:T(8,128)(2,1)} %get-tuple-element.21.refs_4_), channel_id=1, source_target_pairs={{0,6},{2,0},{4,2},{6,4},{8,14},{10,8},{12,10},{14,12},{16,22},{18,... | collective-permute-start | bytes 737288 | tf_op jit(solution)/shard_map/ppermute | solution.py:597
  26.1 12.9 %collective-permute-start.7 = (bf16[192,640]{1,0:T(8,128)(2,1)}, bf16[192,640]{1,0:T(8,128)(2,1)}, u32[]{:S(2)}, u32[]{:S(2)}) collective-permute-start(bf16[192,640]{1,0:T(8,128)(2,1)} %get-tuple-element.22.refs_5_), channel_id=1, source_target_pairs={{0,4},{2,6},{4,0},{6,2},{8,12},{10,14},{12,8},{14,10},{16,20},{18,... | collective-permute-start | bytes 737288 | tf_op jit(solution)/shard_map/ppermute | solution.py:597
  26.7 12.4 %collective-permute-start.8 = (bf16[192,640]{1,0:T(8,128)(2,1)}, bf16[192,640]{1,0:T(8,128)(2,1)}, u32[]{:S(2)}, u32[]{:S(2)}) collective-permute-start(bf16[192,640]{1,0:T(8,128)(2,1)} %get-tuple-element.23.refs_6_), channel_id=1, source_target_pairs={{0,2},{2,4},{4,6},{6,0},{8,10},{10,12},{12,14},{14,8},{16,18},{18,... | collective-permute-start | bytes 737288 | tf_op jit(solution)/shard_map/ppermute | solution.py:597
  31.2 11.3 %collective-permute-start.13 = (bf16[256,640]{1,0:T(8,128)(2,1)}, bf16[256,640]{1,0:T(8,128)(2,1)}, u32[]{:S(2)}, u32[]{:S(2)}) collective-permute-start(bf16[256,640]{1,0:T(8,128)(2,1)} %get-tuple-element.29.refs_4_), channel_id=1, source_target_pairs={{0,1},{1,0},{2,3},{3,2},{4,5},{5,4},{6,7},{7,6},{8,9},{9,8},{10,11... | collective-permute-start | bytes 983048 | tf_op jit(solution)/shard_map/ppermute | solution.py:602
  31.2 17.7 %all-to-all-start.1 = ((bf16[16,16,512]{2,1,0:T(8,128)(2,1)}), bf16[16,16,512]{2,1,0:T(8,128)(2,1)}, u32[]{:S(2)}, u32[]{:S(2)}) async-start(bf16[16,16,512]{2,1,0:T(8,128)(2,1)} %bitcast.9), calls=%async_computation.1 | async-start | bytes 524288 | tf_op jit(solution)/shard_map/all_to_all | solution.py:596
  39.1 3.4 %copy-start = (bf16[256,512]{1,0:T(8,128)(2,1)S(1)}, bf16[256,512]{1,0:T(8,128)(2,1)}, u32[]{:S(2)}) copy-start(bf16[256,512]{1,0:T(8,128)(2,1)} %get-tuple-element.24.refs_0_.refs_10_) | copy-start | bytes 786436
  39.1 3.4 %collective-permute-start.10 = (bf16[192,640]{1,0:T(8,128)(2,1)}, bf16[192,640]{1,0:T(8,128)(2,1)S(1)}, u32[]{:S(2)}, u32[]{:S(2)}) collective-permute-start(bf16[192,640]{1,0:T(8,128)(2,1)} %get-tuple-element.26.refs_1_), channel_id=1, source_target_pairs={{0,1},{1,0},{2,3},{3,2},{4,5},{5,4},{6,7},{7,6},{8,9},{9,8},{10,11... | collective-permute-start | bytes 737288 | tf_op jit(solution)/shard_map/ppermute | solution.py:602
  39.1 3.4 %collective-permute-start.11 = (bf16[192,640]{1,0:T(8,128)(2,1)}, bf16[192,640]{1,0:T(8,128)(2,1)S(1)}, u32[]{:S(2)}, u32[]{:S(2)}) collective-permute-start(bf16[192,640]{1,0:T(8,128)(2,1)} %get-tuple-element.27.refs_2_), channel_id=1, source_target_pairs={{0,1},{1,0},{2,3},{3,2},{4,5},{5,4},{6,7},{7,6},{8,9},{9,8},{10,11... | collective-permute-start | bytes 737288 | tf_op jit(solution)/shard_map/ppermute | solution.py:602
  39.6 2.9 %collective-permute-start.12 = (bf16[192,640]{1,0:T(8,128)(2,1)}, bf16[192,640]{1,0:T(8,128)(2,1)S(1)}, u32[]{:S(2)}, u32[]{:S(2)}) collective-permute-start(bf16[192,640]{1,0:T(8,128)(2,1)} %get-tuple-element.28.refs_3_), channel_id=1, source_target_pairs={{0,1},{1,0},{2,3},{3,2},{4,5},{5,4},{6,7},{7,6},{8,9},{9,8},{10,11... | collective-permute-start | bytes 737288 | tf_op jit(solution)/shard_map/ppermute | solution.py:602
  39.7 2.8 %collective-permute-start.9 = (bf16[192,640]{1,0:T(8,128)(2,1)}, bf16[192,640]{1,0:T(8,128)(2,1)S(1)}, u32[]{:S(2)}, u32[]{:S(2)}) collective-permute-start(bf16[192,640]{1,0:T(8,128)(2,1)} %get-tuple-element.25.refs_0_), channel_id=1, source_target_pairs={{0,1},{1,0},{2,3},{3,2},{4,5},{5,4},{6,7},{7,6},{8,9},{9,8},{10,11... | collective-permute-start | bytes 737288 | tf_op jit(solution)/shard_map/ppermute | solution.py:602

commit v6 on v5

--- a/solution.py
+++ b/solution.py
@@ -229,14 +229,19 @@
     shape = (2 * per * parts, rows)
     part, place = fan_rows(geo, shape, 1, me)
     pick = one_hot((lanes(shape, 0) == part * (2 * per) + place) & (place >= 0))
+    y_all = dot(pick, y_ref[...])
     send = []
     for c in range(parts):
         sl = pl.ds(c * wide, wide)
-        y = dot(pick[2 * c * per : 2 * (c + 1) * per], y_ref[...])
+        y = y_all[2 * c * per : 2 * (c + 1) * per]
         for t in range(2):
             o_ref[t, :, sl] = (y[t * per : (t + 1) * per] + a_ref[t, :, sl]).astype(BF16)
-        send.append(pltpu.make_async_copy(o_ref.at[:, :, sl], o_hbm.at[:, :, sl], sems.at[1 + c]))
-        send[c].start()
+        if c % 2 == 1 or c == parts - 1:
+            at = pl.ds(c // 2 * 2 * wide, (c % 2 + 1) * wide)
+            send.append(
+                pltpu.make_async_copy(o_ref.at[:, :, at], o_hbm.at[:, :, at], sems.at[1 + c])
+            )
+            send[-1].start()
     for copy in send:
         copy.wait()
 

time: 51.4 us -> 51.4 us (level)
  no operation moved by 1% of the time
where the time goes in v6:
time: 51.4 us; the launch traced here: 50.9 us
  starting transfers between devices  27.3 us (53%)
  Pallas kernels  18.7 us (36%)
  waiting for transfers between devices  4.11 us (8%)
  between operations  0.78 us (2%)
    pallas_call x6, Pallas kernels, call(): pl.pallas_call(functools.partial(kernel, geo), out_shape=out, in_specs=[p...  18.7 us
    all_to_all x1, starting transfers between devices, on_device(): back = lax.all_to_all(products, 'roll', 0, 0, tiled=True)  7.17 us
    ppermute x3, starting transfers between devices, on_device(): lax.ppermute(latent_prefill, 'roll', [(i, (i - width * h) % group) for i...  6.11 us
    ppermute x3, starting transfers between devices, on_device(): lax.ppermute(latent_prefill, 'roll', mates(-1, s))  4.88 us
    all_to_all x1, starting transfers between devices, on_device(): got = lax.all_to_all(reads, 'roll', 0, 0, tiled=True)  4.53 us
    ppermute x3, starting transfers between devices, on_device(): lax.ppermute(chosen[s], 'roll', mates(-1, s))  3.55 us
    ppermute x3, waiting for transfers between devices, on_device(): lax.ppermute(latent_prefill, 'roll', [(i, (i - width * h) % group) for i...  2.94 us
    ppermute x5, starting transfers between devices, on_device(): caches += [lax.ppermute(piece, 'exp', pairs) for piece in taken]  1.09 us
  transfers between devices with their start and end apart: 16, of which 4 were waited for; matrix products, arithmetic and copies ran while one was open for 0% of the time, Pallas kernels for 33%

profile of v6, /device:TPU:0, one launch (start us, length us, event | category | flops | bytes accessed | tf_op | source)
XLA Modules:
  0.0 50.9 jit_solution(3438717294953902683)
XLA Ops:
  0.6 3.1 %collective-permute-start.3 = (bf16[4,32,576]{2,1,0:T(8,128)(2,1)}, bf16[4,32,576]{2,1,0:T(8,128)(2,1)S(1)}, u32[]{:S(2)}, u32[]{:S(2)}) collective-permute-start(bf16[4,32,576]{2,1,0:T(8,128)(2,1)} %own_hbm.1), channel_id=1, source_target_pairs={{0,8},{2,10},{4,12},{6,14},{8,16},{10,18},{12,20},{14,22},{16,24},... | collective-permute-start | bytes 442376 | tf_op jit(solution)/shard_map/ppermute | solution.py:537
  3.7 2.1 %collective-permute-start.4 = (bf16[4,32,576]{2,1,0:T(8,128)(2,1)}, bf16[4,32,576]{2,1,0:T(8,128)(2,1)S(1)}, u32[]{:S(2)}, u32[]{:S(2)}) collective-permute-start(bf16[4,32,576]{2,1,0:T(8,128)(2,1)} %own_hbm.1), channel_id=1, source_target_pairs={{0,24},{2,26},{4,28},{6,30},{8,0},{10,2},{12,4},{14,6},{16,8},{18,... | collective-permute-start | bytes 442376 | tf_op jit(solution)/shard_map/ppermute | solution.py:537
  5.8 0.9 %collective-permute-start.5 = (bf16[4,32,576]{2,1,0:T(8,128)(2,1)}, bf16[4,32,576]{2,1,0:T(8,128)(2,1)S(1)}, u32[]{:S(2)}, u32[]{:S(2)}) collective-permute-start(bf16[4,32,576]{2,1,0:T(8,128)(2,1)} %own_hbm.1), channel_id=1, source_target_pairs={{0,16},{2,18},{4,20},{6,22},{8,24},{10,26},{12,28},{14,30},{16,0},... | collective-permute-start | bytes 442376 | tf_op jit(solution)/shard_map/ppermute | solution.py:537
  6.7 2.4 %collective-permute-start = (bf16[4,32,576]{2,1,0:T(8,128)(2,1)}, bf16[4,32,576]{2,1,0:T(8,128)(2,1)}, u32[]{:S(2)}, u32[]{:S(2)}) collective-permute-start(bf16[4,32,576]{2,1,0:T(8,128)(2,1)} %own_hbm.1), channel_id=1, source_target_pairs={{0,6},{2,0},{4,2},{6,4},{8,14},{10,8},{12,10},{14,12},{16,22},{18,... | collective-permute-start | bytes 442376 | tf_op jit(solution)/shard_map/ppermute | solution.py:535
  9.2 0.5 collective-permute-start.1
  9.7 3.1 %reads_kernel.1 = (bf16[256,512]{1,0:T(8,128)(2,1)}, f32[2,32,2048]{2,1,0:T(8,128)S(1)}, s32[32]{0:T(128)S(1)}) custom-call(bf16[2,32,2048]{2,1,0:T(8,128)(2,1)} %q_hbm.1, bf16[2,32,2048]{2,1,0:T(8,128)(2,1)} %k_hbm.1, f32[2,32,2048]{2,1,0:T(8,128)} %g_hbm.1, bf16[2,32,2048]{2,1,0:T(8,128)(2,1)} %v_hbm.1, f32[2,16,32]{2,1,0:T(8,128)} %bitcast.13, ...), custom_call_target="tpu_custom_call" | custom-call | tf_op jit(solution)/shard_map/reads_kernel/pallas_call | solution.py:428
  12.8 4.5 %all-to-all-start = ((bf16[16,16,512]{2,1,0:T(8,128)(2,1)}), bf16[16,16,512]{2,1,0:T(8,128)(2,1)}, u32[]{:S(2)}, u32[]{:S(2)}) async-start(bf16[16,16,512]{2,1,0:T(8,128)(2,1)} %bitcast.2), calls=%async_computation | async-start | bytes 524288 | tf_op jit(solution)/shard_map/all_to_all | solution.py:533
  17.4 0.0 collective-permute-done.3.refs_0_
  17.4 1.9 %collective-permute-start.2 = (bf16[4,32,576]{2,1,0:T(8,128)(2,1)}, bf16[4,32,576]{2,1,0:T(8,128)(2,1)}, u32[]{:S(2)}, u32[]{:S(2)}) collective-permute-start(bf16[4,32,576]{2,1,0:T(8,128)(2,1)} %own_hbm.1), channel_id=1, source_target_pairs={{0,2},{2,4},{4,6},{6,0},{8,10},{10,12},{12,14},{14,8},{16,18},{18,... | collective-permute-start | bytes 442376 | tf_op jit(solution)/shard_map/ppermute | solution.py:535
  19.3 0.0 collective-permute-done.4.refs_1_
  19.3 2.9 %collective-permute-done.5.refs_2_ = bf16[4,32,576]{2,1,0:T(8,128)(2,1)S(1)} collective-permute-done((bf16[4,32,576]{2,1,0:T(8,128)(2,1)}, bf16[4,32,576]{2,1,0:T(8,128)(2,1)S(1)}, u32[]{:S(2)}, u32[]{:S(2)}) %collective-permute-start.5) | collective-permute-done | bytes 147488 | tf_op jit(solution)/shard_map/ppermute | solution.py:537
  22.2 1.5 %select_kernel.1 = (bf16[192,640]{1,0:T(8,128)(2,1)S(1)}, bf16[192,640]{1,0:T(8,128)(2,1)}, bf16[192,640]{1,0:T(8,128)(2,1)}, bf16[192,640]{1,0:T(8,128)(2,1)}) custom-call(s32[32]{0:T(128)S(1)} %get-tuple-element.18.table_ref, bf16[256,512]{1,0:T(8,128)(2,1)} %get-tuple-element.19._, bf16[4,32,576]{2,1,0:T(8,128)(2,1)S(1)} %collective-permute-done.3.refs_0_, ...), custom_call_target="tpu_custom_call" | custom-call | flops 40000000000 | bytes 60000000 | tf_op jit(solution)/shard_map/select_kernel/pallas_call | solution.py:428
  23.7 0.0 copy-start.1
  23.7 2.4 %collective-permute-start.6 = (bf16[192,640]{1,0:T(8,128)(2,1)}, bf16[192,640]{1,0:T(8,128)(2,1)}, u32[]{:S(2)}, u32[]{:S(2)}) collective-permute-start(bf16[192,640]{1,0:T(8,128)(2,1)} %get-tuple-element.21.refs_4_), channel_id=1, source_target_pairs={{0,6},{2,0},{4,2},{6,4},{8,14},{10,8},{12,10},{14,12},{16,22},{18,... | collective-permute-start | bytes 737288 | tf_op jit(solution)/shard_map/ppermute | solution.py:602
  26.1 0.5 collective-permute-start.7
  26.7 0.0 collective-permute-done.refs_0_
  26.7 0.6 %collective-permute-start.8 = (bf16[192,640]{1,0:T(8,128)(2,1)}, bf16[192,640]{1,0:T(8,128)(2,1)}, u32[]{:S(2)}, u32[]{:S(2)}) collective-permute-start(bf16[192,640]{1,0:T(8,128)(2,1)} %get-tuple-element.23.refs_6_), channel_id=1, source_target_pairs={{0,2},{2,4},{4,6},{6,0},{8,10},{10,12},{12,14},{14,8},{16,18},{18,... | collective-permute-start | bytes 737288 | tf_op jit(solution)/shard_map/ppermute | solution.py:602
  27.3 0.0 collective-permute-done.1.refs_1_
  27.3 0.0 collective-permute-done.2.refs_2_
  27.3 0.1 all-to-all-done
  27.4 3.8 %state_kernel.1 = (bf16[256,512]{1,0:T(8,128)(2,1)}, bf16[256,640]{1,0:T(8,128)(2,1)}) custom-call(s32[32]{0:T(128)S(1)} %get-tuple-element.18.table_ref, bf16[4,16,128,128]{3,2,1,0:T(8,128)(2,1)} %s_hbm.1, s32[4,16]{1,0:T(4,128)} %bitcast.15, bf16[4,32,576]{2,1,0:T(8,128)(2,1)} %own_hbm.1, bf16[4,32,576]{2,1,0:T(8,128)(2,1)} %collective-permute-done.refs_0_, ...), custom_call_target="tpu_custom_call" | custom-call | flops 40000000000 | bytes 60000000 | tf_op jit(solution)/shard_map/state_kernel/pallas_call | solution.py:428
  31.1 0.0 copy-done.1
  31.2 0.1 collective-permute-start.13
  31.2 7.2 %all-to-all-start.1 = ((bf16[16,16,512]{2,1,0:T(8,128)(2,1)}), bf16[16,16,512]{2,1,0:T(8,128)(2,1)}, u32[]{:S(2)}, u32[]{:S(2)}) async-start(bf16[16,16,512]{2,1,0:T(8,128)(2,1)} %bitcast.9), calls=%async_computation.1 | async-start | bytes 524288 | tf_op jit(solution)/shard_map/all_to_all | solution.py:601
  38.4 0.0 collective-permute-done.6.refs_2_
  38.4 0.6 %collective-permute-done.7.refs_3_ = bf16[192,640]{1,0:T(8,128)(2,1)} collective-permute-done((bf16[192,640]{1,0:T(8,128)(2,1)}, bf16[192,640]{1,0:T(8,128)(2,1)}, u32[]{:S(2)}, u32[]{:S(2)}) %collective-permute-start.7) | collective-permute-done | bytes 245792 | tf_op jit(solution)/shard_map/ppermute | solution.py:602
  39.1 0.0 collective-permute-done.8.refs_4_
  39.1 0.0 copy-start
  39.1 0.0 collective-permute-start.10
  39.1 0.5 collective-permute-start.11
  39.6 0.1 collective-permute-start.12
  39.7 0.4 collective-permute-start.9
  40.1 2.3 %query_kernel.1 = (bf16[1024,640]{1,0:T(8,128)(2,1)S(1)}, bf16[64,640]{1,0:T(8,128)(2,1)S(1)}, s32[64,128]{1,0:T(8,128)S(1)}) custom-call(bf16[64,9216]{1,0:T(8,128)(2,1)} %bitcast.10, bf16[64,576]{1,0:T(8,128)(2,1)} %bitcast.12, s32[4,16]{1,0:T(4,128)} %bitcast.16, s32[64]{0:T(128)} %l_hbm.1, bf16[256,512]{1,0:T(8,128)(2,1)} %get-tuple-element.19._), custom_call_target="tpu_custom_call" | custom-call | tf_op jit(solution)/shard_map/query_kernel/pallas_call | solution.py:428
  42.4 0.0 collective-permute-done.10.refs_6_
  42.4 0.0 collective-permute-done.11.refs_7_
  42.4 0.0 collective-permute-done.12.refs_8_
  42.5 0.0 collective-permute-done.9.refs_5_
  42.5 0.0 collective-permute-done.13.refs_9_
  42.5 0.0 copy-done
  42.5 6.1 %latent_kernel.1._ = bf16[64,2048]{1,0:T(8,128)(2,1)} custom-call(bf16[16,512,128]{2,1,0:T(8,128)(2,1)} %w_hbm.1, bf16[192,640]{1,0:T(8,128)(2,1)} %get-tuple-element.25.refs_0_, bf16[192,640]{1,0:T(8,128)(2,1)} %get-tuple-element.26.refs_1_, bf16[192,640]{1,0:T(8,128)(2,1)} %get-tuple-element.27.refs_2_, bf16[192,640]{1,0:T(8,128)(2,1)} %get-tuple-element.28.refs_3_, ...), custom_call_target="tpu_custom_call" | custom-call | tf_op jit(solution)/shard_map/latent_kernel/pallas_call | solution.py:428
  48.6 0.4 all-to-all-done.1
  49.0 1.9 %kda_out_kernel.1 = bf16[2,32,2048]{2,1,0:T(8,128)(2,1)} custom-call(bf16[64,2048]{1,0:T(8,128)(2,1)} %latent_kernel.1._, bf16[256,512]{1,0:T(8,128)(2,1)} %bitcast.7.y_ref, f32[2,32,2048]{2,1,0:T(8,128)S(1)} %get-tuple-element.33.a_ref), custom_call_target="tpu_custom_call" | custom-call | tf_op jit(solution)/shard_map/kda_out_kernel/pallas_call | solution.py:428
  (1 shorter events, 0.0 us)
Async XLA Ops:
  0.6 16.7 %collective-permute-start.3 = (bf16[4,32,576]{2,1,0:T(8,128)(2,1)}, bf16[4,32,576]{2,1,0:T(8,128)(2,1)S(1)}, u32[]{:S(2)}, u32[]{:S(2)}) collective-permute-start(bf16[4,32,576]{2,1,0:T(8,128)(2,1)} %own_hbm.1), channel_id=1, source_target_pairs={{0,8},{2,10},{4,12},{6,14},{8,16},{10,18},{12,20},{14,22},{16,24},... | collective-permute-start | bytes 442376 | tf_op jit(solution)/shard_map/ppermute | solution.py:537
  3.7 15.6 %collective-permute-start.4 = (bf16[4,32,576]{2,1,0:T(8,128)(2,1)}, bf16[4,32,576]{2,1,0:T(8,128)(2,1)S(1)}, u32[]{:S(2)}, u32[]{:S(2)}) collective-permute-start(bf16[4,32,576]{2,1,0:T(8,128)(2,1)} %own_hbm.1), channel_id=1, source_target_pairs={{0,24},{2,26},{4,28},{6,30},{8,0},{10,2},{12,4},{14,6},{16,8},{18,... | collective-permute-start | bytes 442376 | tf_op jit(solution)/shard_map/ppermute | solution.py:537
  5.8 16.4 %collective-permute-start.5 = (bf16[4,32,576]{2,1,0:T(8,128)(2,1)}, bf16[4,32,576]{2,1,0:T(8,128)(2,1)S(1)}, u32[]{:S(2)}, u32[]{:S(2)}) collective-permute-start(bf16[4,32,576]{2,1,0:T(8,128)(2,1)} %own_hbm.1), channel_id=1, source_target_pairs={{0,16},{2,18},{4,20},{6,22},{8,24},{10,26},{12,28},{14,30},{16,0},... | collective-permute-start | bytes 442376 | tf_op jit(solution)/shard_map/ppermute | solution.py:537
  6.7 19.9 %collective-permute-start = (bf16[4,32,576]{2,1,0:T(8,128)(2,1)}, bf16[4,32,576]{2,1,0:T(8,128)(2,1)}, u32[]{:S(2)}, u32[]{:S(2)}) collective-permute-start(bf16[4,32,576]{2,1,0:T(8,128)(2,1)} %own_hbm.1), channel_id=1, source_target_pairs={{0,6},{2,0},{4,2},{6,4},{8,14},{10,8},{12,10},{14,12},{16,22},{18,... | collective-permute-start | bytes 442376 | tf_op jit(solution)/shard_map/ppermute | solution.py:535
  9.2 18.1 %collective-permute-start.1 = (bf16[4,32,576]{2,1,0:T(8,128)(2,1)}, bf16[4,32,576]{2,1,0:T(8,128)(2,1)}, u32[]{:S(2)}, u32[]{:S(2)}) collective-permute-start(bf16[4,32,576]{2,1,0:T(8,128)(2,1)} %own_hbm.1), channel_id=1, source_target_pairs={{0,4},{2,6},{4,0},{6,2},{8,12},{10,14},{12,8},{14,10},{16,20},{18,... | collective-permute-start | bytes 442376 | tf_op jit(solution)/shard_map/ppermute | solution.py:535
  12.8 14.5 %all-to-all-start = ((bf16[16,16,512]{2,1,0:T(8,128)(2,1)}), bf16[16,16,512]{2,1,0:T(8,128)(2,1)}, u32[]{:S(2)}, u32[]{:S(2)}) async-start(bf16[16,16,512]{2,1,0:T(8,128)(2,1)} %bitcast.2), calls=%async_computation | async-start | bytes 524288 | tf_op jit(solution)/shard_map/all_to_all | solution.py:533
  17.4 9.9 %collective-permute-start.2 = (bf16[4,32,576]{2,1,0:T(8,128)(2,1)}, bf16[4,32,576]{2,1,0:T(8,128)(2,1)}, u32[]{:S(2)}, u32[]{:S(2)}) collective-permute-start(bf16[4,32,576]{2,1,0:T(8,128)(2,1)} %own_hbm.1), channel_id=1, source_target_pairs={{0,2},{2,4},{4,6},{6,0},{8,10},{10,12},{12,14},{14,8},{16,18},{18,... | collective-permute-start | bytes 442376 | tf_op jit(solution)/shard_map/ppermute | solution.py:535
  23.7 7.4 %copy-start.1 = (bf16[192,640]{1,0:T(8,128)(2,1)}, bf16[192,640]{1,0:T(8,128)(2,1)S(1)}, u32[]{:S(2)}) copy-start(bf16[192,640]{1,0:T(8,128)(2,1)S(1)} %get-tuple-element.20.refs_3_.refs_1_) | copy-start | bytes 737284
  23.7 14.7 %collective-permute-start.6 = (bf16[192,640]{1,0:T(8,128)(2,1)}, bf16[192,640]{1,0:T(8,128)(2,1)}, u32[]{:S(2)}, u32[]{:S(2)}) collective-permute-start(bf16[192,640]{1,0:T(8,128)(2,1)} %get-tuple-element.21.refs_4_), channel_id=1, source_target_pairs={{0,6},{2,0},{4,2},{6,4},{8,14},{10,8},{12,10},{14,12},{16,22},{18,... | collective-permute-start | bytes 737288 | tf_op jit(solution)/shard_map/ppermute | solution.py:602
  26.1 12.9 %collective-permute-start.7 = (bf16[192,640]{1,0:T(8,128)(2,1)}, bf16[192,640]{1,0:T(8,128)(2,1)}, u32[]{:S(2)}, u32[]{:S(2)}) collective-permute-start(bf16[192,640]{1,0:T(8,128)(2,1)} %get-tuple-element.22.refs_5_), channel_id=1, source_target_pairs={{0,4},{2,6},{4,0},{6,2},{8,12},{10,14},{12,8},{14,10},{16,20},{18,... | collective-permute-start | bytes 737288 | tf_op jit(solution)/shard_map/ppermute | solution.py:602
  26.7 12.4 %collective-permute-start.8 = (bf16[192,640]{1,0:T(8,128)(2,1)}, bf16[192,640]{1,0:T(8,128)(2,1)}, u32[]{:S(2)}, u32[]{:S(2)}) collective-permute-start(bf16[192,640]{1,0:T(8,128)(2,1)} %get-tuple-element.23.refs_6_), channel_id=1, source_target_pairs={{0,2},{2,4},{4,6},{6,0},{8,10},{10,12},{12,14},{14,8},{16,18},{18,... | collective-permute-start | bytes 737288 | tf_op jit(solution)/shard_map/ppermute | solution.py:602
  31.2 11.3 %collective-permute-start.13 = (bf16[256,640]{1,0:T(8,128)(2,1)}, bf16[256,640]{1,0:T(8,128)(2,1)}, u32[]{:S(2)}, u32[]{:S(2)}) collective-permute-start(bf16[256,640]{1,0:T(8,128)(2,1)} %get-tuple-element.29.refs_4_), channel_id=1, source_target_pairs={{0,1},{1,0},{2,3},{3,2},{4,5},{5,4},{6,7},{7,6},{8,9},{9,8},{10,11... | collective-permute-start | bytes 983048 | tf_op jit(solution)/shard_map/ppermute | solution.py:607
  31.2 17.7 %all-to-all-start.1 = ((bf16[16,16,512]{2,1,0:T(8,128)(2,1)}), bf16[16,16,512]{2,1,0:T(8,128)(2,1)}, u32[]{:S(2)}, u32[]{:S(2)}) async-start(bf16[16,16,512]{2,1,0:T(8,128)(2,1)} %bitcast.9), calls=%async_computation.1 | async-start | bytes 524288 | tf_op jit(solution)/shard_map/all_to_all | solution.py:601
  39.1 3.4 %copy-start = (bf16[256,512]{1,0:T(8,128)(2,1)S(1)}, bf16[256,512]{1,0:T(8,128)(2,1)}, u32[]{:S(2)}) copy-start(bf16[256,512]{1,0:T(8,128)(2,1)} %get-tuple-element.24.refs_0_.refs_10_) | copy-start | bytes 786436
  39.1 3.4 %collective-permute-start.10 = (bf16[192,640]{1,0:T(8,128)(2,1)}, bf16[192,640]{1,0:T(8,128)(2,1)S(1)}, u32[]{:S(2)}, u32[]{:S(2)}) collective-permute-start(bf16[192,640]{1,0:T(8,128)(2,1)} %get-tuple-element.26.refs_1_), channel_id=1, source_target_pairs={{0,1},{1,0},{2,3},{3,2},{4,5},{5,4},{6,7},{7,6},{8,9},{9,8},{10,11... | collective-permute-start | bytes 737288 | tf_op jit(solution)/shard_map/ppermute | solution.py:607
  39.1 3.4 %collective-permute-start.11 = (bf16[192,640]{1,0:T(8,128)(2,1)}, bf16[192,640]{1,0:T(8,128)(2,1)S(1)}, u32[]{:S(2)}, u32[]{:S(2)}) collective-permute-start(bf16[192,640]{1,0:T(8,128)(2,1)} %get-tuple-element.27.refs_2_), channel_id=1, source_target_pairs={{0,1},{1,0},{2,3},{3,2},{4,5},{5,4},{6,7},{7,6},{8,9},{9,8},{10,11... | collective-permute-start | bytes 737288 | tf_op jit(solution)/shard_map/ppermute | solution.py:607
  39.6 2.9 %collective-permute-start.12 = (bf16[192,640]{1,0:T(8,128)(2,1)}, bf16[192,640]{1,0:T(8,128)(2,1)S(1)}, u32[]{:S(2)}, u32[]{:S(2)}) collective-permute-start(bf16[192,640]{1,0:T(8,128)(2,1)} %get-tuple-element.28.refs_3_), channel_id=1, source_target_pairs={{0,1},{1,0},{2,3},{3,2},{4,5},{5,4},{6,7},{7,6},{8,9},{9,8},{10,11... | collective-permute-start | bytes 737288 | tf_op jit(solution)/shard_map/ppermute | solution.py:607
  39.7 2.8 %collective-permute-start.9 = (bf16[192,640]{1,0:T(8,128)(2,1)}, bf16[192,640]{1,0:T(8,128)(2,1)S(1)}, u32[]{:S(2)}, u32[]{:S(2)}) collective-permute-start(bf16[192,640]{1,0:T(8,128)(2,1)} %get-tuple-element.25.refs_0_), channel_id=1, source_target_pairs={{0,1},{1,0},{2,3},{3,2},{4,5},{5,4},{6,7},{7,6},{8,9},{9,8},{10,11... | collective-permute-start | bytes 737288 | tf_op jit(solution)/shard_map/ppermute | solution.py:607

commit v7 on v6

--- a/solution.py
+++ b/solution.py
@@ -600,7 +600,7 @@
     )
     back = lax.all_to_all(products, "roll", 0, 0, tiled=True)
     taken = [lax.ppermute(chosen[s], "roll", mates(-1, s)) for s in range(1, width)]
-    taken = [*hold([chosen[0], *taken], products), own]
+    taken = [chosen[0], *hold(taken, products), own]
     caches = list(taken)
     for e in range(1, halves):
         pairs = [(i, (i - e) % halves) for i in range(halves)]

time: 51.4 us -> 51.4 us (level)
    all_to_all x1, waiting for transfers between devices: 0.4 us -> 1.02 us  [on_device(): back = lax.all_to_all(products, 'roll', 0, 0, tiled=True)]
  transfers between devices with their start and end apart: 16 -> 16, of which waited for: 4 -> 3; matrix products, arithmetic and copies ran while one was open for 0% -> 0% of each run, Pallas kernels for 33% -> 33%
where the time goes in v7:
time: 51.4 us; the launch traced here: 50.9 us
  starting transfers between devices  27.4 us (53%)
  Pallas kernels  18.6 us (36%)
  waiting for transfers between devices  4.19 us (8%)
  between operations  0.76 us (1%)
    pallas_call x6, Pallas kernels, call(): pl.pallas_call(functools.partial(kernel, geo), out_shape=out, in_specs=[p...  18.6 us
    all_to_all x1, starting transfers between devices, on_device(): back = lax.all_to_all(products, 'roll', 0, 0, tiled=True)  7.25 us
    ppermute x3, starting transfers between devices, on_device(): lax.ppermute(latent_prefill, 'roll', [(i, (i - width * h) % group) for i...  6.11 us
    ppermute x3, starting transfers between devices, on_device(): lax.ppermute(latent_prefill, 'roll', mates(-1, s))  4.88 us
    all_to_all x1, starting transfers between devices, on_device(): got = lax.all_to_all(reads, 'roll', 0, 0, tiled=True)  4.53 us
    ppermute x3, starting transfers between devices, on_device(): lax.ppermute(chosen[s], 'roll', mates(-1, s))  3.55 us
    ppermute x3, waiting for transfers between devices, on_device(): lax.ppermute(latent_prefill, 'roll', [(i, (i - width * h) % group) for i...  2.94 us
    ppermute x5, starting transfers between devices, on_device(): caches += [lax.ppermute(piece, 'exp', pairs) for piece in taken]  1.11 us
  transfers between devices with their start and end apart: 16, of which 3 were waited for; matrix products, arithmetic and copies ran while one was open for 0% of the time, Pallas kernels for 33%

profile of v7, /device:TPU:0, one launch (start us, length us, event | category | flops | bytes accessed | tf_op | source)
XLA Modules:
  0.0 50.9 jit_solution(13028591216994154837)
XLA Ops:
  0.6 3.1 %collective-permute-start = (bf16[4,32,576]{2,1,0:T(8,128)(2,1)}, bf16[4,32,576]{2,1,0:T(8,128)(2,1)S(1)}, u32[]{:S(2)}, u32[]{:S(2)}) collective-permute-start(bf16[4,32,576]{2,1,0:T(8,128)(2,1)} %own_hbm.1), channel_id=1, source_target_pairs={{0,8},{2,10},{4,12},{6,14},{8,16},{10,18},{12,20},{14,22},{16,24},... | collective-permute-start | bytes 442376 | tf_op jit(solution)/shard_map/ppermute | solution.py:537
  3.7 2.1 %collective-permute-start.1 = (bf16[4,32,576]{2,1,0:T(8,128)(2,1)}, bf16[4,32,576]{2,1,0:T(8,128)(2,1)S(1)}, u32[]{:S(2)}, u32[]{:S(2)}) collective-permute-start(bf16[4,32,576]{2,1,0:T(8,128)(2,1)} %own_hbm.1), channel_id=1, source_target_pairs={{0,24},{2,26},{4,28},{6,30},{8,0},{10,2},{12,4},{14,6},{16,8},{18,... | collective-permute-start | bytes 442376 | tf_op jit(solution)/shard_map/ppermute | solution.py:537
  5.8 0.9 %collective-permute-start.2 = (bf16[4,32,576]{2,1,0:T(8,128)(2,1)}, bf16[4,32,576]{2,1,0:T(8,128)(2,1)S(1)}, u32[]{:S(2)}, u32[]{:S(2)}) collective-permute-start(bf16[4,32,576]{2,1,0:T(8,128)(2,1)} %own_hbm.1), channel_id=1, source_target_pairs={{0,16},{2,18},{4,20},{6,22},{8,24},{10,26},{12,28},{14,30},{16,0},... | collective-permute-start | bytes 442376 | tf_op jit(solution)/shard_map/ppermute | solution.py:537
  6.7 2.4 %collective-permute-start.3 = (bf16[4,32,576]{2,1,0:T(8,128)(2,1)}, bf16[4,32,576]{2,1,0:T(8,128)(2,1)}, u32[]{:S(2)}, u32[]{:S(2)}) collective-permute-start(bf16[4,32,576]{2,1,0:T(8,128)(2,1)} %own_hbm.1), channel_id=1, source_target_pairs={{0,6},{2,0},{4,2},{6,4},{8,14},{10,8},{12,10},{14,12},{16,22},{18,... | collective-permute-start | bytes 442376 | tf_op jit(solution)/shard_map/ppermute | solution.py:535
  9.2 0.5 collective-permute-start.4
  9.7 3.1 %reads_kernel.1 = (bf16[256,512]{1,0:T(8,128)(2,1)}, f32[2,32,2048]{2,1,0:T(8,128)S(1)}, s32[32]{0:T(128)S(1)}) custom-call(bf16[2,32,2048]{2,1,0:T(8,128)(2,1)} %q_hbm.1, bf16[2,32,2048]{2,1,0:T(8,128)(2,1)} %k_hbm.1, f32[2,32,2048]{2,1,0:T(8,128)} %g_hbm.1, bf16[2,32,2048]{2,1,0:T(8,128)(2,1)} %v_hbm.1, f32[2,16,32]{2,1,0:T(8,128)} %bitcast.13, ...), custom_call_target="tpu_custom_call" | custom-call | tf_op jit(solution)/shard_map/reads_kernel/pallas_call | solution.py:428
  12.8 4.5 %all-to-all-start = ((bf16[16,16,512]{2,1,0:T(8,128)(2,1)}), bf16[16,16,512]{2,1,0:T(8,128)(2,1)}, u32[]{:S(2)}, u32[]{:S(2)}) async-start(bf16[16,16,512]{2,1,0:T(8,128)(2,1)} %bitcast.2), calls=%async_computation | async-start | bytes 524288 | tf_op jit(solution)/shard_map/all_to_all | solution.py:533
  17.4 0.0 collective-permute-done.refs_0_
  17.4 1.9 %collective-permute-start.5 = (bf16[4,32,576]{2,1,0:T(8,128)(2,1)}, bf16[4,32,576]{2,1,0:T(8,128)(2,1)}, u32[]{:S(2)}, u32[]{:S(2)}) collective-permute-start(bf16[4,32,576]{2,1,0:T(8,128)(2,1)} %own_hbm.1), channel_id=1, source_target_pairs={{0,2},{2,4},{4,6},{6,0},{8,10},{10,12},{12,14},{14,8},{16,18},{18,... | collective-permute-start | bytes 442376 | tf_op jit(solution)/shard_map/ppermute | solution.py:535
  19.3 0.0 collective-permute-done.1.refs_1_
  19.3 2.9 %collective-permute-done.2.refs_2_ = bf16[4,32,576]{2,1,0:T(8,128)(2,1)S(1)} collective-permute-done((bf16[4,32,576]{2,1,0:T(8,128)(2,1)}, bf16[4,32,576]{2,1,0:T(8,128)(2,1)S(1)}, u32[]{:S(2)}, u32[]{:S(2)}) %collective-permute-start.2) | collective-permute-done | bytes 147488 | tf_op jit(solution)/shard_map/ppermute | solution.py:537
  22.2 1.5 %select_kernel.1 = (bf16[192,640]{1,0:T(8,128)(2,1)}, bf16[192,640]{1,0:T(8,128)(2,1)}, bf16[192,640]{1,0:T(8,128)(2,1)}, bf16[192,640]{1,0:T(8,128)(2,1)}) custom-call(s32[32]{0:T(128)S(1)} %get-tuple-element.17.table_ref, bf16[256,512]{1,0:T(8,128)(2,1)} %get-tuple-element.18._, bf16[4,32,576]{2,1,0:T(8,128)(2,1)S(1)} %collective-permute-done.refs_0_, ...), custom_call_target="tpu_custom_call" | custom-call | flops 40000000000 | bytes 60000000 | tf_op jit(solution)/shard_map/select_kernel/pallas_call | solution.py:428
  23.8 2.4 %collective-permute-start.6 = (bf16[192,640]{1,0:T(8,128)(2,1)}, bf16[192,640]{1,0:T(8,128)(2,1)}, u32[]{:S(2)}, u32[]{:S(2)}) collective-permute-start(bf16[192,640]{1,0:T(8,128)(2,1)} %get-tuple-element.20.refs_4_), channel_id=1, source_target_pairs={{0,6},{2,0},{4,2},{6,4},{8,14},{10,8},{12,10},{14,12},{16,22},{18,... | collective-permute-start | bytes 737288 | tf_op jit(solution)/shard_map/ppermute | solution.py:602
  26.2 0.5 collective-permute-start.7
  26.7 0.0 collective-permute-done.3.refs_0_
  26.7 0.6 %collective-permute-start.8 = (bf16[192,640]{1,0:T(8,128)(2,1)}, bf16[192,640]{1,0:T(8,128)(2,1)}, u32[]{:S(2)}, u32[]{:S(2)}) collective-permute-start(bf16[192,640]{1,0:T(8,128)(2,1)} %get-tuple-element.22.refs_6_), channel_id=1, source_target_pairs={{0,2},{2,4},{4,6},{6,0},{8,10},{10,12},{12,14},{14,8},{16,18},{18,... | collective-permute-start | bytes 737288 | tf_op jit(solution)/shard_map/ppermute | solution.py:602
  27.3 0.0 collective-permute-done.4.refs_1_
  27.3 0.0 collective-permute-start.9
  27.3 0.0 collective-permute-done.5.refs_2_
  27.3 0.0 all-to-all-done
  27.4 3.8 %state_kernel.1 = (bf16[256,512]{1,0:T(8,128)(2,1)}, bf16[256,640]{1,0:T(8,128)(2,1)}) custom-call(s32[32]{0:T(128)S(1)} %get-tuple-element.17.table_ref, bf16[4,16,128,128]{3,2,1,0:T(8,128)(2,1)} %s_hbm.1, s32[4,16]{1,0:T(4,128)} %bitcast.15, bf16[4,32,576]{2,1,0:T(8,128)(2,1)} %own_hbm.1, bf16[4,32,576]{2,1,0:T(8,128)(2,1)} %collective-permute-done.3.refs_0_, ...), custom_call_target="tpu_custom_call" | custom-call | flops 40000000000 | bytes 60000000 | tf_op jit(solution)/shard_map/state_kernel/pallas_call | solution.py:428
  31.1 0.5 %collective-permute-start.13 = (bf16[256,640]{1,0:T(8,128)(2,1)}, bf16[256,640]{1,0:T(8,128)(2,1)}, u32[]{:S(2)}, u32[]{:S(2)}) collective-permute-start(bf16[256,640]{1,0:T(8,128)(2,1)} %get-tuple-element.27.refs_4_), channel_id=1, source_target_pairs={{0,1},{1,0},{2,3},{3,2},{4,5},{5,4},{6,7},{7,6},{8,9},{9,8},{10,11... | collective-permute-start | bytes 983048 | tf_op jit(solution)/shard_map/ppermute | solution.py:607
  31.7 7.3 %all-to-all-start.1 = ((bf16[16,16,512]{2,1,0:T(8,128)(2,1)}), bf16[16,16,512]{2,1,0:T(8,128)(2,1)}, u32[]{:S(2)}, u32[]{:S(2)}) async-start(bf16[16,16,512]{2,1,0:T(8,128)(2,1)} %bitcast.9), calls=%async_computation.1 | async-start | bytes 524288 | tf_op jit(solution)/shard_map/all_to_all | solution.py:601
  38.9 0.0 collective-permute-done.6.refs_1_
  39.0 0.2 collective-permute-done.7.refs_2_
  39.1 0.0 collective-permute-done.8.refs_3_
  39.1 0.0 copy-start
  39.1 0.0 collective-permute-start.10
  39.1 0.5 collective-permute-start.11
  39.6 0.1 collective-permute-start.12
  39.7 2.3 %query_kernel.1 = (bf16[1024,640]{1,0:T(8,128)(2,1)S(1)}, bf16[64,640]{1,0:T(8,128)(2,1)S(1)}, s32[64,128]{1,0:T(8,128)S(1)}) custom-call(bf16[64,9216]{1,0:T(8,128)(2,1)} %bitcast.10, bf16[64,576]{1,0:T(8,128)(2,1)} %bitcast.12, s32[4,16]{1,0:T(4,128)} %bitcast.16, s32[64]{0:T(128)} %l_hbm.1, bf16[256,512]{1,0:T(8,128)(2,1)} %get-tuple-element.18._), custom_call_target="tpu_custom_call" | custom-call | tf_op jit(solution)/shard_map/query_kernel/pallas_call | solution.py:428
  42.0 0.0 collective-permute-done.9.refs_5_
  42.1 0.0 collective-permute-done.10.refs_6_
  42.1 0.0 collective-permute-done.11.refs_7_
  42.1 0.0 collective-permute-done.12.refs_8_
  42.1 0.0 collective-permute-done.13.refs_9_
  42.1 0.0 copy-done
  42.1 5.9 %latent_kernel.1._ = bf16[64,2048]{1,0:T(8,128)(2,1)} custom-call(bf16[16,512,128]{2,1,0:T(8,128)(2,1)} %w_hbm.1, bf16[192,640]{1,0:T(8,128)(2,1)} %get-tuple-element.19.refs_3_.refs_0_, bf16[192,640]{1,0:T(8,128)(2,1)} %get-tuple-element.24.refs_1_, bf16[192,640]{1,0:T(8,128)(2,1)} %get-tuple-element.25.refs_2_, ...), custom_call_target="tpu_custom_call" | custom-call | tf_op jit(solution)/shard_map/latent_kernel/pallas_call | solution.py:428
  48.0 1.0 %all-to-all-done.1 = bf16[16,16,512]{2,1,0:T(8,128)(2,1)} async-done(((bf16[16,16,512]{2,1,0:T(8,128)(2,1)}), bf16[16,16,512]{2,1,0:T(8,128)(2,1)}, u32[]{:S(2)}, u32[]{:S(2)}) %all-to-all-start.1) | async-done | bytes 262176 | tf_op jit(solution)/shard_map/all_to_all | solution.py:601
  49.1 1.9 %kda_out_kernel.1 = bf16[2,32,2048]{2,1,0:T(8,128)(2,1)} custom-call(bf16[64,2048]{1,0:T(8,128)(2,1)} %latent_kernel.1._, bf16[256,512]{1,0:T(8,128)(2,1)} %bitcast.7.y_ref, f32[2,32,2048]{2,1,0:T(8,128)S(1)} %get-tuple-element.31.a_ref), custom_call_target="tpu_custom_call" | custom-call | tf_op jit(solution)/shard_map/kda_out_kernel/pallas_call | solution.py:428
  (1 shorter events, 0.0 us)
Async XLA Ops:
  0.6 16.7 %collective-permute-start = (bf16[4,32,576]{2,1,0:T(8,128)(2,1)}, bf16[4,32,576]{2,1,0:T(8,128)(2,1)S(1)}, u32[]{:S(2)}, u32[]{:S(2)}) collective-permute-start(bf16[4,32,576]{2,1,0:T(8,128)(2,1)} %own_hbm.1), channel_id=1, source_target_pairs={{0,8},{2,10},{4,12},{6,14},{8,16},{10,18},{12,20},{14,22},{16,24},... | collective-permute-start | bytes 442376 | tf_op jit(solution)/shard_map/ppermute | solution.py:537
  3.7 15.6 %collective-permute-start.1 = (bf16[4,32,576]{2,1,0:T(8,128)(2,1)}, bf16[4,32,576]{2,1,0:T(8,128)(2,1)S(1)}, u32[]{:S(2)}, u32[]{:S(2)}) collective-permute-start(bf16[4,32,576]{2,1,0:T(8,128)(2,1)} %own_hbm.1), channel_id=1, source_target_pairs={{0,24},{2,26},{4,28},{6,30},{8,0},{10,2},{12,4},{14,6},{16,8},{18,... | collective-permute-start | bytes 442376 | tf_op jit(solution)/shard_map/ppermute | solution.py:537
  5.8 16.4 %collective-permute-start.2 = (bf16[4,32,576]{2,1,0:T(8,128)(2,1)}, bf16[4,32,576]{2,1,0:T(8,128)(2,1)S(1)}, u32[]{:S(2)}, u32[]{:S(2)}) collective-permute-start(bf16[4,32,576]{2,1,0:T(8,128)(2,1)} %own_hbm.1), channel_id=1, source_target_pairs={{0,16},{2,18},{4,20},{6,22},{8,24},{10,26},{12,28},{14,30},{16,0},... | collective-permute-start | bytes 442376 | tf_op jit(solution)/shard_map/ppermute | solution.py:537
  6.7 20.0 %collective-permute-start.3 = (bf16[4,32,576]{2,1,0:T(8,128)(2,1)}, bf16[4,32,576]{2,1,0:T(8,128)(2,1)}, u32[]{:S(2)}, u32[]{:S(2)}) collective-permute-start(bf16[4,32,576]{2,1,0:T(8,128)(2,1)} %own_hbm.1), channel_id=1, source_target_pairs={{0,6},{2,0},{4,2},{6,4},{8,14},{10,8},{12,10},{14,12},{16,22},{18,... | collective-permute-start | bytes 442376 | tf_op jit(solution)/shard_map/ppermute | solution.py:535
  9.2 18.1 %collective-permute-start.4 = (bf16[4,32,576]{2,1,0:T(8,128)(2,1)}, bf16[4,32,576]{2,1,0:T(8,128)(2,1)}, u32[]{:S(2)}, u32[]{:S(2)}) collective-permute-start(bf16[4,32,576]{2,1,0:T(8,128)(2,1)} %own_hbm.1), channel_id=1, source_target_pairs={{0,4},{2,6},{4,0},{6,2},{8,12},{10,14},{12,8},{14,10},{16,20},{18,... | collective-permute-start | bytes 442376 | tf_op jit(solution)/shard_map/ppermute | solution.py:535
  12.8 14.5 %all-to-all-start = ((bf16[16,16,512]{2,1,0:T(8,128)(2,1)}), bf16[16,16,512]{2,1,0:T(8,128)(2,1)}, u32[]{:S(2)}, u32[]{:S(2)}) async-start(bf16[16,16,512]{2,1,0:T(8,128)(2,1)} %bitcast.2), calls=%async_computation | async-start | bytes 524288 | tf_op jit(solution)/shard_map/all_to_all | solution.py:533
  17.4 10.0 %collective-permute-start.5 = (bf16[4,32,576]{2,1,0:T(8,128)(2,1)}, bf16[4,32,576]{2,1,0:T(8,128)(2,1)}, u32[]{:S(2)}, u32[]{:S(2)}) collective-permute-start(bf16[4,32,576]{2,1,0:T(8,128)(2,1)} %own_hbm.1), channel_id=1, source_target_pairs={{0,2},{2,4},{4,6},{6,0},{8,10},{10,12},{12,14},{14,8},{16,18},{18,... | collective-permute-start | bytes 442376 | tf_op jit(solution)/shard_map/ppermute | solution.py:535
  23.8 15.2 %collective-permute-start.6 = (bf16[192,640]{1,0:T(8,128)(2,1)}, bf16[192,640]{1,0:T(8,128)(2,1)}, u32[]{:S(2)}, u32[]{:S(2)}) collective-permute-start(bf16[192,640]{1,0:T(8,128)(2,1)} %get-tuple-element.20.refs_4_), channel_id=1, source_target_pairs={{0,6},{2,0},{4,2},{6,4},{8,14},{10,8},{12,10},{14,12},{16,22},{18,... | collective-permute-start | bytes 737288 | tf_op jit(solution)/shard_map/ppermute | solution.py:602
  26.2 12.9 %collective-permute-start.7 = (bf16[192,640]{1,0:T(8,128)(2,1)}, bf16[192,640]{1,0:T(8,128)(2,1)}, u32[]{:S(2)}, u32[]{:S(2)}) collective-permute-start(bf16[192,640]{1,0:T(8,128)(2,1)} %get-tuple-element.21.refs_5_), channel_id=1, source_target_pairs={{0,4},{2,6},{4,0},{6,2},{8,12},{10,14},{12,8},{14,10},{16,20},{18,... | collective-permute-start | bytes 737288 | tf_op jit(solution)/shard_map/ppermute | solution.py:602
  26.7 12.4 %collective-permute-start.8 = (bf16[192,640]{1,0:T(8,128)(2,1)}, bf16[192,640]{1,0:T(8,128)(2,1)}, u32[]{:S(2)}, u32[]{:S(2)}) collective-permute-start(bf16[192,640]{1,0:T(8,128)(2,1)} %get-tuple-element.22.refs_6_), channel_id=1, source_target_pairs={{0,2},{2,4},{4,6},{6,0},{8,10},{10,12},{12,14},{14,8},{16,18},{18,... | collective-permute-start | bytes 737288 | tf_op jit(solution)/shard_map/ppermute | solution.py:602
  27.3 14.7 %collective-permute-start.9 = (bf16[192,640]{1,0:T(8,128)(2,1)}, bf16[192,640]{1,0:T(8,128)(2,1)}, u32[]{:S(2)}, u32[]{:S(2)}) collective-permute-start(bf16[192,640]{1,0:T(8,128)(2,1)} %get-tuple-element.19.refs_3_.refs_0_), channel_id=1, source_target_pairs={{0,1},{1,0},{2,3},{3,2},{4,5},{5,4},{6,7},{7,6},{8,9},{9,8},{10,11... | collective-permute-start | bytes 737288 | tf_op jit(solution)/shard_map/ppermute | solution.py:607
  31.1 10.9 %collective-permute-start.13 = (bf16[256,640]{1,0:T(8,128)(2,1)}, bf16[256,640]{1,0:T(8,128)(2,1)}, u32[]{:S(2)}, u32[]{:S(2)}) collective-permute-start(bf16[256,640]{1,0:T(8,128)(2,1)} %get-tuple-element.27.refs_4_), channel_id=1, source_target_pairs={{0,1},{1,0},{2,3},{3,2},{4,5},{5,4},{6,7},{7,6},{8,9},{9,8},{10,11... | collective-permute-start | bytes 983048 | tf_op jit(solution)/shard_map/ppermute | solution.py:607
  31.7 17.4 %all-to-all-start.1 = ((bf16[16,16,512]{2,1,0:T(8,128)(2,1)}), bf16[16,16,512]{2,1,0:T(8,128)(2,1)}, u32[]{:S(2)}, u32[]{:S(2)}) async-start(bf16[16,16,512]{2,1,0:T(8,128)(2,1)} %bitcast.9), calls=%async_computation.1 | async-start | bytes 524288 | tf_op jit(solution)/shard_map/all_to_all | solution.py:601
  39.1 3.0 %copy-start = (bf16[256,512]{1,0:T(8,128)(2,1)S(1)}, bf16[256,512]{1,0:T(8,128)(2,1)}, u32[]{:S(2)}) copy-start(bf16[256,512]{1,0:T(8,128)(2,1)} %get-tuple-element.23.refs_0_.refs_10_) | copy-start | bytes 786436
  39.1 2.9 %collective-permute-start.10 = (bf16[192,640]{1,0:T(8,128)(2,1)}, bf16[192,640]{1,0:T(8,128)(2,1)S(1)}, u32[]{:S(2)}, u32[]{:S(2)}) collective-permute-start(bf16[192,640]{1,0:T(8,128)(2,1)} %get-tuple-element.24.refs_1_), channel_id=1, source_target_pairs={{0,1},{1,0},{2,3},{3,2},{4,5},{5,4},{6,7},{7,6},{8,9},{9,8},{10,11... | collective-permute-start | bytes 737288 | tf_op jit(solution)/shard_map/ppermute | solution.py:607
  39.1 2.9 %collective-permute-start.11 = (bf16[192,640]{1,0:T(8,128)(2,1)}, bf16[192,640]{1,0:T(8,128)(2,1)S(1)}, u32[]{:S(2)}, u32[]{:S(2)}) collective-permute-start(bf16[192,640]{1,0:T(8,128)(2,1)} %get-tuple-element.25.refs_2_), channel_id=1, source_target_pairs={{0,1},{1,0},{2,3},{3,2},{4,5},{5,4},{6,7},{7,6},{8,9},{9,8},{10,11... | collective-permute-start | bytes 737288 | tf_op jit(solution)/shard_map/ppermute | solution.py:607
  39.6 2.4 %collective-permute-start.12 = (bf16[192,640]{1,0:T(8,128)(2,1)}, bf16[192,640]{1,0:T(8,128)(2,1)S(1)}, u32[]{:S(2)}, u32[]{:S(2)}) collective-permute-start(bf16[192,640]{1,0:T(8,128)(2,1)} %get-tuple-element.26.refs_3_), channel_id=1, source_target_pairs={{0,1},{1,0},{2,3},{3,2},{4,5},{5,4},{6,7},{7,6},{8,9},{9,8},{10,11... | collective-permute-start | bytes 737288 | tf_op jit(solution)/shard_map/ppermute | solution.py:607
